TPU v7x, 32 devices: a whole 2x2x4 slice. The times are simulated.
32 devices in a mesh: chan: 16 (over z, y, x), src: 2 (over core).
Axes of the slice: x: 2, y: 2, z: 4, core: 2. Of those that a mesh axis runs over, the one named last changes fastest.
Arguments:
- strain: bfloat16 [256, 65536], P('src', 'chan'), may hold values from -6 to 6
- seg_start: int32 [3], replicated, may hold values from 0 to 8704
- src_chan: int32 [256], replicated, may hold values from 0 to 255
Outputs:
- correlation: bfloat16 [256, 2, 128, 512], P('src', None, 'chan')
All inputs are finite; a program needn't handle non-finite values.
Results may differ from a plain program's by a relative error of at most 0.0083.
Values may be sent and summed in bfloat16 or wider, within the bound.
No kernel may reach another device: no remote copies, remote signals or barrier semaphores. Data moves between devices by JAX's collectives and lax.ppermute only.
A program may use at most 64 MiB of HBM per device.

v0:
```python
import math

import jax
import jax.numpy as jnp
import numpy as np
from jax import lax
from jax.sharding import PartitionSpec as P

DEC = 4
SEG = 7680
NSEG = 3
BIN_LOW = 61
NBIN = 384
NLAG = 512


def shifted_2(value, axis, by):
    peers = lax.axis_size(axis)
    pairs = [(i, i + by) for i in range(peers) if 0 <= i + by < peers]
    return lax.ppermute(value, axis, pairs)


def decimation_tables():
    length = 4 * DEC
    offsets = np.arange(length)
    centred = (offsets - (length - 1) / 2.0) / DEC
    coeffs = (
        np.sin(np.pi * centred)
        / (np.pi * centred)
        * (0.54 - 0.46 * np.cos(2.0 * np.pi * (offsets + 0.5) / length))
    )
    coeffs = coeffs / coeffs.sum()
    sample_pos = np.arange(128)[:, None]
    output_pos = np.arange(128 // DEC)[None, :]
    tables = []
    for carried in (0, 128):
        tap_pos = sample_pos + carried - DEC * output_pos
        inside = (tap_pos >= 0) & (tap_pos < length)
        values = np.where(inside, coeffs[np.clip(tap_pos, 0, length - 1)], 0.0)
        tables.append(jnp.asarray(values, jnp.float32).astype(jnp.bfloat16))
    return (tables[0], tables[1])


def decimate(series, following, first_tab, second_tab):
    row_count, length = series.shape
    blocks = series.reshape(row_count, length // 128, 128)
    shifted = jnp.concatenate([blocks[:, 1:], following[:, None, :]], axis=1)
    summed = jnp.dot(blocks.reshape(-1, 128), first_tab, preferred_element_type=jnp.float32)
    summed = summed + jnp.dot(
        shifted.reshape(-1, 128), second_tab, preferred_element_type=jnp.float32
    )
    return summed.astype(jnp.bfloat16).reshape(row_count, length // DEC)


def whiten(spectrum):
    real_part = spectrum[..., :NBIN]
    imag_part = spectrum[..., NBIN:]
    energy = real_part * real_part + imag_part * imag_part
    offsets = np.arange(NBIN)
    band_mask = jnp.asarray((np.abs(offsets[:, None] - offsets[None, :]) <= 32).astype(np.float32))
    smooth = jnp.matmul(energy, band_mask, precision=lax.Precision.HIGHEST) / 65.0
    inverse = lax.rsqrt(smooth + 1e-05)
    return jnp.concatenate([real_part * inverse, imag_part * inverse], axis=-1).astype(jnp.bfloat16)


def lag_table():
    bin_ids = BIN_LOW + np.arange(NBIN)
    delays = np.arange(NLAG) - NLAG // 2
    angles = 2.0 * np.pi * np.mod(np.outer(bin_ids, delays), SEG) / SEG
    basis = np.concatenate([np.cos(angles), -np.sin(angles)], axis=0) / np.sqrt(NBIN)
    return jnp.asarray(basis, jnp.float32).astype(jnp.bfloat16)


def band_spectrum(segments):
    row_count = segments.shape[0]
    block_count = SEG // 512
    bin_ids = BIN_LOW + np.arange(NBIN)
    inner = 2.0 * np.pi * np.mod(np.outer(np.arange(512), bin_ids), SEG) / SEG
    table = jnp.asarray(np.concatenate([np.cos(inner), -np.sin(inner)], axis=1), jnp.float32)
    table_high = table.astype(jnp.bfloat16)
    table_low = (table - table_high.astype(jnp.float32)).astype(jnp.bfloat16)
    outer = 2.0 * np.pi * np.mod(np.outer(512 * np.arange(block_count), bin_ids), SEG) / SEG
    phase_cos = jnp.asarray(np.cos(outer), jnp.float32)
    phase_sin = jnp.asarray(np.sin(outer), jnp.float32)
    flat = segments.reshape(row_count * block_count, 512)
    partial_value = jnp.dot(flat, table_high, preferred_element_type=jnp.float32)
    partial_value = partial_value + jnp.dot(flat, table_low, preferred_element_type=jnp.float32)
    partial_value = partial_value.reshape(row_count, block_count, 2 * NBIN)
    part_re = partial_value[..., :NBIN]
    part_im = partial_value[..., NBIN:]
    total_re = jnp.sum(part_re * phase_cos + part_im * phase_sin, axis=1)
    total_im = jnp.sum(part_im * phase_cos - part_re * phase_sin, axis=1)
    return jnp.concatenate([total_re, total_im], axis=1) / math.sqrt(SEG)


def on_device(strain, seg_start, src_chan):
    first_tab, second_tab = decimation_tables()
    chan_count = lax.axis_size("chan")
    group_count = lax.axis_size("src")
    local_rows = strain.shape[0]
    per_device = local_rows // chan_count
    following = shifted_2(strain[:, :128], "chan", -1)
    reduced = decimate(strain, following, first_tab, second_tab)
    decimated = lax.all_to_all(reduced, "chan", split_axis=0, concat_axis=1, tiled=True)
    pieces = [
        lax.dynamic_slice_in_dim(decimated, seg_start[number], SEG, 1) for number in range(NSEG)
    ]
    segments = jnp.stack(pieces, axis=1).reshape(per_device * NSEG, SEG)
    spectra = whiten(band_spectrum(segments)).reshape(per_device, NSEG, 2 * NBIN)
    receivers = lax.all_gather(spectra, "src", axis=0, tiled=True)
    own_channels = (
        lax.axis_index("src") * local_rows
        + lax.axis_index("chan") * per_device
        + lax.iota(jnp.int32, per_device)
    )
    selector = (src_chan[:, None] == own_channels[None, :]).astype(jnp.bfloat16)
    picked = jnp.dot(
        selector, spectra.reshape(per_device, NSEG * 2 * NBIN), preferred_element_type=jnp.float32
    )
    summed_all = lax.psum(picked, "chan")
    grouped = lax.psum_scatter(
        summed_all.astype(jnp.bfloat16), "src", scatter_dimension=0, tiled=True
    )
    sources = grouped.reshape(-1, NSEG, 2 * NBIN)
    source_re = sources[..., :NBIN]
    source_im = sources[..., NBIN:]
    recv_re = receivers[..., :NBIN]
    recv_im = receivers[..., NBIN:]
    cross_re = jnp.einsum("ksf,rsf->krf", source_re, recv_re, preferred_element_type=jnp.float32)
    cross_re = (
        cross_re
        + jnp.einsum("ksf,rsf->krf", source_im, recv_im, preferred_element_type=jnp.float32)
    ) / NSEG
    cross_im = jnp.einsum("ksf,rsf->krf", source_re, recv_im, preferred_element_type=jnp.float32)
    cross_im = (
        cross_im
        - jnp.einsum("ksf,rsf->krf", source_im, recv_re, preferred_element_type=jnp.float32)
    ) / NSEG
    merged = jnp.concatenate([cross_re, cross_im], axis=-1).astype(jnp.bfloat16)
    lagged = jnp.dot(merged.reshape(-1, 2 * NBIN), lag_table(), preferred_element_type=jnp.float32)
    return lagged.astype(jnp.bfloat16).reshape(sources.shape[0], group_count, per_device, NLAG)


def solution(mesh):
    return jax.shard_map(
        on_device,
        mesh=mesh,
        in_specs=(P("src", "chan"), P(), P()),
        out_specs=P("src", None, "chan", None),
        check_vma=False,
    )
```

profile of v0, /device:TPU:0, one launch (start us, length us, event | category | flops | bytes accessed | tf_op | source)
XLA Modules:
  0.0 177.0 jit_solution(11885928159048033535)
XLA Ops:
  6.5 0.8 slice.40
  7.4 1.3 collective-permute-start
  8.7 1.6 reshape_reshape.7
  10.3 0.5 convolution_bitcast_fusion
  10.7 0.3 copy.51
  11.0 0.0 copy-start.9
  11.0 0.5 slice.54
  11.5 2.6 %collective-permute-done = bf16[128,128]{1,0:T(8,128)(2,1)S(1)} collective-permute-done((bf16[128,128]{1,0:T(8,128)(2,1)S(1)}, bf16[128,128]{1,0:T(8,128)(2,1)S(1)}, u32[]{:S(2)}, u32[]{:S(2)}) %collective-permute-start) | collective-permute-done | bytes 32800 | tf_op jit(solution)/shard_map/ppermute | solution.py:20
  14.1 0.1 copy.35
  14.2 0.2 pad_maximum_fusion
  14.4 0.5 fusion
  14.9 0.5 copy.36
  15.4 1.8 %all_to_all.14 = bf16[16,8,1024]{2,1,0:T(8,128)(2,1)} reshape(bf16[4096,32]{1,0:T(8,128)(2,1)S(1)} %copy.36) | data formatting | bytes 524288 | tf_op jit(solution)/shard_map/all_to_all | solution.py:104
  17.2 8.3 %all-to-all-start = ((bf16[16,8,1024]{2,1,0:T(8,128)(2,1)}), bf16[16,8,1024]{2,1,0:T(8,128)(2,1)S(1)}, u32[]{:S(2)}, u32[]{:S(2)}) async-start(bf16[16,8,1024]{2,1,0:T(8,128)(2,1)} %all_to_all.14), calls=%async_computation | async-start | bytes 524288 | tf_op jit(solution)/shard_map/all_to_all | solution.py:104
  25.6 0.0 reduce-scatter.2.cloned.1.call-start
  25.6 0.6 fusion.20
  31.6 2.4 %all-to-all-done = bf16[16,8,1024]{2,1,0:T(8,128)(2,1)S(1)} async-done(((bf16[16,8,1024]{2,1,0:T(8,128)(2,1)}), bf16[16,8,1024]{2,1,0:T(8,128)(2,1)S(1)}, u32[]{:S(2)}, u32[]{:S(2)}) %all-to-all-start) | async-done | bytes 262176 | tf_op jit(solution)/shard_map/all_to_all | solution.py:104
  34.1 0.2 dynamic-slice_bitcast_fusion.2
  34.3 0.3 copy.37
  34.6 0.3 reshape_reshape.8
  34.9 0.4 fusion.21
  35.4 0.0 copy-done.5
  35.4 0.5 convolution_add_fusion.1
  35.9 0.1 reshape.41
  36.1 0.1 copy-done.11
  36.2 0.0 copy-done.12
  36.2 0.3 add_reduce_fusion
  36.5 0.5 copy-done.6
  37.0 0.4 multiply_convert_fusion.3
  37.4 0.5 fusion.11
  38.0 105.4 %all-reduce.1 = bf16[256,2304]{1,0:T(8,128)(2,1)} all-reduce(f32[256,2304]{1,0:T(8,128)S(1)} %fusion.11), channel_id=1, replica_groups=mesh['chan'=16,'src'=2] {'chan'}, use_global_device_ids=true, to_apply=%region_2.0 | all-reduce | flops 589824 | bytes 3538944 | tf_op jit(solution)/shard_map/psum | solution.py:120
  143.3 0.0 reduce-scatter.2.cloned.1.call-update
  143.4 2.0 %all_gather.3 = bf16[16,3,768]{2,0,1:T(8,128)(2,1)S(1)} all-gather(bf16[8,3,768]{2,0,1:T(8,128)(2,1)S(1)} %pad_maximum_fusion.2), channel_id=1, replica_groups=mesh['chan'=16,'src'=2] {'src'}, dimensions={0}, use_global_device_ids=true | all-gather | bytes 110592 | tf_op jit(solution)/shard_map/all_gather | solution.py:110
  145.5 0.2 copy.49
  145.8 1.0 copy.47
  146.7 3.9 %reduce-scatter.2.cloned.1.call-done = bf16[128,2304]{1,0:T(8,128)(2,1)} async-done(((bf16[256,2304]{1,0:T(8,128)(2,1)}), bf16[128,2304]{1,0:T(8,128)(2,1)}) %reduce-scatter.2.cloned.1.call-update) | async-done | bytes 589840 | tf_op jit(solution)/shard_map/reduce_scatter | solution.py:121
  150.6 1.4 copy.41
  152.1 0.7 fusion.7
  152.8 0.3 copy-done.3
  153.1 0.7 fusion.9
  153.8 3.1 %fusion.2 = bf16[128,16,384]{0,1,2:T(8,128)(2,1)} fusion(f32[384,16,128]{2,1,0:T(8,128)S(1)} %fusion.7, bf16[16,3,384]{0,1,2:T(4,128)(2,1)S(1)} %copy-done.3, bf16[128,3,384]{0,2,1:T(8,128)(2,1)S(1)} %get-tuple-element.7), kind=kOutput, calls=%fused_computation.7 | convolution fusion | flops 7077888 | bytes 5050368 | tf_op jit(solution)/shard_map/ksf,rsf->krf/dot_general | solution.py:137
  156.9 3.4 %copy.46 = bf16[128,16,384]{2,1,0:T(8,128)(2,1)} copy(bf16[128,16,384]{0,1,2:T(8,128)(2,1)} %fusion.2) | data formatting | bytes 3145728 | tf_op jit(solution)/shard_map/div | solution.py:135
  160.3 3.0 %fusion.1 = bf16[128,16,384]{0,1,2:T(8,128)(2,1)} fusion(f32[384,16,128]{2,1,0:T(8,128)S(1)} %fusion.9, bf16[16,3,384]{0,1,2:T(4,128)(2,1)} %copy-done.2, bf16[128,3,384]{0,2,1:T(8,128)(2,1)S(1)} %get-tuple-element.7), kind=kOutput, calls=%fused_computation.6 | convolution fusion | flops 7077888 | bytes 5050368 | tf_op jit(solution)/shard_map/ksf,rsf->krf/dot_general | solution.py:132
  163.3 2.6 %copy.45 = bf16[128,16,384]{2,1,0:T(8,128)(2,1)S(1)} copy(bf16[128,16,384]{0,1,2:T(8,128)(2,1)} %fusion.1) | data formatting | bytes 3145728 | tf_op jit(solution)/shard_map/div | solution.py:130
  166.0 1.2 fusion.22
  167.2 0.1 copy-done
  167.4 0.1 copy-done.7
  167.4 2.7 %add_convert_fusion = bf16[2048,512]{1,0:T(8,128)(2,1)} fusion(f32[2048,512]{1,0:T(8,128)S(1)} %fusion.22, bf16[2048,384]{1,0:T(8,128)(2,1)S(1)} %bitcast.45, bf16[384,512]{1,0:T(8,128)(2,1)S(1)} %copy-done.7), kind=kOutput, calls=%fused_computation.3 | convolution fusion | flops 807403520 | bytes 8257536 | tf_op jit(solution)/shard_map/dot_general | solution.py:140
  (34 shorter events, 0.2 us)
Async XLA Ops:
  6.5 3.7 %copy-start.10 = (bf16[128,32]{1,0:T(8,128)(2,1)S(1)}, bf16[128,32]{1,0:T(8,128)(2,1)}, u32[]{:S(2)}) copy-start(bf16[128,32]{1,0:T(8,128)(2,1)} %constant.51) | copy-start | bytes 24580
  6.5 4.2 %copy-start.1 = (bf16[128,4096]{1,0:T(8,128)(2,1)S(1)}, bf16[128,4096]{1,0:T(8,128)(2,1)}, u32[]{:S(2)}) copy-start(bf16[128,4096]{1,0:T(8,128)(2,1)} %param.10) | copy-start | bytes 3145732
  7.4 6.7 %collective-permute-start = (bf16[128,128]{1,0:T(8,128)(2,1)S(1)}, bf16[128,128]{1,0:T(8,128)(2,1)S(1)}, u32[]{:S(2)}, u32[]{:S(2)}) collective-permute-start(bf16[128,128]{1,0:T(8,128)(2,1)S(1)} %slice.40), channel_id=1, source_target_pairs={{2,0},{4,2},{6,4},{8,6},{10,8},{12,10},{14,12},{16,14},{18,16},{20... | collective-permute-start | bytes 98312 | tf_op jit(solution)/shard_map/ppermute | solution.py:20
  11.0 3.4 %copy-start.9 = (bf16[128,32]{1,0:T(8,128)(2,1)S(1)}, bf16[128,32]{1,0:T(8,128)(2,1)}, u32[]{:S(2)}) copy-start(bf16[128,32]{1,0:T(8,128)(2,1)} %constant.52) | copy-start | bytes 24580
  14.4 11.2 %copy-start.13 = (s32[3]{0:T(128)S(1)}, s32[3]{0:T(128)}, u32[]{:S(2)}) copy-start(s32[3]{0:T(128)} %param.11) | copy-start | bytes 40
  17.2 17.7 %copy-start.4 = (bf16[512,768]{1,0:T(8,128)(2,1)S(1)}, bf16[512,768]{1,0:T(8,128)(2,1)}, u32[]{:S(2)}) copy-start(bf16[512,768]{1,0:T(8,128)(2,1)} %constant.53) | copy-start | bytes 2359300
  17.2 16.8 %all-to-all-start = ((bf16[16,8,1024]{2,1,0:T(8,128)(2,1)}), bf16[16,8,1024]{2,1,0:T(8,128)(2,1)S(1)}, u32[]{:S(2)}, u32[]{:S(2)}) async-start(bf16[16,8,1024]{2,1,0:T(8,128)(2,1)} %all_to_all.14), calls=%async_computation | async-start | bytes 524288 | tf_op jit(solution)/shard_map/all_to_all | solution.py:104
  25.6 125.1 %reduce-scatter.2.cloned.1.call-start = ((), (), s32[]{:S(2)}) async-start(), calls=%async_computation.2 | async-start | bytes 1769472 | tf_op jit(solution)/shard_map/reduce_scatter | solution.py:121
  34.3 1.1 copy-start.5
  35.4 0.7 copy-start.11
  35.4 0.8 copy-start.12
  35.9 1.1 copy-start.6
  35.9 1.5 copy-start.14
  145.7 6.3 %copy-start.2 = (bf16[16,3,384]{0,1,2:T(4,128)(2,1)}, bf16[16,3,384]{0,1,2:T(4,128)(2,1)S(1)}, u32[]{:S(2)}) copy-start(bf16[16,3,384]{0,1,2:T(4,128)(2,1)S(1)} %copy.49) | copy-start | bytes 110596
  152.1 1.0 copy-start.3
  163.3 2.6 %copy-start.8 = (bf16[384,512]{1,0:T(8,128)(2,1)S(1)}, bf16[384,512]{1,0:T(8,128)(2,1)}, u32[]{:S(2)}) copy-start(bf16[384,512]{1,0:T(8,128)(2,1)} %constant.58) | copy-start | bytes 1179652
  166.0 1.4 copy-start
  166.0 1.5 copy-start.7
Sparse Core Ops, SparseCore 0:
  143.5 7.1 reduce-scatter.1
where the time goes:
time: 178 us; the launch traced here: 177 us
  blocking collectives  107 us (60%)
  between operations  19.2 us (11%)
  local copies, waits for them, and re-layouts  16.9 us (9%)
  matrix products  14.3 us (8%)
  starting transfers between devices  9.62 us (5%)
  waiting for transfers between devices  8.94 us (5%)
    psum x1, blocking collectives, on_device(): summed_all = lax.psum(picked, 'chan')  105 us
    all_to_all x1, starting transfers between devices, on_device(): lax.all_to_all(reduced, 'chan', split_axis=0, concat_axis=1, tiled=True)  8.3 us
    dot_general x2, matrix products, on_device(): jnp.dot(merged.reshape(-1, 2 * NBIN), lag_table(), preferred_element_type...  3.95 us
    reduce_scatter x1, waiting for transfers between devices, on_device(): lax.psum_scatter(summed_all.astype(jnp.bfloat16), 'src', scatter_dimensio...  3.93 us
  transfers between devices with their start and end apart: 3, of which 3 were waited for; matrix products, arithmetic and copies ran while one was open for 3% of the time, Pallas kernels for 0%

commit v1 on v0

v1 whole, which is shorter than its diff:
```python
import math

import jax
import jax.numpy as jnp
import numpy as np
from jax import lax
from jax.experimental import pallas as pl
from jax.experimental.pallas import tpu as pltpu
from jax.sharding import PartitionSpec as P

DEC = 4
SEG = 7680
NSEG = 3
BIN_LOW = 61
NBIN = 384
NLAG = 512
LANES = 128
BLOCK = 512
HALVES = 2
CHUNKS = NBIN // LANES
VMEM = pl.BlockSpec(memory_space=pltpu.VMEM)
SMEM = pl.BlockSpec(memory_space=pltpu.SMEM)


def filter_table():
    length = 4 * DEC
    offsets = np.arange(length)
    centred = (offsets - (length - 1) / 2.0) / DEC
    coeffs = (
        np.sin(np.pi * centred)
        / (np.pi * centred)
        * (0.54 - 0.46 * np.cos(2.0 * np.pi * (offsets + 0.5) / length))
    )
    coeffs = coeffs / coeffs.sum()
    tap = np.arange(DEC * LANES + LANES)[:, None] - DEC * np.arange(LANES)[None, :]
    inside = (tap >= 0) & (tap < length)
    values = np.where(inside, coeffs[np.clip(tap, 0, length - 1)], 0.0)
    return jnp.asarray(values, jnp.float32).astype(jnp.bfloat16)


def inner_table():
    bin_ids = BIN_LOW + np.arange(NBIN)
    angle = 2.0 * np.pi * np.mod(np.outer(np.arange(BLOCK), bin_ids), SEG) / SEG
    parts = np.stack([np.cos(angle), -np.sin(angle)], axis=1)
    parts = parts.reshape(BLOCK, 2, CHUNKS, LANES).transpose(0, 2, 1, 3)
    return jnp.asarray(parts.reshape(BLOCK, 2 * NBIN), jnp.float32).astype(jnp.bfloat16)


def phase_table(first, count):
    bin_ids = BIN_LOW + np.arange(NBIN)
    angle = 2.0 * np.pi * np.mod(np.outer(BLOCK * (first + np.arange(count)), bin_ids), SEG) / SEG
    parts = np.stack([np.cos(angle), np.sin(angle)], axis=1) / math.sqrt(SEG)
    return jnp.asarray(parts.reshape(count, 1, 2 * NBIN), jnp.float32)


def lag_table():
    bin_ids = BIN_LOW + np.arange(NBIN)
    delays = np.arange(NLAG) - NLAG // 2
    angles = 2.0 * np.pi * np.mod(np.outer(bin_ids, delays), SEG) / SEG
    basis = np.concatenate([np.cos(angles), -np.sin(angles)], axis=0) / np.sqrt(NBIN)
    return jnp.asarray(basis, jnp.float32).astype(jnp.bfloat16)


def band_table():
    offsets = np.arange(NBIN)
    band = np.abs(offsets[:, None] - offsets[None, :]) <= 32
    return jnp.asarray(band.astype(np.float32)).astype(jnp.bfloat16)


def dot(left, right):
    return jnp.dot(left, right, preferred_element_type=jnp.float32)


def decimate_kernel(strain_ref, table_ref, out_ref):
    halves, rows, length = strain_ref.shape
    group = out_ref.shape[1] // halves
    tiles = length // BLOCK
    x = strain_ref[...].reshape(halves * rows, length)

    def put(values, at):
        for peer in range(rows // group):
            part = [
                values[half * rows + peer * group : half * rows + (peer + 1) * group]
                for half in range(halves)
            ]
            out_ref[peer, :, at : at + LANES] = jnp.concatenate(part, axis=0).astype(jnp.bfloat16)

    for tile in range(tiles):
        stop = min(BLOCK * tile + BLOCK + LANES, length)
        piece = x[:, BLOCK * tile : stop]
        put(dot(piece, table_ref[: piece.shape[1], :]), tile * LANES)
    put(dot(x[:, :LANES], table_ref[BLOCK:, :]), tiles * LANES)


def decimate(strain, peers, group):
    rows, length = strain.shape
    half_rows = rows // HALVES
    width = length // DEC + LANES
    steps = 2
    return pl.pallas_call(
        decimate_kernel,
        out_shape=jax.ShapeDtypeStruct((peers, HALVES * group, width), jnp.bfloat16),
        grid=(steps,),
        in_specs=[
            pl.BlockSpec((HALVES, half_rows // steps, length), lambda i: (0, i, 0)),
            pl.BlockSpec((BLOCK + LANES, LANES), lambda i: (0, 0)),
        ],
        out_specs=pl.BlockSpec((peers // steps, HALVES * group, width), lambda i: (i, 0, 0)),
        name="decimate",
    )(strain.reshape(HALVES, half_rows, length), filter_table())


def spectrum_kernel(place_ref, start_ref, recv_ref, inner_ref, phase_ref, own_ref, send_ref, lhs, edge):
    peers, rows, width = recv_ref.shape
    span = width - LANES
    blocks = peers * span // BLOCK
    base = place_ref[0] * (peers * span)
    first = place_ref[0] * blocks
    starts = [start_ref[number] for number in range(NSEG)]
    lane = lax.broadcasted_iota(jnp.int32, (rows, LANES), 1)

    def windows(values, at):
        pos = lane + at
        return [
            jnp.where((pos >= start) & (pos < start + SEG), values, 0.0).astype(jnp.bfloat16)
            for start in starts
        ]

    for peer in range(peers):
        for tile in range(span // LANES):
            values = recv_ref[peer, :, tile * LANES : (tile + 1) * LANES].astype(jnp.float32)
            if tile == span // LANES - 1 and peer + 1 < peers:
                values = values + recv_ref[peer + 1, :, span:].astype(jnp.float32)
            at = peer * span + tile * LANES
            block, inside = divmod(at, BLOCK)
            for number, part in enumerate(windows(values, base + at)):
                row = (block * NSEG + number) * rows
                lhs[row : row + rows, inside : inside + LANES] = part
    for number, part in enumerate(windows(recv_ref[0, :, span:].astype(jnp.float32), base - LANES)):
        edge[number * rows : (number + 1) * rows, :] = part
    many = NSEG * rows
    for chunk in range(CHUNKS):
        columns = slice(2 * chunk * LANES, 2 * (chunk + 1) * LANES)
        re_at = slice(chunk * LANES, (chunk + 1) * LANES)
        im_at = slice(NBIN + chunk * LANES, NBIN + (chunk + 1) * LANES)
        table = inner_ref[:, columns]
        body = dot(lhs[...], table)
        parts = [dot(edge[...], table[BLOCK - LANES :])]
        parts += [body[block * many : (block + 1) * many] for block in range(blocks)]
        total_re = total_im = 0.0
        for number, part in enumerate(parts):
            cos, sin = phase_ref[first + number, :, re_at], phase_ref[first + number, :, im_at]
            part_re, part_im = part[:, :LANES], part[:, LANES:]
            total_re = total_re + (part_re * cos + part_im * sin)
            total_im = total_im + (part_im * cos - part_re * sin)
        own_ref[:, re_at] = total_re
        own_ref[:, im_at] = total_im
        send_ref[:, re_at] = total_re.astype(jnp.bfloat16)
        send_ref[:, im_at] = total_im.astype(jnp.bfloat16)


def partial_spectrum(place, seg_start, recv):
    peers, rows, width = recv.shape
    blocks = peers * (width - LANES) // BLOCK
    many = NSEG * rows
    return pl.pallas_call(
        spectrum_kernel,
        out_shape=[
            jax.ShapeDtypeStruct((many, 2 * NBIN), jnp.float32),
            jax.ShapeDtypeStruct((many, 2 * NBIN), jnp.bfloat16),
        ],
        in_specs=[SMEM, SMEM, VMEM, VMEM, VMEM],
        out_specs=[VMEM, VMEM],
        scratch_shapes=[
            pltpu.VMEM((blocks * many, BLOCK), jnp.bfloat16),
            pltpu.VMEM((many, LANES), jnp.bfloat16),
        ],
        compiler_params=pltpu.CompilerParams(vmem_limit_bytes=32 * 1024 * 1024),
        name="spectrum",
    )(place, seg_start, recv, inner_table(), phase_table(-1, HALVES * blocks + 1))


def whiten_kernel(own_ref, other_ref, band_ref, out_ref):
    total = own_ref[...] + other_ref[...].astype(jnp.float32)
    real_part, imag_part = total[:, :NBIN], total[:, NBIN:]
    energy = real_part * real_part + imag_part * imag_part
    high = energy.astype(jnp.bfloat16)
    low = (energy - high.astype(jnp.float32)).astype(jnp.bfloat16)
    smooth = (dot(high, band_ref[...]) + dot(low, band_ref[...])) / 65.0
    inverse = lax.rsqrt(smooth + 1e-05)
    white_re = (real_part * inverse).astype(jnp.bfloat16)
    white_im = (imag_part * inverse).astype(jnp.bfloat16)
    for peer in range(out_ref.shape[0]):
        out_ref[peer, :, :NBIN] = white_re
        out_ref[peer, :, NBIN:] = white_im


def whiten(own, other, peers):
    return pl.pallas_call(
        whiten_kernel,
        out_shape=jax.ShapeDtypeStruct((peers, *own.shape), jnp.bfloat16),
        in_specs=[VMEM] * 3,
        out_specs=VMEM,
        compiler_params=pltpu.CompilerParams(vmem_limit_bytes=32 * 1024 * 1024),
        name="whiten",
    )(own, other, band_table())


def correlate_kernel(groups, group, place_ref, chan_ref, *refs):
    spectra, (basis_ref, out_ref, source, receiver, cross) = refs[:groups], refs[groups:]
    peers = spectra[0].shape[0]
    rows = HALVES * group
    channels = peers * rows
    many = source.shape[1]
    block = out_ref.shape[0] // (groups * group)
    half, peer, mine = place_ref[0], place_ref[1], place_ref[2]

    @pl.when(pl.program_id(0) == 0)
    def _():
        wanted = chan_ref[pl.ds(pl.multiple_of(mine * many, many), many), :]
        spot = lax.broadcasted_iota(jnp.int32, (many, channels), 1)
        total = [0.0] * NSEG
        for step, spectrum in enumerate(spectra):
            owner = lax.rem(mine + step, groups)
            local = wanted - owner * channels
            in_half = jnp.bitwise_and(local, channels // HALVES - 1)
            place = (in_half // group) * rows + (local // (channels // HALVES)) * group + in_half % group
            place = jnp.where((local >= 0) & (local < channels), place, -1)
            pick = (spot == place).astype(jnp.float32).astype(jnp.bfloat16)
            for number in range(NSEG):
                held = spectrum[:, number * rows : (number + 1) * rows, :]
                total[number] = total[number] + dot(pick, held.reshape(channels, 2 * NBIN))
                here = spectrum[peer, number * rows : (number + 1) * rows, :].astype(jnp.float32)
                here = jnp.where(half == 0, here[:group], here[group:]) * (1.0 / NSEG)
                receiver[number, owner] = here
        for number in range(NSEG):
            source[number] = total[number]

    start = pl.program_id(0) * block
    for chunk in range(CHUNKS):
        re_at = slice(chunk * LANES, (chunk + 1) * LANES)
        im_at = slice(NBIN + chunk * LANES, NBIN + (chunk + 1) * LANES)
        recv = [receiver[number].reshape(groups * group, 2 * NBIN) for number in range(NSEG)]
        for k in range(block):
            total_re = total_im = 0.0
            for number in range(NSEG):
                row = source[number, pl.ds(start + k, 1), :]
                source_re, source_im = row[:, re_at], row[:, im_at]
                recv_re, recv_im = recv[number][:, re_at], recv[number][:, im_at]
                total_re = total_re + (source_re * recv_re + source_im * recv_im)
                total_im = total_im + (source_re * recv_im - source_im * recv_re)
            at = slice(k * groups * group, (k + 1) * groups * group)
            cross[at, re_at] = total_re.astype(jnp.bfloat16)
            cross[at, im_at] = total_im.astype(jnp.bfloat16)
    out_ref[...] = dot(cross[...], basis_ref[...]).astype(jnp.bfloat16)


def correlate(place, src_chan, spectra, group):
    groups = len(spectra)
    many = src_chan.shape[0] // groups
    rows = groups * group
    block = max(1, 256 // rows)

    def kernel(*refs):
        correlate_kernel(groups, group, *refs)

    whole = lambda array: pl.BlockSpec(array.shape, lambda i: (0,) * array.ndim)
    column = src_chan.reshape(-1, 1)
    basis = lag_table()
    return pl.pallas_call(
        kernel,
        out_shape=jax.ShapeDtypeStruct((many * rows, NLAG), jnp.bfloat16),
        grid=(many // block,),
        in_specs=[SMEM] + [whole(a) for a in (column, *spectra, basis)],
        out_specs=pl.BlockSpec((block * rows, NLAG), lambda i: (i, 0)),
        scratch_shapes=[
            pltpu.VMEM((NSEG, many, 2 * NBIN), jnp.float32),
            pltpu.VMEM((NSEG, groups, group, 2 * NBIN), jnp.float32),
            pltpu.VMEM((block * rows, 2 * NBIN), jnp.bfloat16),
        ],
        compiler_params=pltpu.CompilerParams(vmem_limit_bytes=56 * 1024 * 1024),
        name="correlate",
    )(place, column, *spectra, basis)


def on_device(strain, seg_start, src_chan):
    chan_count = lax.axis_size("chan")
    group_count = lax.axis_size("src")
    peers = chan_count // HALVES
    per_device = strain.shape[0] // chan_count
    index = lax.axis_index("chan")
    place = jnp.stack([index // peers, index % peers, lax.axis_index("src")]).astype(jnp.int32)
    cubes = [[half * peers + peer for peer in range(peers)] for half in range(HALVES)]

    sent = decimate(strain, peers, per_device)
    samples = lax.all_to_all(sent, "chan", 0, 0, tiled=True, axis_index_groups=cubes)
    own, send = partial_spectrum(place, seg_start, samples)
    across = [(i, (i + peers) % chan_count) for i in range(chan_count)]
    white = whiten(own, lax.ppermute(send, "chan", across), peers)
    held = lax.all_to_all(white, "chan", 0, 0, tiled=True, axis_index_groups=cubes)
    spectra = [held]
    for step in range(1, group_count):
        pairs = [((i + step) % group_count, i) for i in range(group_count)]
        spectra.append(lax.ppermute(held, "src", pairs))
    lagged = correlate(place, src_chan, spectra, per_device)
    return lagged.reshape(-1, group_count, per_device, NLAG)


def solution(mesh):
    return jax.shard_map(
        on_device,
        mesh=mesh,
        in_specs=(P("src", "chan"), P(), P()),
        out_specs=P("src", None, "chan", None),
        check_vma=False,
    )
```

time: 178 us -> 46.2 us (0.26)
  blocking collectives: 107 us -> 11 us
  between operations: 19.2 us -> 0.03 us
  local copies, waits for them, and re-layouts: 16.9 us -> 1.71 us
  matrix products: 14.3 us -> 0 us
  Pallas kernels: 0 us -> 12.6 us
  waiting for transfers between devices: 8.94 us -> 11.4 us
    psum x1 -> x0, blocking collectives: 105 us -> none  [on_device(): summed_all = lax.psum(picked, 'chan')]
    dot_general x12 -> x0, matrix products: 14.3 us -> none  [the longest x2 3.95 us: on_device(): jnp.dot(merged.reshape(-1, 2 * NBIN), lag_table(), preferred_element_type...]
    pallas_call x0 -> x4, Pallas kernels: none -> 12.6 us  [the longest x1 8.33 us: correlate(): pl.pallas_call(kernel, out_shape=jax.ShapeDtypeStruct((many * rows, NLAG)...]
    all_to_all x0 -> x1, blocking collectives: none -> 11 us  [on_device(): lax.all_to_all(white, 'chan', 0, 0, tiled=True, axis_index_groups=cubes)]
    div x2 -> x0, local copies, waits for them, and re-layouts: 6 us -> none  [the longest x1 3.36 us: on_device(): (cross_im - jnp.einsum('ksf,rsf->krf', source_im, recv_re, preferred_elem...]
    all_to_all x1, waiting for transfers between devices: 2.4 us -> 6.84 us  [on_device(): lax.all_to_all(sent, 'chan', 0, 0, tiled=True, axis_index_groups=cubes)]
    reduce_scatter x1 -> x0, waiting for transfers between devices: 3.93 us -> none  [on_device(): lax.psum_scatter(summed_all.astype(jnp.bfloat16), 'src', scatter_dimensio...]
    another operation x4 -> x0, local copies, waits for them, and re-layouts: 2.33 us -> none  [the longest x1 1.56 us: decimate(): blocks.reshape(-1, 128)]
  transfers between devices with their start and end apart: 3 -> 3, of which waited for: 3 -> 3; matrix products, arithmetic and copies ran while one was open for 3% -> 2% of each run, Pallas kernels for 0% -> 0%
where the time goes in v1:
time: 46.2 us; the launch traced here: 45.9 us
  Pallas kernels  12.6 us (27%)
  waiting for transfers between devices  11.4 us (25%)
  blocking collectives  11 us (24%)
  starting transfers between devices  8.98 us (19%)
  local copies, waits for them, and re-layouts  1.71 us (4%)
    all_to_all x1, blocking collectives, on_device(): lax.all_to_all(white, 'chan', 0, 0, tiled=True, axis_index_groups=cubes)  11 us
    pallas_call x1, Pallas kernels, correlate(): pl.pallas_call(kernel, out_shape=jax.ShapeDtypeStruct((many * rows, NLAG)...  8.33 us
    all_to_all x1, waiting for transfers between devices, on_device(): lax.all_to_all(sent, 'chan', 0, 0, tiled=True, axis_index_groups=cubes)  6.84 us
    all_to_all x1, starting transfers between devices, on_device(): lax.all_to_all(sent, 'chan', 0, 0, tiled=True, axis_index_groups=cubes)  6.33 us
    ppermute x1, waiting for transfers between devices, on_device(): white = whiten(own, lax.ppermute(send, 'chan', across), peers)  3.46 us
    ppermute x1, starting transfers between devices, on_device(): white = whiten(own, lax.ppermute(send, 'chan', across), peers)  2.65 us
    pallas_call x1, Pallas kernels, decimate(): pl.pallas_call(decimate_kernel, out_shape=jax.ShapeDtypeStruct((peers, HA...  2.57 us
    pallas_call x1, Pallas kernels, partial_spectrum(): pl.pallas_call(spectrum_kernel, out_shape=[jax.ShapeDtypeStruct((many, 2...  1.44 us
  transfers between devices with their start and end apart: 3, of which 3 were waited for; matrix products, arithmetic and copies ran while one was open for 2% of the time, Pallas kernels for 0%

profile of v1, /device:TPU:0, one launch (start us, length us, event | category | flops | bytes accessed | tf_op | source)
XLA Modules:
  0.0 45.9 jit_solution(13775521010758137958)
XLA Ops:
  0.0 0.0 copy-start
  0.0 0.0 copy-start.2
  0.0 0.0 copy-start.1
  0.0 0.0 copy-start.4
  0.0 2.6 %decimate.1 = bf16[8,16,1152]{2,1,0:T(8,128)(2,1)} custom-call(bf16[2,64,4096]{2,1,0:T(8,128)(2,1)} %bitcast.6, bf16[640,128]{1,0:T(8,128)(2,1)} %constant.49.table_ref), custom_call_target="tpu_custom_call" | custom-call | tf_op jit(solution)/shard_map/decimate/pallas_call | solution.py:100
  2.6 0.0 copy-start.7
  2.6 6.3 %all-to-all-start = ((bf16[8,16,1152]{2,1,0:T(8,128)(2,1)}), bf16[8,16,1152]{2,1,0:T(8,128)(2,1)S(1)}, u32[]{:S(2)}, u32[]{:S(2)}) async-start(bf16[8,16,1152]{2,1,0:T(8,128)(2,1)} %decimate.1), calls=%async_computation | async-start | bytes 589824 | tf_op jit(solution)/shard_map/all_to_all | solution.py:296
  8.9 0.1 pad_add_fusion.place_ref.refs_0_
  9.0 0.0 copy-start.3
  9.0 6.8 %all-to-all-done.recv_ref = bf16[8,16,1152]{2,1,0:T(8,128)(2,1)S(1)} async-done(((bf16[8,16,1152]{2,1,0:T(8,128)(2,1)}), bf16[8,16,1152]{2,1,0:T(8,128)(2,1)S(1)}, u32[]{:S(2)}, u32[]{:S(2)}) %all-to-all-start) | async-done | bytes 294944 | tf_op jit(solution)/shard_map/all_to_all | solution.py:296
  15.8 0.0 copy-done
  15.8 0.0 copy-done.2
  15.8 0.0 copy-done.4
  15.8 1.4 %spectrum.1 = (f32[48,768]{1,0:T(8,128)S(1)}, bf16[48,768]{1,0:T(8,128)(2,1)S(1)}) custom-call(s32[3]{0:T(128)S(1)} %pad_add_fusion.place_ref.refs_0_, s32[3]{0:T(128)S(1)} %copy-done.4, bf16[8,16,1152]{2,1,0:T(8,128)(2,1)S(1)} %all-to-all-done.recv_ref, bf16[512,768]{1,0:T(8,128)(2,1)S(1)} %copy-done, f32[33,1,768]{2,1,0:T(1,128)S(1)} %copy-done.2), custom_call_target="tpu_custom_call" | custom-call | tf_op jit(solution)/shard_map/spectrum/pallas_call | solution.py:166
  17.3 2.7 %collective-permute-start = (bf16[48,768]{1,0:T(8,128)(2,1)S(1)}, bf16[48,768]{1,0:T(8,128)(2,1)S(1)}, u32[]{:S(2)}, u32[]{:S(2)}) collective-permute-start(bf16[48,768]{1,0:T(8,128)(2,1)S(1)} %get-tuple-element.8), channel_id=1, source_target_pairs={{0,16},{2,18},{4,20},{6,22},{8,24},{10,26},{12,28},{14,30},{16,0},... | collective-permute-start | bytes 221192 | tf_op jit(solution)/shard_map/ppermute | solution.py:299
  19.9 3.5 %collective-permute-done.other_ref = bf16[48,768]{1,0:T(8,128)(2,1)S(1)} collective-permute-done((bf16[48,768]{1,0:T(8,128)(2,1)S(1)}, bf16[48,768]{1,0:T(8,128)(2,1)S(1)}, u32[]{:S(2)}, u32[]{:S(2)}) %collective-permute-start) | collective-permute-done | bytes 73760 | tf_op jit(solution)/shard_map/ppermute | solution.py:299
  23.4 0.0 copy-done.1
  23.4 0.3 whiten.1
  23.7 11.0 %all_to_all.10.refs_2_ = bf16[8,48,768]{2,1,0:T(8,128)(2,1)S(1)} all-to-all(bf16[8,48,768]{2,1,0:T(8,128)(2,1)S(1)} %whiten.1), channel_id=1, replica_groups={{0,2,4,6,8,10,12,14},{16,18,20,22,24,26,28,30},{1,3,5,7,9,11,13,15},{17..., dimensions={0} | all-to-all | bytes 1179648 | tf_op jit(solution)/shard_map/all_to_all | solution.py:300
  34.7 0.0 copy-start.5
  34.7 0.0 collective-permute-start.1
  34.7 0.0 copy-done.7
  34.7 0.9 %copy.9.refs_1_ = s32[256,1]{1,0:T(8,128)} copy(s32[256,1]{0,1:T(1,128)S(1)} %bitcast.7) | data formatting | bytes 2048 | tf_op jit(solution)/shard_map/reshape | solution.py:268
  35.6 1.1 %collective-permute-done.1.refs_3_ = bf16[8,48,768]{2,1,0:T(8,128)(2,1)S(1)} collective-permute-done((bf16[8,48,768]{2,1,0:T(8,128)(2,1)S(1)}, bf16[8,48,768]{2,1,0:T(8,128)(2,1)S(1)}, u32[]{:S(2)}, u32[]{:S(2)}) %collective-permute-start.1) | collective-permute-done | bytes 589856 | tf_op jit(solution)/shard_map/ppermute | solution.py:304
  36.7 0.0 copy-done.3
  36.7 0.0 copy-done.5
  36.7 0.0 copy-start.6
  36.7 0.8 %copy-done.6 = bf16[8,48,768]{2,1,0:T(8,128)(2,1)} copy-done((bf16[8,48,768]{2,1,0:T(8,128)(2,1)}, bf16[8,48,768]{2,1,0:T(8,128)(2,1)S(1)}, u32[]{:S(2)}) %copy-start.6) | copy-done | bytes 589848
  37.5 8.3 %correlate.1 = bf16[2048,512]{1,0:T(8,128)(2,1)} custom-call(s32[3]{0:T(128)} %copy-done.3, s32[256,1]{1,0:T(8,128)} %copy.9.refs_1_, bf16[8,48,768]{2,1,0:T(8,128)(2,1)} %copy-done.5, bf16[8,48,768]{2,1,0:T(8,128)(2,1)} %copy-done.6, bf16[768,512]{1,0:T(8,128)(2,1)} %constant.52.refs_4_), custom_call_target="tpu_custom_call" | custom-call | tf_op jit(solution)/shard_map/correlate/pallas_call | solution.py:270
Async XLA Ops:
  0.0 15.8 %copy-start = (bf16[512,768]{1,0:T(8,128)(2,1)S(1)}, bf16[512,768]{1,0:T(8,128)(2,1)}, u32[]{:S(2)}) copy-start(bf16[512,768]{1,0:T(8,128)(2,1)} %constant.50.inner_ref) | copy-start | bytes 2359300
  0.0 15.8 %copy-start.2 = (f32[33,1,768]{2,1,0:T(1,128)S(1)}, f32[33,1,768]{2,1,0:T(1,128)}, u32[]{:S(2)}) copy-start(f32[33,1,768]{2,1,0:T(1,128)} %constant.46.clone.phase_ref) | copy-start | bytes 304132
  0.0 23.4 %copy-start.1 = (bf16[384,384]{1,0:T(8,128)(2,1)S(1)}, bf16[384,384]{1,0:T(8,128)(2,1)}, u32[]{:S(2)}) copy-start(bf16[384,384]{1,0:T(8,128)(2,1)} %constant.51.band_ref) | copy-start | bytes 884740
  0.0 15.8 %copy-start.4 = (s32[3]{0:T(128)S(1)}, s32[3]{0:T(128)}, u32[]{:S(2)}) copy-start(s32[3]{0:T(128)} %start_ref.1) | copy-start | bytes 40
  2.6 32.1 %copy-start.7 = (s32[256]{0:T(256)S(1)}, s32[256]{0:T(256)}, u32[]{:S(2)}) copy-start(s32[256]{0:T(256)} %param.10) | copy-start | bytes 3076
  2.6 13.2 %all-to-all-start = ((bf16[8,16,1152]{2,1,0:T(8,128)(2,1)}), bf16[8,16,1152]{2,1,0:T(8,128)(2,1)S(1)}, u32[]{:S(2)}, u32[]{:S(2)}) async-start(bf16[8,16,1152]{2,1,0:T(8,128)(2,1)} %decimate.1), calls=%async_computation | async-start | bytes 589824 | tf_op jit(solution)/shard_map/all_to_all | solution.py:296
  9.0 27.7 %copy-start.3 = (s32[3]{0:T(128)}, s32[3]{0:T(128)S(1)}, u32[]{:S(2)}) copy-start(s32[3]{0:T(128)S(1)} %pad_add_fusion.place_ref.refs_0_) | copy-start | bytes 40
  17.3 6.1 %collective-permute-start = (bf16[48,768]{1,0:T(8,128)(2,1)S(1)}, bf16[48,768]{1,0:T(8,128)(2,1)S(1)}, u32[]{:S(2)}, u32[]{:S(2)}) collective-permute-start(bf16[48,768]{1,0:T(8,128)(2,1)S(1)} %get-tuple-element.8), channel_id=1, source_target_pairs={{0,16},{2,18},{4,20},{6,22},{8,24},{10,26},{12,28},{14,30},{16,0},... | collective-permute-start | bytes 221192 | tf_op jit(solution)/shard_map/ppermute | solution.py:299
  34.7 2.0 %copy-start.5 = (bf16[8,48,768]{2,1,0:T(8,128)(2,1)}, bf16[8,48,768]{2,1,0:T(8,128)(2,1)S(1)}, u32[]{:S(2)}) copy-start(bf16[8,48,768]{2,1,0:T(8,128)(2,1)S(1)} %all_to_all.10.refs_2_) | copy-start | bytes 1769476
  34.7 2.0 %collective-permute-start.1 = (bf16[8,48,768]{2,1,0:T(8,128)(2,1)S(1)}, bf16[8,48,768]{2,1,0:T(8,128)(2,1)S(1)}, u32[]{:S(2)}, u32[]{:S(2)}) collective-permute-start(bf16[8,48,768]{2,1,0:T(8,128)(2,1)S(1)} %all_to_all.10.refs_2_), channel_id=1, source_target_pairs={{1,0},{0,1},{3,2},{2,3},{5,4},{4,5},{7,6},{6,7},{9,8},{8,9},{11,10... | collective-permute-start | bytes 1769480 | tf_op jit(solution)/shard_map/ppermute | solution.py:304
  36.7 0.8 %copy-start.6 = (bf16[8,48,768]{2,1,0:T(8,128)(2,1)}, bf16[8,48,768]{2,1,0:T(8,128)(2,1)S(1)}, u32[]{:S(2)}) copy-start(bf16[8,48,768]{2,1,0:T(8,128)(2,1)S(1)} %collective-permute-done.1.refs_3_) | copy-start | bytes 1769476

commit v2 on v1

--- a/solution.py
+++ b/solution.py
@@ -206,81 +206,124 @@
     )(own, other, band_table())
 
 
-def correlate_kernel(groups, group, place_ref, chan_ref, *refs):
-    spectra, (basis_ref, out_ref, source, receiver, cross) = refs[:groups], refs[groups:]
+def correlate_kernel(groups, group, block, place_ref, chan_ref, *refs):
+    spectra = refs[:groups]
+    basis_ref, out_ref, source, receiver, cross_even, cross_odd, lagged, sent = refs[groups:]
     peers = spectra[0].shape[0]
     rows = HALVES * group
     channels = peers * rows
-    many = source.shape[1]
-    block = out_ref.shape[0] // (groups * group)
+    receivers = groups * group
+    many = chan_ref.shape[1]
+    blocks = many // block
     half, peer, mine = place_ref[0], place_ref[1], place_ref[2]
 
-    @pl.when(pl.program_id(0) == 0)
-    def _():
-        wanted = chan_ref[pl.ds(pl.multiple_of(mine * many, many), many), :]
-        spot = lax.broadcasted_iota(jnp.int32, (many, channels), 1)
-        total = [0.0] * NSEG
-        for step, spectrum in enumerate(spectra):
-            owner = lax.rem(mine + step, groups)
-            local = wanted - owner * channels
-            in_half = jnp.bitwise_and(local, channels // HALVES - 1)
-            place = (in_half // group) * rows + (local // (channels // HALVES)) * group + in_half % group
-            place = jnp.where((local >= 0) & (local < channels), place, -1)
-            pick = (spot == place).astype(jnp.float32).astype(jnp.bfloat16)
-            for number in range(NSEG):
-                held = spectrum[:, number * rows : (number + 1) * rows, :]
-                total[number] = total[number] + dot(pick, held.reshape(channels, 2 * NBIN))
-                here = spectrum[peer, number * rows : (number + 1) * rows, :].astype(jnp.float32)
-                here = jnp.where(half == 0, here[:group], here[group:]) * (1.0 / NSEG)
-                receiver[number, owner] = here
+    wanted = chan_ref[pl.ds(mine, 1), :]
+    spot = lax.broadcasted_iota(jnp.int32, (channels, many), 0)
+    picks = []
+    for step, spectrum in enumerate(spectra):
+        owner = lax.rem(mine + step, groups)
+        local = wanted - owner * channels
+        in_half = jnp.bitwise_and(local, channels // HALVES - 1)
+        row = (in_half // group) * rows + (local // (channels // HALVES)) * group + in_half % group
+        row = jnp.where((local >= 0) & (local < channels), row, -1)
+        picks.append((spot == row).astype(jnp.float32))
         for number in range(NSEG):
-            source[number] = total[number]
-
-    start = pl.program_id(0) * block
-    for chunk in range(CHUNKS):
-        re_at = slice(chunk * LANES, (chunk + 1) * LANES)
-        im_at = slice(NBIN + chunk * LANES, NBIN + (chunk + 1) * LANES)
-        recv = [receiver[number].reshape(groups * group, 2 * NBIN) for number in range(NSEG)]
-        for k in range(block):
-            total_re = total_im = 0.0
-            for number in range(NSEG):
-                row = source[number, pl.ds(start + k, 1), :]
-                source_re, source_im = row[:, re_at], row[:, im_at]
-                recv_re, recv_im = recv[number][:, re_at], recv[number][:, im_at]
-                total_re = total_re + (source_re * recv_re + source_im * recv_im)
-                total_im = total_im + (source_re * recv_im - source_im * recv_re)
-            at = slice(k * groups * group, (k + 1) * groups * group)
-            cross[at, re_at] = total_re.astype(jnp.bfloat16)
-            cross[at, im_at] = total_im.astype(jnp.bfloat16)
-    out_ref[...] = dot(cross[...], basis_ref[...]).astype(jnp.bfloat16)
+            here = spectrum[peer, number * rows : (number + 1) * rows, :].astype(jnp.float32)
+            here = jnp.where(half == 0, here[:group], here[group:]) * (1.0 / NSEG)
+            receiver[number, owner] = here
+    pick = jnp.concatenate(picks, axis=0).T.astype(jnp.bfloat16)
+    for number in range(NSEG):
+        at = slice(number * rows, (number + 1) * rows)
+        held = [spectrum[:, at, :].reshape(channels, 2 * NBIN) for spectrum in spectra]
+        held = jnp.concatenate(held, axis=0)
+        for pair in range(CHUNKS):
+            found = dot(pick, held[:, 2 * pair * LANES : 2 * (pair + 1) * LANES])
+            source[number, 2 * pair] = found[:, :LANES]
+            source[number, 2 * pair + 1] = found[:, LANES:]
+
+    def fill(number, cross):
+        for chunk in range(CHUNKS):
+            re_at = slice(chunk * LANES, (chunk + 1) * LANES)
+            im_at = slice(NBIN + chunk * LANES, NBIN + (chunk + 1) * LANES)
+            recv = [receiver[seg].reshape(receivers, 2 * NBIN) for seg in range(NSEG)]
+            recv_re = [part[:, re_at].astype(jnp.bfloat16) for part in recv]
+            recv_im = [part[:, im_at].astype(jnp.bfloat16) for part in recv]
+            for k in range(block):
+                total_re = total_im = None
+                for seg in range(NSEG):
+                    same = pl.ds(number * block + k, 8, stride=0)
+                    source_re = source[seg, chunk, same, :]
+                    source_im = source[seg, CHUNKS + chunk, same, :]
+                    source_re = jnp.concatenate([source_re] * (receivers // 8), axis=0)
+                    source_im = jnp.concatenate([source_im] * (receivers // 8), axis=0)
+                    source_re = source_re.astype(jnp.bfloat16)
+                    source_im = source_im.astype(jnp.bfloat16)
+                    part_re = source_re * recv_re[seg] + source_im * recv_im[seg]
+                    part_im = source_re * recv_im[seg] - source_im * recv_re[seg]
+                    total_re = part_re if seg == 0 else total_re + part_re
+                    total_im = part_im if seg == 0 else total_im + part_im
+                at = slice(k * receivers, (k + 1) * receivers)
+                cross[at, re_at] = total_re
+                cross[at, im_at] = total_im
+
+    def span(number):
+        size = block * receivers
+        return pl.ds(pl.multiple_of(number * size, size), size)
+
+    def lag(number, cross):
+        lagged[span(number), :] = dot(cross[...], basis_ref[...]).astype(jnp.bfloat16)
+
+    def store(number):
+        at = span(number)
+        return pltpu.make_async_copy(lagged.at[at], out_ref.at[at], sent.at[number])
+
+    fill(0, cross_even)
+
+    def step(number, carry):
+        lag(2 * number, cross_even)
+        fill(2 * number + 1, cross_odd)
+        store(2 * number).start()
+        lag(2 * number + 1, cross_odd)
+        fill(jnp.minimum(2 * number + 2, blocks - 1), cross_even)
+        store(2 * number + 1).start()
+        return carry
+
+    lax.fori_loop(0, blocks // 2, step, 0)
+
+    def finish(number, carry):
+        store(number).wait()
+        return carry
+
+    lax.fori_loop(0, blocks, finish, 0)
 
 
 def correlate(place, src_chan, spectra, group):
     groups = len(spectra)
     many = src_chan.shape[0] // groups
-    rows = groups * group
-    block = max(1, 256 // rows)
+    receivers = groups * group
+    block = 256 // receivers
+    rows = block * receivers
 
     def kernel(*refs):
-        correlate_kernel(groups, group, *refs)
-
-    whole = lambda array: pl.BlockSpec(array.shape, lambda i: (0,) * array.ndim)
-    column = src_chan.reshape(-1, 1)
-    basis = lag_table()
+        correlate_kernel(groups, group, block, *refs)
+
+    held = sum(spectrum.size * spectrum.dtype.itemsize for spectrum in spectra)
     return pl.pallas_call(
         kernel,
-        out_shape=jax.ShapeDtypeStruct((many * rows, NLAG), jnp.bfloat16),
-        grid=(many // block,),
-        in_specs=[SMEM] + [whole(a) for a in (column, *spectra, basis)],
-        out_specs=pl.BlockSpec((block * rows, NLAG), lambda i: (i, 0)),
+        out_shape=jax.ShapeDtypeStruct((many * receivers, NLAG), jnp.bfloat16),
+        in_specs=[SMEM] + [VMEM] * (groups + 2),
+        out_specs=pl.BlockSpec(memory_space=pl.ANY),
         scratch_shapes=[
-            pltpu.VMEM((NSEG, many, 2 * NBIN), jnp.float32),
+            pltpu.VMEM((NSEG, 2 * CHUNKS, many, LANES), jnp.float32),
             pltpu.VMEM((NSEG, groups, group, 2 * NBIN), jnp.float32),
-            pltpu.VMEM((block * rows, 2 * NBIN), jnp.bfloat16),
+            pltpu.VMEM((rows, 2 * NBIN), jnp.bfloat16),
+            pltpu.VMEM((rows, 2 * NBIN), jnp.bfloat16),
+            pltpu.VMEM((many * receivers, NLAG), jnp.bfloat16),
+            pltpu.SemaphoreType.DMA((many // block,)),
         ],
-        compiler_params=pltpu.CompilerParams(vmem_limit_bytes=56 * 1024 * 1024),
+        compiler_params=pltpu.CompilerParams(vmem_limit_bytes=16 * 1024 * 1024 + 2 * held),
         name="correlate",
-    )(place, column, *spectra, basis)
+    )(place, src_chan.reshape(groups, many), *spectra, lag_table())
 
 
 def on_device(strain, seg_start, src_chan):

time: 46.2 us -> 42 us (0.909)
  Pallas kernels: 12.6 us -> 9.27 us
  local copies, waits for them, and re-layouts: 1.71 us -> 0.02 us
  waiting for transfers between devices: 11.4 us -> 12.3 us
    pallas_call x1, Pallas kernels: 8.33 us -> 4.97 us  [correlate(): pl.pallas_call(kernel, out_shape=jax.ShapeDtypeStruct((many * receivers,...]
    ppermute x1, waiting for transfers between devices: 1.13 us -> 2 us  [on_device(): spectra.append(lax.ppermute(held, 'src', pairs))]
    reshape x1 -> x0, local copies, waits for them, and re-layouts: 0.87 us -> none  [correlate(): column = src_chan.reshape(-1, 1)]
    unnamed x16 -> x12, local copies, waits for them, and re-layouts: 0.84 us -> 0.02 us
  transfers between devices with their start and end apart: 3 -> 3, of which waited for: 3 -> 3; matrix products, arithmetic and copies ran while one was open for 2% -> 0% of each run, Pallas kernels for 0% -> 0%
where the time goes in v2:
time: 42 us; the launch traced here: 41.7 us
  waiting for transfers between devices  12.3 us (29%)
  blocking collectives  11 us (26%)
  Pallas kernels  9.27 us (22%)
  starting transfers between devices  8.98 us (21%)
    all_to_all x1, blocking collectives, on_device(): lax.all_to_all(white, 'chan', 0, 0, tiled=True, axis_index_groups=cubes)  11 us
    all_to_all x1, waiting for transfers between devices, on_device(): lax.all_to_all(sent, 'chan', 0, 0, tiled=True, axis_index_groups=cubes)  6.84 us
    all_to_all x1, starting transfers between devices, on_device(): lax.all_to_all(sent, 'chan', 0, 0, tiled=True, axis_index_groups=cubes)  6.33 us
    pallas_call x1, Pallas kernels, correlate(): pl.pallas_call(kernel, out_shape=jax.ShapeDtypeStruct((many * receivers,...  4.97 us
    ppermute x1, waiting for transfers between devices, on_device(): white = whiten(own, lax.ppermute(send, 'chan', across), peers)  3.46 us
    ppermute x1, starting transfers between devices, on_device(): white = whiten(own, lax.ppermute(send, 'chan', across), peers)  2.65 us
    pallas_call x1, Pallas kernels, decimate(): pl.pallas_call(decimate_kernel, out_shape=jax.ShapeDtypeStruct((peers, HA...  2.57 us
    ppermute x1, waiting for transfers between devices, on_device(): spectra.append(lax.ppermute(held, 'src', pairs))  2 us
  transfers between devices with their start and end apart: 3, of which 3 were waited for; matrix products, arithmetic and copies ran while one was open for 0% of the time, Pallas kernels for 0%

profile of v2, /device:TPU:0, one launch (start us, length us, event | category | flops | bytes accessed | tf_op | source)
XLA Modules:
  0.0 41.7 jit_solution(12369824135767352246)
XLA Ops:
  0.0 0.0 copy-start.1
  0.0 0.0 copy-start.3
  0.0 0.0 copy-start.2
  0.0 0.0 copy-start.5
  0.0 2.6 %decimate.1 = bf16[8,16,1152]{2,1,0:T(8,128)(2,1)} custom-call(bf16[2,64,4096]{2,1,0:T(8,128)(2,1)} %bitcast.7, bf16[640,128]{1,0:T(8,128)(2,1)} %constant.49.table_ref), custom_call_target="tpu_custom_call" | custom-call | tf_op jit(solution)/shard_map/decimate/pallas_call | solution.py:100
  2.6 0.0 copy-start
  2.6 0.0 copy-start.4
  2.6 6.3 %all-to-all-start = ((bf16[8,16,1152]{2,1,0:T(8,128)(2,1)}), bf16[8,16,1152]{2,1,0:T(8,128)(2,1)S(1)}, u32[]{:S(2)}, u32[]{:S(2)}) async-start(bf16[8,16,1152]{2,1,0:T(8,128)(2,1)} %decimate.1), calls=%async_computation | async-start | bytes 589824 | tf_op jit(solution)/shard_map/all_to_all | solution.py:339
  8.9 0.1 pad_add_fusion.place_ref.refs_0_
  9.0 6.8 %all-to-all-done.recv_ref = bf16[8,16,1152]{2,1,0:T(8,128)(2,1)S(1)} async-done(((bf16[8,16,1152]{2,1,0:T(8,128)(2,1)}), bf16[8,16,1152]{2,1,0:T(8,128)(2,1)S(1)}, u32[]{:S(2)}, u32[]{:S(2)}) %all-to-all-start) | async-done | bytes 294944 | tf_op jit(solution)/shard_map/all_to_all | solution.py:339
  15.8 0.0 copy-done.1
  15.8 0.0 copy-done.3
  15.8 0.0 copy-done.5
  15.8 1.5 %spectrum.1 = (f32[48,768]{1,0:T(8,128)S(1)}, bf16[48,768]{1,0:T(8,128)(2,1)S(1)}) custom-call(s32[3]{0:T(128)S(1)} %pad_add_fusion.place_ref.refs_0_, s32[3]{0:T(128)S(1)} %copy-done.5, bf16[8,16,1152]{2,1,0:T(8,128)(2,1)S(1)} %all-to-all-done.recv_ref, bf16[512,768]{1,0:T(8,128)(2,1)S(1)} %copy-done.1, f32[33,1,768]{2,1,0:T(1,128)S(1)} %copy-done.3), custom_call_target="tpu_custom_call" | custom-call | tf_op jit(solution)/shard_map/spectrum/pallas_call | solution.py:166
  17.3 2.7 %collective-permute-start = (bf16[48,768]{1,0:T(8,128)(2,1)S(1)}, bf16[48,768]{1,0:T(8,128)(2,1)S(1)}, u32[]{:S(2)}, u32[]{:S(2)}) collective-permute-start(bf16[48,768]{1,0:T(8,128)(2,1)S(1)} %get-tuple-element.8), channel_id=1, source_target_pairs={{0,16},{2,18},{4,20},{6,22},{8,24},{10,26},{12,28},{14,30},{16,0},... | collective-permute-start | bytes 221192 | tf_op jit(solution)/shard_map/ppermute | solution.py:342
  19.9 3.5 %collective-permute-done.other_ref = bf16[48,768]{1,0:T(8,128)(2,1)S(1)} collective-permute-done((bf16[48,768]{1,0:T(8,128)(2,1)S(1)}, bf16[48,768]{1,0:T(8,128)(2,1)S(1)}, u32[]{:S(2)}, u32[]{:S(2)}) %collective-permute-start) | collective-permute-done | bytes 73760 | tf_op jit(solution)/shard_map/ppermute | solution.py:342
  23.4 0.0 copy-done.2
  23.4 0.3 whiten.1
  23.7 11.0 %all_to_all.10.refs_2_ = bf16[8,48,768]{2,1,0:T(8,128)(2,1)S(1)} all-to-all(bf16[8,48,768]{2,1,0:T(8,128)(2,1)S(1)} %whiten.1), channel_id=1, replica_groups={{0,2,4,6,8,10,12,14},{16,18,20,22,24,26,28,30},{1,3,5,7,9,11,13,15},{17..., dimensions={0} | all-to-all | bytes 1179648 | tf_op jit(solution)/shard_map/all_to_all | solution.py:343
  34.7 0.0 collective-permute-start.1
  34.7 2.0 %collective-permute-done.1.refs_3_ = bf16[8,48,768]{2,1,0:T(8,128)(2,1)S(1)} collective-permute-done((bf16[8,48,768]{2,1,0:T(8,128)(2,1)S(1)}, bf16[8,48,768]{2,1,0:T(8,128)(2,1)S(1)}, u32[]{:S(2)}, u32[]{:S(2)}) %collective-permute-start.1) | collective-permute-done | bytes 589856 | tf_op jit(solution)/shard_map/ppermute | solution.py:347
  36.7 0.0 copy-done
  36.7 0.0 copy-done.4
  36.7 5.0 %correlate.1 = bf16[2048,512]{1,0:T(8,128)(2,1)} custom-call(s32[3]{0:T(128)S(1)} %pad_add_fusion.place_ref.refs_0_, s32[2,128]{1,0:T(2,128)S(1)} %bitcast.6, bf16[8,48,768]{2,1,0:T(8,128)(2,1)S(1)} %all_to_all.10.refs_2_, bf16[8,48,768]{2,1,0:T(8,128)(2,1)S(1)} %collective-permute-done.1.refs_3_, bf16[768,512]{1,0:T(8,128)(2,1)S(1)} %copy-done), custom_call_target="tpu_custom_call" | custom-call | tf_op jit(solution)/shard_map/correlate/pallas_call | solution.py:311
Async XLA Ops:
  0.0 15.8 %copy-start.1 = (bf16[512,768]{1,0:T(8,128)(2,1)S(1)}, bf16[512,768]{1,0:T(8,128)(2,1)}, u32[]{:S(2)}) copy-start(bf16[512,768]{1,0:T(8,128)(2,1)} %constant.50.inner_ref) | copy-start | bytes 2359300
  0.0 15.8 %copy-start.3 = (f32[33,1,768]{2,1,0:T(1,128)S(1)}, f32[33,1,768]{2,1,0:T(1,128)}, u32[]{:S(2)}) copy-start(f32[33,1,768]{2,1,0:T(1,128)} %constant.46.clone.phase_ref) | copy-start | bytes 304132
  0.0 23.4 %copy-start.2 = (bf16[384,384]{1,0:T(8,128)(2,1)S(1)}, bf16[384,384]{1,0:T(8,128)(2,1)}, u32[]{:S(2)}) copy-start(bf16[384,384]{1,0:T(8,128)(2,1)} %constant.51.band_ref) | copy-start | bytes 884740
  0.0 15.8 %copy-start.5 = (s32[3]{0:T(128)S(1)}, s32[3]{0:T(128)}, u32[]{:S(2)}) copy-start(s32[3]{0:T(128)} %start_ref.1) | copy-start | bytes 40
  2.6 34.1 %copy-start = (bf16[768,512]{1,0:T(8,128)(2,1)S(1)}, bf16[768,512]{1,0:T(8,128)(2,1)}, u32[]{:S(2)}) copy-start(bf16[768,512]{1,0:T(8,128)(2,1)} %constant.52.refs_4_) | copy-start | bytes 2359300
  2.6 34.1 %copy-start.4 = (s32[256]{0:T(256)S(1)}, s32[256]{0:T(256)}, u32[]{:S(2)}) copy-start(s32[256]{0:T(256)} %param.10) | copy-start | bytes 3076
  2.6 13.2 %all-to-all-start = ((bf16[8,16,1152]{2,1,0:T(8,128)(2,1)}), bf16[8,16,1152]{2,1,0:T(8,128)(2,1)S(1)}, u32[]{:S(2)}, u32[]{:S(2)}) async-start(bf16[8,16,1152]{2,1,0:T(8,128)(2,1)} %decimate.1), calls=%async_computation | async-start | bytes 589824 | tf_op jit(solution)/shard_map/all_to_all | solution.py:339
  17.3 6.1 %collective-permute-start = (bf16[48,768]{1,0:T(8,128)(2,1)S(1)}, bf16[48,768]{1,0:T(8,128)(2,1)S(1)}, u32[]{:S(2)}, u32[]{:S(2)}) collective-permute-start(bf16[48,768]{1,0:T(8,128)(2,1)S(1)} %get-tuple-element.8), channel_id=1, source_target_pairs={{0,16},{2,18},{4,20},{6,22},{8,24},{10,26},{12,28},{14,30},{16,0},... | collective-permute-start | bytes 221192 | tf_op jit(solution)/shard_map/ppermute | solution.py:342
  34.7 2.0 %collective-permute-start.1 = (bf16[8,48,768]{2,1,0:T(8,128)(2,1)S(1)}, bf16[8,48,768]{2,1,0:T(8,128)(2,1)S(1)}, u32[]{:S(2)}, u32[]{:S(2)}) collective-permute-start(bf16[8,48,768]{2,1,0:T(8,128)(2,1)S(1)} %all_to_all.10.refs_2_), channel_id=1, source_target_pairs={{1,0},{0,1},{3,2},{2,3},{5,4},{4,5},{7,6},{6,7},{9,8},{8,9},{11,10... | collective-permute-start | bytes 1769480 | tf_op jit(solution)/shard_map/ppermute | solution.py:347

commit v3 on v2

--- a/solution.py
+++ b/solution.py
@@ -22,6 +22,16 @@
 SMEM = pl.BlockSpec(memory_space=pltpu.SMEM)
 
 
+def chunked(real, imag):
+    parts = np.stack([real, imag], axis=1).reshape(-1, 2, CHUNKS, LANES)
+    return parts.transpose(0, 2, 1, 3).reshape(-1, 2 * NBIN)
+
+
+def places(chunk):
+    start = 2 * chunk * LANES
+    return slice(start, start + LANES), slice(start + LANES, start + 2 * LANES)
+
+
 def filter_table():
     length = 4 * DEC
     offsets = np.arange(length)
@@ -32,7 +42,8 @@
         * (0.54 - 0.46 * np.cos(2.0 * np.pi * (offsets + 0.5) / length))
     )
     coeffs = coeffs / coeffs.sum()
-    tap = np.arange(DEC * LANES + LANES)[:, None] - DEC * np.arange(LANES)[None, :]
+    first = np.concatenate([np.arange(LANES), np.arange(LANES) - LANES])
+    tap = np.arange(BLOCK)[:, None] - DEC * first[None, :]
     inside = (tap >= 0) & (tap < length)
     values = np.where(inside, coeffs[np.clip(tap, 0, length - 1)], 0.0)
     return jnp.asarray(values, jnp.float32).astype(jnp.bfloat16)
@@ -41,15 +52,14 @@
 def inner_table():
     bin_ids = BIN_LOW + np.arange(NBIN)
     angle = 2.0 * np.pi * np.mod(np.outer(np.arange(BLOCK), bin_ids), SEG) / SEG
-    parts = np.stack([np.cos(angle), -np.sin(angle)], axis=1)
-    parts = parts.reshape(BLOCK, 2, CHUNKS, LANES).transpose(0, 2, 1, 3)
-    return jnp.asarray(parts.reshape(BLOCK, 2 * NBIN), jnp.float32).astype(jnp.bfloat16)
+    parts = chunked(np.cos(angle), -np.sin(angle))
+    return jnp.asarray(parts, jnp.float32).astype(jnp.bfloat16)
 
 
 def phase_table(first, count):
     bin_ids = BIN_LOW + np.arange(NBIN)
     angle = 2.0 * np.pi * np.mod(np.outer(BLOCK * (first + np.arange(count)), bin_ids), SEG) / SEG
-    parts = np.stack([np.cos(angle), np.sin(angle)], axis=1) / math.sqrt(SEG)
+    parts = chunked(np.cos(angle), np.sin(angle)) / math.sqrt(SEG)
     return jnp.asarray(parts.reshape(count, 1, 2 * NBIN), jnp.float32)
 
 
@@ -57,7 +67,7 @@
     bin_ids = BIN_LOW + np.arange(NBIN)
     delays = np.arange(NLAG) - NLAG // 2
     angles = 2.0 * np.pi * np.mod(np.outer(bin_ids, delays), SEG) / SEG
-    basis = np.concatenate([np.cos(angles), -np.sin(angles)], axis=0) / np.sqrt(NBIN)
+    basis = chunked(np.cos(angles).T, -np.sin(angles).T).T / np.sqrt(NBIN)
     return jnp.asarray(basis, jnp.float32).astype(jnp.bfloat16)
 
 
@@ -71,41 +81,53 @@
     return jnp.dot(left, right, preferred_element_type=jnp.float32)
 
 
-def decimate_kernel(strain_ref, table_ref, out_ref):
-    halves, rows, length = strain_ref.shape
+def decimate_kernel(strain_hbm, table_hbm, out_ref, strain, table, arrived):
+    halves, rows, length = strain.shape
     group = out_ref.shape[1] // halves
     tiles = length // BLOCK
-    x = strain_ref[...].reshape(halves * rows, length)
-
-    def put(values, at):
+    many = halves * rows
+    reads = [
+        pltpu.make_async_copy(table_hbm, table, arrived.at[0]),
+        pltpu.make_async_copy(strain_hbm, strain, arrived.at[1]),
+    ]
+    for read in reads:
+        read.start()
+    for read in reads:
+        read.wait()
+    x = strain[...].reshape(many, length)
+    stacked = [x[:, tile * BLOCK : (tile + 1) * BLOCK] for tile in range(tiles)]
+    sums = dot(jnp.concatenate(stacked, axis=0), table[...])
+    for tile in range(tiles + 1):
+        if tile == tiles:
+            values = sums[:many, LANES:]
+        else:
+            values = sums[tile * many : (tile + 1) * many, :LANES]
+        if tile + 1 < tiles:
+            values = values + sums[(tile + 1) * many : (tile + 2) * many, LANES:]
         for peer in range(rows // group):
             part = [
                 values[half * rows + peer * group : half * rows + (peer + 1) * group]
                 for half in range(halves)
             ]
-            out_ref[peer, :, at : at + LANES] = jnp.concatenate(part, axis=0).astype(jnp.bfloat16)
-
-    for tile in range(tiles):
-        stop = min(BLOCK * tile + BLOCK + LANES, length)
-        piece = x[:, BLOCK * tile : stop]
-        put(dot(piece, table_ref[: piece.shape[1], :]), tile * LANES)
-    put(dot(x[:, :LANES], table_ref[BLOCK:, :]), tiles * LANES)
+            part = jnp.concatenate(part, axis=0).astype(jnp.bfloat16)
+            out_ref[peer, :, tile * LANES : (tile + 1) * LANES] = part
 
 
 def decimate(strain, peers, group):
     rows, length = strain.shape
     half_rows = rows // HALVES
     width = length // DEC + LANES
-    steps = 2
     return pl.pallas_call(
         decimate_kernel,
         out_shape=jax.ShapeDtypeStruct((peers, HALVES * group, width), jnp.bfloat16),
-        grid=(steps,),
-        in_specs=[
-            pl.BlockSpec((HALVES, half_rows // steps, length), lambda i: (0, i, 0)),
-            pl.BlockSpec((BLOCK + LANES, LANES), lambda i: (0, 0)),
+        in_specs=[pl.BlockSpec(memory_space=pl.ANY)] * 2,
+        out_specs=VMEM,
+        scratch_shapes=[
+            pltpu.VMEM((HALVES, half_rows, length), jnp.bfloat16),
+            pltpu.VMEM((BLOCK, 2 * LANES), jnp.bfloat16),
+            pltpu.SemaphoreType.DMA((2,)),
         ],
-        out_specs=pl.BlockSpec((peers // steps, HALVES * group, width), lambda i: (i, 0, 0)),
+        compiler_params=pltpu.CompilerParams(vmem_limit_bytes=16 * 1024 * 1024),
         name="decimate",
     )(strain.reshape(HALVES, half_rows, length), filter_table())
 
@@ -140,10 +162,8 @@
         edge[number * rows : (number + 1) * rows, :] = part
     many = NSEG * rows
     for chunk in range(CHUNKS):
-        columns = slice(2 * chunk * LANES, 2 * (chunk + 1) * LANES)
-        re_at = slice(chunk * LANES, (chunk + 1) * LANES)
-        im_at = slice(NBIN + chunk * LANES, NBIN + (chunk + 1) * LANES)
-        table = inner_ref[:, columns]
+        re_at, im_at = places(chunk)
+        table = inner_ref[:, re_at.start : im_at.stop]
         body = dot(lhs[...], table)
         parts = [dot(edge[...], table[BLOCK - LANES :])]
         parts += [body[block * many : (block + 1) * many] for block in range(blocks)]
@@ -182,17 +202,20 @@
 
 def whiten_kernel(own_ref, other_ref, band_ref, out_ref):
     total = own_ref[...] + other_ref[...].astype(jnp.float32)
-    real_part, imag_part = total[:, :NBIN], total[:, NBIN:]
+    real_part = jnp.concatenate([total[:, places(chunk)[0]] for chunk in range(CHUNKS)], axis=1)
+    imag_part = jnp.concatenate([total[:, places(chunk)[1]] for chunk in range(CHUNKS)], axis=1)
     energy = real_part * real_part + imag_part * imag_part
     high = energy.astype(jnp.bfloat16)
     low = (energy - high.astype(jnp.float32)).astype(jnp.bfloat16)
     smooth = (dot(high, band_ref[...]) + dot(low, band_ref[...])) / 65.0
     inverse = lax.rsqrt(smooth + 1e-05)
-    white_re = (real_part * inverse).astype(jnp.bfloat16)
-    white_im = (imag_part * inverse).astype(jnp.bfloat16)
+    white = []
+    for chunk in range(CHUNKS):
+        at = slice(chunk * LANES, (chunk + 1) * LANES)
+        white += [real_part[:, at] * inverse[:, at], imag_part[:, at] * inverse[:, at]]
+    white = jnp.concatenate(white, axis=1).astype(jnp.bfloat16)
     for peer in range(out_ref.shape[0]):
-        out_ref[peer, :, :NBIN] = white_re
-        out_ref[peer, :, NBIN:] = white_im
+        out_ref[peer] = white
 
 
 def whiten(own, other, peers):
@@ -232,19 +255,19 @@
             here = jnp.where(half == 0, here[:group], here[group:]) * (1.0 / NSEG)
             receiver[number, owner] = here
     pick = jnp.concatenate(picks, axis=0).T.astype(jnp.bfloat16)
-    for number in range(NSEG):
-        at = slice(number * rows, (number + 1) * rows)
-        held = [spectrum[:, at, :].reshape(channels, 2 * NBIN) for spectrum in spectra]
-        held = jnp.concatenate(held, axis=0)
-        for pair in range(CHUNKS):
-            found = dot(pick, held[:, 2 * pair * LANES : 2 * (pair + 1) * LANES])
-            source[number, 2 * pair] = found[:, :LANES]
-            source[number, 2 * pair + 1] = found[:, LANES:]
-
-    def fill(number, cross):
-        for chunk in range(CHUNKS):
-            re_at = slice(chunk * LANES, (chunk + 1) * LANES)
-            im_at = slice(NBIN + chunk * LANES, NBIN + (chunk + 1) * LANES)
+
+    def get(chunk):
+        columns = slice(2 * chunk * LANES, 2 * (chunk + 1) * LANES)
+        for number in range(NSEG):
+            at = slice(number * rows, (number + 1) * rows)
+            held = [part[:, at, columns].reshape(channels, 2 * LANES) for part in spectra]
+            found = dot(pick, jnp.concatenate(held, axis=0))
+            source[number, 2 * chunk] = found[:, :LANES]
+            source[number, 2 * chunk + 1] = found[:, LANES:]
+
+    def fill(number, cross, chunks):
+        for chunk in chunks:
+            re_at, im_at = places(chunk)
             recv = [receiver[seg].reshape(receivers, 2 * NBIN) for seg in range(NSEG)]
             recv_re = [part[:, re_at].astype(jnp.bfloat16) for part in recv]
             recv_im = [part[:, im_at].astype(jnp.bfloat16) for part in recv]
@@ -252,8 +275,8 @@
                 total_re = total_im = None
                 for seg in range(NSEG):
                     same = pl.ds(number * block + k, 8, stride=0)
-                    source_re = source[seg, chunk, same, :]
-                    source_im = source[seg, CHUNKS + chunk, same, :]
+                    source_re = source[seg, 2 * chunk, same, :]
+                    source_im = source[seg, 2 * chunk + 1, same, :]
                     source_re = jnp.concatenate([source_re] * (receivers // 8), axis=0)
                     source_im = jnp.concatenate([source_im] * (receivers // 8), axis=0)
                     source_re = source_re.astype(jnp.bfloat16)
@@ -266,8 +289,9 @@
                 cross[at, re_at] = total_re
                 cross[at, im_at] = total_im
 
+    size = block * receivers
+
     def span(number):
-        size = block * receivers
         return pl.ds(pl.multiple_of(number * size, size), size)
 
     def lag(number, cross):
@@ -277,18 +301,28 @@
         at = span(number)
         return pltpu.make_async_copy(lagged.at[at], out_ref.at[at], sent.at[number])
 
-    fill(0, cross_even)
+    everything = range(CHUNKS)
+    for chunk in everything:
+        get(chunk)
+        fill(0, cross_even, [chunk])
+
+    def pair(number):
+        lag(2 * number, cross_even)
+        fill(2 * number + 1, cross_odd, everything)
+        store(2 * number).start()
 
     def step(number, carry):
-        lag(2 * number, cross_even)
-        fill(2 * number + 1, cross_odd)
-        store(2 * number).start()
+        pair(number)
         lag(2 * number + 1, cross_odd)
-        fill(jnp.minimum(2 * number + 2, blocks - 1), cross_even)
+        fill(2 * number + 2, cross_even, everything)
         store(2 * number + 1).start()
         return carry
 
-    lax.fori_loop(0, blocks // 2, step, 0)
+    last = blocks // 2 - 1
+    lax.fori_loop(0, last, step, 0)
+    pair(last)
+    lag(2 * last + 1, cross_odd)
+    store(2 * last + 1).start()
 
     def finish(number, carry):
         store(number).wait()

time: 42 us -> 42.5 us (1.012)
  local copies, waits for them, and re-layouts: 0.02 us -> 2.22 us
  Pallas kernels: 9.27 us -> 7.57 us
    unnamed x12 -> x16, local copies, waits for them, and re-layouts: 0.02 us -> 2.22 us
    pallas_call x1, Pallas kernels: 2.57 us -> 1.26 us  [decimate(): pl.pallas_call(decimate_kernel, out_shape=jax.ShapeDtypeStruct((peers, HA...]
where the time goes in v3:
time: 42.5 us; the launch traced here: 42.2 us
  waiting for transfers between devices  12.3 us (29%)
  blocking collectives  11 us (26%)
  starting transfers between devices  8.98 us (21%)
  Pallas kernels  7.57 us (18%)
  local copies, waits for them, and re-layouts  2.22 us (5%)
    all_to_all x1, blocking collectives, on_device(): lax.all_to_all(white, 'chan', 0, 0, tiled=True, axis_index_groups=cubes)  11 us
    all_to_all x1, waiting for transfers between devices, on_device(): lax.all_to_all(sent, 'chan', 0, 0, tiled=True, axis_index_groups=cubes)  6.84 us
    all_to_all x1, starting transfers between devices, on_device(): lax.all_to_all(sent, 'chan', 0, 0, tiled=True, axis_index_groups=cubes)  6.33 us
    pallas_call x1, Pallas kernels, correlate(): pl.pallas_call(kernel, out_shape=jax.ShapeDtypeStruct((many * receivers,...  4.61 us
    ppermute x1, waiting for transfers between devices, on_device(): white = whiten(own, lax.ppermute(send, 'chan', across), peers)  3.46 us
    ppermute x1, starting transfers between devices, on_device(): white = whiten(own, lax.ppermute(send, 'chan', across), peers)  2.65 us
    unnamed x16, local copies, waits for them, and re-layouts  2.22 us
    ppermute x1, waiting for transfers between devices, on_device(): spectra.append(lax.ppermute(held, 'src', pairs))  2 us
  transfers between devices with their start and end apart: 3, of which 3 were waited for; matrix products, arithmetic and copies ran while one was open for 0% of the time, Pallas kernels for 0%

profile of v3, /device:TPU:0, one launch (start us, length us, event | category | flops | bytes accessed | tf_op | source)
XLA Modules:
  0.0 42.2 jit_solution(10061541528759235484)
XLA Ops:
  0.0 0.0 copy-start.7
  0.0 0.0 copy-start
  0.0 1.2 %copy-done = bf16[128,4096]{1,0:T(8,128)(2,1)S(1)} copy-done((bf16[128,4096]{1,0:T(8,128)(2,1)S(1)}, bf16[128,4096]{1,0:T(8,128)(2,1)}, u32[]{:S(2)}) %copy-start) | copy-done | bytes 1048600
  1.2 0.0 copy-start.4
  1.2 0.9 %copy-done.4 = bf16[512,256]{1,0:T(8,128)(2,1)S(1)} copy-done((bf16[512,256]{1,0:T(8,128)(2,1)S(1)}, bf16[512,256]{1,0:T(8,128)(2,1)}, u32[]{:S(2)}) %copy-start.4) | copy-done | bytes 262168
  2.2 0.0 copy-start.2
  2.2 0.0 copy-start.5
  2.2 0.0 copy-start.3
  2.2 1.3 %decimate.1 = bf16[8,16,1152]{2,1,0:T(8,128)(2,1)} custom-call(bf16[2,64,4096]{2,1,0:T(8,128)(2,1)S(1)} %bitcast.6, bf16[512,256]{1,0:T(8,128)(2,1)S(1)} %copy-done.4), custom_call_target="tpu_custom_call" | custom-call | tf_op jit(solution)/shard_map/decimate/pallas_call | solution.py:120
  3.5 0.0 copy-start.1
  3.5 0.0 copy-start.6
  3.5 6.3 %all-to-all-start = ((bf16[8,16,1152]{2,1,0:T(8,128)(2,1)}), bf16[8,16,1152]{2,1,0:T(8,128)(2,1)S(1)}, u32[]{:S(2)}, u32[]{:S(2)}) async-start(bf16[8,16,1152]{2,1,0:T(8,128)(2,1)} %decimate.1), calls=%async_computation | async-start | bytes 589824 | tf_op jit(solution)/shard_map/all_to_all | solution.py:373
  9.8 0.1 pad_add_fusion.place_ref.refs_0_
  9.9 6.8 %all-to-all-done.recv_ref = bf16[8,16,1152]{2,1,0:T(8,128)(2,1)S(1)} async-done(((bf16[8,16,1152]{2,1,0:T(8,128)(2,1)}), bf16[8,16,1152]{2,1,0:T(8,128)(2,1)S(1)}, u32[]{:S(2)}, u32[]{:S(2)}) %all-to-all-start) | async-done | bytes 294944 | tf_op jit(solution)/shard_map/all_to_all | solution.py:373
  16.7 0.0 copy-done.7
  16.7 0.0 copy-done.2
  16.7 0.0 copy-done.5
  16.7 1.4 %spectrum.1 = (f32[48,768]{1,0:T(8,128)S(1)}, bf16[48,768]{1,0:T(8,128)(2,1)S(1)}) custom-call(s32[3]{0:T(128)S(1)} %pad_add_fusion.place_ref.refs_0_, s32[3]{0:T(128)S(1)} %copy-done.7, bf16[8,16,1152]{2,1,0:T(8,128)(2,1)S(1)} %all-to-all-done.recv_ref, bf16[512,768]{1,0:T(8,128)(2,1)S(1)} %copy-done.2, f32[33,1,768]{2,1,0:T(1,128)S(1)} %copy-done.5), custom_call_target="tpu_custom_call" | custom-call | tf_op jit(solution)/shard_map/spectrum/pallas_call | solution.py:186
  18.2 2.6 %collective-permute-start = (bf16[48,768]{1,0:T(8,128)(2,1)S(1)}, bf16[48,768]{1,0:T(8,128)(2,1)S(1)}, u32[]{:S(2)}, u32[]{:S(2)}) collective-permute-start(bf16[48,768]{1,0:T(8,128)(2,1)S(1)} %get-tuple-element.8), channel_id=1, source_target_pairs={{0,16},{2,18},{4,20},{6,22},{8,24},{10,26},{12,28},{14,30},{16,0},... | collective-permute-start | bytes 221192 | tf_op jit(solution)/shard_map/ppermute | solution.py:376
  20.8 3.5 %collective-permute-done.other_ref = bf16[48,768]{1,0:T(8,128)(2,1)S(1)} collective-permute-done((bf16[48,768]{1,0:T(8,128)(2,1)S(1)}, bf16[48,768]{1,0:T(8,128)(2,1)S(1)}, u32[]{:S(2)}, u32[]{:S(2)}) %collective-permute-start) | collective-permute-done | bytes 73760 | tf_op jit(solution)/shard_map/ppermute | solution.py:376
  24.3 0.0 copy-done.3
  24.3 0.3 whiten.1
  24.6 11.0 %all_to_all.10.refs_2_ = bf16[8,48,768]{2,1,0:T(8,128)(2,1)S(1)} all-to-all(bf16[8,48,768]{2,1,0:T(8,128)(2,1)S(1)} %whiten.1), channel_id=1, replica_groups={{0,2,4,6,8,10,12,14},{16,18,20,22,24,26,28,30},{1,3,5,7,9,11,13,15},{17..., dimensions={0} | all-to-all | bytes 1179648 | tf_op jit(solution)/shard_map/all_to_all | solution.py:377
  35.6 0.0 collective-permute-start.1
  35.6 2.0 %collective-permute-done.1.refs_3_ = bf16[8,48,768]{2,1,0:T(8,128)(2,1)S(1)} collective-permute-done((bf16[8,48,768]{2,1,0:T(8,128)(2,1)S(1)}, bf16[8,48,768]{2,1,0:T(8,128)(2,1)S(1)}, u32[]{:S(2)}, u32[]{:S(2)}) %collective-permute-start.1) | collective-permute-done | bytes 589856 | tf_op jit(solution)/shard_map/ppermute | solution.py:381
  37.6 0.0 copy-done.1
  37.6 0.0 copy-done.6
  37.6 4.6 %correlate.1 = bf16[2048,512]{1,0:T(8,128)(2,1)} custom-call(s32[3]{0:T(128)S(1)} %pad_add_fusion.place_ref.refs_0_, s32[2,128]{1,0:T(2,128)S(1)} %bitcast.7, bf16[8,48,768]{2,1,0:T(8,128)(2,1)S(1)} %all_to_all.10.refs_2_, bf16[8,48,768]{2,1,0:T(8,128)(2,1)S(1)} %collective-permute-done.1.refs_3_, bf16[768,512]{1,0:T(8,128)(2,1)S(1)} %copy-done.1), custom_call_target="tpu_custom_call" | custom-call | tf_op jit(solution)/shard_map/correlate/pallas_call | solution.py:345
Async XLA Ops:
  0.0 16.7 %copy-start.7 = (s32[3]{0:T(128)S(1)}, s32[3]{0:T(128)}, u32[]{:S(2)}) copy-start(s32[3]{0:T(128)} %start_ref.1) | copy-start | bytes 40
  0.0 1.2 %copy-start = (bf16[128,4096]{1,0:T(8,128)(2,1)S(1)}, bf16[128,4096]{1,0:T(8,128)(2,1)}, u32[]{:S(2)}) copy-start(bf16[128,4096]{1,0:T(8,128)(2,1)} %param.8) | copy-start | bytes 3145732
  1.2 0.9 %copy-start.4 = (bf16[512,256]{1,0:T(8,128)(2,1)S(1)}, bf16[512,256]{1,0:T(8,128)(2,1)}, u32[]{:S(2)}) copy-start(bf16[512,256]{1,0:T(8,128)(2,1)} %constant.49.table_hbm) | copy-start | bytes 786436
  2.2 14.5 %copy-start.2 = (bf16[512,768]{1,0:T(8,128)(2,1)S(1)}, bf16[512,768]{1,0:T(8,128)(2,1)}, u32[]{:S(2)}) copy-start(bf16[512,768]{1,0:T(8,128)(2,1)} %constant.50.inner_ref) | copy-start | bytes 2359300
  2.2 14.5 %copy-start.5 = (f32[33,1,768]{2,1,0:T(1,128)S(1)}, f32[33,1,768]{2,1,0:T(1,128)}, u32[]{:S(2)}) copy-start(f32[33,1,768]{2,1,0:T(1,128)} %constant.46.clone.phase_ref) | copy-start | bytes 304132
  2.2 22.1 %copy-start.3 = (bf16[384,384]{1,0:T(8,128)(2,1)S(1)}, bf16[384,384]{1,0:T(8,128)(2,1)}, u32[]{:S(2)}) copy-start(bf16[384,384]{1,0:T(8,128)(2,1)} %constant.51.band_ref) | copy-start | bytes 884740
  3.5 34.1 %copy-start.1 = (bf16[768,512]{1,0:T(8,128)(2,1)S(1)}, bf16[768,512]{1,0:T(8,128)(2,1)}, u32[]{:S(2)}) copy-start(bf16[768,512]{1,0:T(8,128)(2,1)} %constant.52.refs_4_) | copy-start | bytes 2359300
  3.5 34.1 %copy-start.6 = (s32[256]{0:T(256)S(1)}, s32[256]{0:T(256)}, u32[]{:S(2)}) copy-start(s32[256]{0:T(256)} %param.10) | copy-start | bytes 3076
  3.5 13.2 %all-to-all-start = ((bf16[8,16,1152]{2,1,0:T(8,128)(2,1)}), bf16[8,16,1152]{2,1,0:T(8,128)(2,1)S(1)}, u32[]{:S(2)}, u32[]{:S(2)}) async-start(bf16[8,16,1152]{2,1,0:T(8,128)(2,1)} %decimate.1), calls=%async_computation | async-start | bytes 589824 | tf_op jit(solution)/shard_map/all_to_all | solution.py:373
  18.2 6.1 %collective-permute-start = (bf16[48,768]{1,0:T(8,128)(2,1)S(1)}, bf16[48,768]{1,0:T(8,128)(2,1)S(1)}, u32[]{:S(2)}, u32[]{:S(2)}) collective-permute-start(bf16[48,768]{1,0:T(8,128)(2,1)S(1)} %get-tuple-element.8), channel_id=1, source_target_pairs={{0,16},{2,18},{4,20},{6,22},{8,24},{10,26},{12,28},{14,30},{16,0},... | collective-permute-start | bytes 221192 | tf_op jit(solution)/shard_map/ppermute | solution.py:376
  35.6 2.0 %collective-permute-start.1 = (bf16[8,48,768]{2,1,0:T(8,128)(2,1)S(1)}, bf16[8,48,768]{2,1,0:T(8,128)(2,1)S(1)}, u32[]{:S(2)}, u32[]{:S(2)}) collective-permute-start(bf16[8,48,768]{2,1,0:T(8,128)(2,1)S(1)} %all_to_all.10.refs_2_), channel_id=1, source_target_pairs={{1,0},{0,1},{3,2},{2,3},{5,4},{4,5},{7,6},{6,7},{9,8},{8,9},{11,10... | collective-permute-start | bytes 1769480 | tf_op jit(solution)/shard_map/ppermute | solution.py:381

commit v4 on v3

--- a/solution.py
+++ b/solution.py
@@ -81,22 +81,14 @@
     return jnp.dot(left, right, preferred_element_type=jnp.float32)
 
 
-def decimate_kernel(strain_hbm, table_hbm, out_ref, strain, table, arrived):
-    halves, rows, length = strain.shape
+def decimate_kernel(strain_ref, table_ref, out_ref):
+    halves, rows, length = strain_ref.shape
     group = out_ref.shape[1] // halves
     tiles = length // BLOCK
     many = halves * rows
-    reads = [
-        pltpu.make_async_copy(table_hbm, table, arrived.at[0]),
-        pltpu.make_async_copy(strain_hbm, strain, arrived.at[1]),
-    ]
-    for read in reads:
-        read.start()
-    for read in reads:
-        read.wait()
-    x = strain[...].reshape(many, length)
+    x = strain_ref[...].reshape(many, length)
     stacked = [x[:, tile * BLOCK : (tile + 1) * BLOCK] for tile in range(tiles)]
-    sums = dot(jnp.concatenate(stacked, axis=0), table[...])
+    sums = dot(jnp.concatenate(stacked, axis=0), table_ref[...])
     for tile in range(tiles + 1):
         if tile == tiles:
             values = sums[:many, LANES:]
@@ -117,17 +109,16 @@
     rows, length = strain.shape
     half_rows = rows // HALVES
     width = length // DEC + LANES
+    steps = 2
     return pl.pallas_call(
         decimate_kernel,
         out_shape=jax.ShapeDtypeStruct((peers, HALVES * group, width), jnp.bfloat16),
-        in_specs=[pl.BlockSpec(memory_space=pl.ANY)] * 2,
-        out_specs=VMEM,
-        scratch_shapes=[
-            pltpu.VMEM((HALVES, half_rows, length), jnp.bfloat16),
-            pltpu.VMEM((BLOCK, 2 * LANES), jnp.bfloat16),
-            pltpu.SemaphoreType.DMA((2,)),
+        grid=(steps,),
+        in_specs=[
+            pl.BlockSpec((HALVES, half_rows // steps, length), lambda i: (0, i, 0)),
+            pl.BlockSpec((BLOCK, 2 * LANES), lambda i: (0, 0)),
         ],
-        compiler_params=pltpu.CompilerParams(vmem_limit_bytes=16 * 1024 * 1024),
+        out_specs=pl.BlockSpec((peers // steps, HALVES * group, width), lambda i: (i, 0, 0)),
         name="decimate",
     )(strain.reshape(HALVES, half_rows, length), filter_table())
 
@@ -137,46 +128,75 @@
     span = width - LANES
     blocks = peers * span // BLOCK
     base = place_ref[0] * (peers * span)
-    first = place_ref[0] * blocks
-    starts = [start_ref[number] for number in range(NSEG)]
-    lane = lax.broadcasted_iota(jnp.int32, (rows, LANES), 1)
-
-    def windows(values, at):
-        pos = lane + at
-        return [
-            jnp.where((pos >= start) & (pos < start + SEG), values, 0.0).astype(jnp.bfloat16)
-            for start in starts
-        ]
+    first = place_ref[0] * blocks + 1
+    starts = [start_ref[number] - base for number in range(NSEG)]
 
     for peer in range(peers):
         for tile in range(span // LANES):
-            values = recv_ref[peer, :, tile * LANES : (tile + 1) * LANES].astype(jnp.float32)
+            values = recv_ref[peer, :, tile * LANES : (tile + 1) * LANES]
             if tile == span // LANES - 1 and peer + 1 < peers:
-                values = values + recv_ref[peer + 1, :, span:].astype(jnp.float32)
-            at = peer * span + tile * LANES
-            block, inside = divmod(at, BLOCK)
-            for number, part in enumerate(windows(values, base + at)):
-                row = (block * NSEG + number) * rows
-                lhs[row : row + rows, inside : inside + LANES] = part
-    for number, part in enumerate(windows(recv_ref[0, :, span:].astype(jnp.float32), base - LANES)):
-        edge[number * rows : (number + 1) * rows, :] = part
-    many = NSEG * rows
+                carried = recv_ref[peer + 1, :, span:].astype(jnp.float32)
+                values = (values.astype(jnp.float32) + carried).astype(jnp.bfloat16)
+            block, inside = divmod(peer * span + tile * LANES, BLOCK)
+            lhs[block * rows : (block + 1) * rows, inside : inside + LANES] = values
+
+    cuts = []
+    lane = lax.broadcasted_iota(jnp.int32, (rows, BLOCK), 1)
+    for number, start in enumerate(starts):
+        offset = jnp.bitwise_and(start, BLOCK - 1)
+        for side, limit in enumerate((start, start + SEG)):
+            block = lax.shift_right_arithmetic(limit, jnp.int32(BLOCK.bit_length() - 1))
+            held = jnp.clip(block, 0, blocks - 1)
+            cut = (block == held) & (offset != 0)
+            kept = jnp.where(side == 0, lane >= offset, lane < offset)
+            values = lhs[pl.ds(pl.multiple_of(held * rows, rows), rows), :].astype(jnp.float32)
+            values = jnp.where(kept & cut, values, 0.0).astype(jnp.bfloat16)
+            row = (blocks + len(cuts)) * rows
+            lhs[row : row + rows, :] = values
+            cuts.append((number, held))
+    before = lax.broadcasted_iota(jnp.int32, (rows, LANES), 1) - LANES
+    carried = recv_ref[0, :, span:].astype(jnp.float32)
+    for number, start in enumerate(starts):
+        kept = (before >= start) & (before < start + SEG)
+        values = jnp.where(kept, carried, 0.0).astype(jnp.bfloat16)
+        edge[number * rows : (number + 1) * rows, :] = values
+
+    whole = [
+        [
+            ((start <= block * BLOCK) & ((block + 1) * BLOCK <= start + SEG)).astype(jnp.float32)
+            for block in range(blocks)
+        ]
+        for start in starts
+    ]
     for chunk in range(CHUNKS):
         re_at, im_at = places(chunk)
+
+        def turned(part, block):
+            cos, sin = phase_ref[first + block, :, re_at], phase_ref[first + block, :, im_at]
+            part_re, part_im = part[:, :LANES], part[:, LANES:]
+            return part_re * cos + part_im * sin, part_im * cos - part_re * sin
+
         table = inner_ref[:, re_at.start : im_at.stop]
         body = dot(lhs[...], table)
-        parts = [dot(edge[...], table[BLOCK - LANES :])]
-        parts += [body[block * many : (block + 1) * many] for block in range(blocks)]
-        total_re = total_im = 0.0
-        for number, part in enumerate(parts):
-            cos, sin = phase_ref[first + number, :, re_at], phase_ref[first + number, :, im_at]
-            part_re, part_im = part[:, :LANES], part[:, LANES:]
-            total_re = total_re + (part_re * cos + part_im * sin)
-            total_im = total_im + (part_im * cos - part_re * sin)
-        own_ref[:, re_at] = total_re
-        own_ref[:, im_at] = total_im
-        send_ref[:, re_at] = total_re.astype(jnp.bfloat16)
-        send_ref[:, im_at] = total_im.astype(jnp.bfloat16)
+        tail = dot(edge[...], table[BLOCK - LANES :])
+        totals = [turned(tail[number * rows : (number + 1) * rows], -1) for number in range(NSEG)]
+        for block in range(blocks):
+            part_re, part_im = turned(body[block * rows : (block + 1) * rows], block)
+            for number in range(NSEG):
+                factor = whole[number][block]
+                total_re, total_im = totals[number]
+                totals[number] = total_re + factor * part_re, total_im + factor * part_im
+        for index, (number, block) in enumerate(cuts):
+            at = (blocks + index) * rows
+            part_re, part_im = turned(body[at : at + rows], block)
+            total_re, total_im = totals[number]
+            totals[number] = total_re + part_re, total_im + part_im
+        for number, (total_re, total_im) in enumerate(totals):
+            at = slice(number * rows, (number + 1) * rows)
+            own_ref[at, re_at] = total_re
+            own_ref[at, im_at] = total_im
+            send_ref[at, re_at] = total_re.astype(jnp.bfloat16)
+            send_ref[at, im_at] = total_im.astype(jnp.bfloat16)
 
 
 def partial_spectrum(place, seg_start, recv):
@@ -192,7 +212,7 @@
         in_specs=[SMEM, SMEM, VMEM, VMEM, VMEM],
         out_specs=[VMEM, VMEM],
         scratch_shapes=[
-            pltpu.VMEM((blocks * many, BLOCK), jnp.bfloat16),
+            pltpu.VMEM(((blocks + 2 * NSEG) * rows, BLOCK), jnp.bfloat16),
             pltpu.VMEM((many, LANES), jnp.bfloat16),
         ],
         compiler_params=pltpu.CompilerParams(vmem_limit_bytes=32 * 1024 * 1024),

time: 42.5 us -> 41.3 us (0.972)
  local copies, waits for them, and re-layouts: 2.22 us -> 0.02 us
  Pallas kernels: 7.57 us -> 8.56 us
    unnamed x16 -> x12, local copies, waits for them, and re-layouts: 2.22 us -> 0.02 us
    pallas_call x1, Pallas kernels: 1.26 us -> 2.49 us  [decimate(): pl.pallas_call(decimate_kernel, out_shape=jax.ShapeDtypeStruct((peers, HA...]
where the time goes in v4:
time: 41.3 us; the launch traced here: 41 us
  waiting for transfers between devices  12.3 us (30%)
  blocking collectives  11 us (27%)
  starting transfers between devices  8.99 us (22%)
  Pallas kernels  8.56 us (21%)
    all_to_all x1, blocking collectives, on_device(): lax.all_to_all(white, 'chan', 0, 0, tiled=True, axis_index_groups=cubes)  11 us
    all_to_all x1, waiting for transfers between devices, on_device(): lax.all_to_all(sent, 'chan', 0, 0, tiled=True, axis_index_groups=cubes)  6.84 us
    all_to_all x1, starting transfers between devices, on_device(): lax.all_to_all(sent, 'chan', 0, 0, tiled=True, axis_index_groups=cubes)  6.34 us
    pallas_call x1, Pallas kernels, correlate(): pl.pallas_call(kernel, out_shape=jax.ShapeDtypeStruct((many * receivers,...  4.65 us
    ppermute x1, waiting for transfers between devices, on_device(): white = whiten(own, lax.ppermute(send, 'chan', across), peers)  3.46 us
    ppermute x1, starting transfers between devices, on_device(): white = whiten(own, lax.ppermute(send, 'chan', across), peers)  2.64 us
    pallas_call x1, Pallas kernels, decimate(): pl.pallas_call(decimate_kernel, out_shape=jax.ShapeDtypeStruct((peers, HA...  2.49 us
    ppermute x1, waiting for transfers between devices, on_device(): spectra.append(lax.ppermute(held, 'src', pairs))  2 us
  transfers between devices with their start and end apart: 3, of which 3 were waited for; matrix products, arithmetic and copies ran while one was open for 0% of the time, Pallas kernels for 0%

profile of v4, /device:TPU:0, one launch (start us, length us, event | category | flops | bytes accessed | tf_op | source)
XLA Modules:
  0.0 41.0 jit_solution(17588731893786614482)
XLA Ops:
  0.0 0.0 copy-start.1
  0.0 0.0 copy-start.3
  0.0 0.0 copy-start.2
  0.0 0.0 copy-start.5
  0.0 2.5 %decimate.1 = bf16[8,16,1152]{2,1,0:T(8,128)(2,1)} custom-call(bf16[2,64,4096]{2,1,0:T(8,128)(2,1)} %bitcast.7, bf16[512,256]{1,0:T(8,128)(2,1)} %constant.49.table_ref), custom_call_target="tpu_custom_call" | custom-call | tf_op jit(solution)/shard_map/decimate/pallas_call | solution.py:113
  2.5 0.0 copy-start
  2.5 0.0 copy-start.4
  2.5 6.3 %all-to-all-start = ((bf16[8,16,1152]{2,1,0:T(8,128)(2,1)}), bf16[8,16,1152]{2,1,0:T(8,128)(2,1)S(1)}, u32[]{:S(2)}, u32[]{:S(2)}) async-start(bf16[8,16,1152]{2,1,0:T(8,128)(2,1)} %decimate.1), calls=%async_computation | async-start | bytes 589824 | tf_op jit(solution)/shard_map/all_to_all | solution.py:393
  8.8 0.1 pad_add_fusion.place_ref.refs_0_
  8.9 6.8 %all-to-all-done.recv_ref = bf16[8,16,1152]{2,1,0:T(8,128)(2,1)S(1)} async-done(((bf16[8,16,1152]{2,1,0:T(8,128)(2,1)}), bf16[8,16,1152]{2,1,0:T(8,128)(2,1)S(1)}, u32[]{:S(2)}, u32[]{:S(2)}) %all-to-all-start) | async-done | bytes 294944 | tf_op jit(solution)/shard_map/all_to_all | solution.py:393
  15.8 0.0 copy-done.1
  15.8 0.0 copy-done.3
  15.8 0.0 copy-done.5
  15.8 1.2 %spectrum.1 = (f32[48,768]{1,0:T(8,128)S(1)}, bf16[48,768]{1,0:T(8,128)(2,1)S(1)}) custom-call(s32[3]{0:T(128)S(1)} %pad_add_fusion.place_ref.refs_0_, s32[3]{0:T(128)S(1)} %copy-done.5, bf16[8,16,1152]{2,1,0:T(8,128)(2,1)S(1)} %all-to-all-done.recv_ref, bf16[512,768]{1,0:T(8,128)(2,1)S(1)} %copy-done.1, f32[33,1,768]{2,1,0:T(1,128)S(1)} %copy-done.3), custom_call_target="tpu_custom_call" | custom-call | tf_op jit(solution)/shard_map/spectrum/pallas_call | solution.py:206
  16.9 2.6 %collective-permute-start = (bf16[48,768]{1,0:T(8,128)(2,1)S(1)}, bf16[48,768]{1,0:T(8,128)(2,1)S(1)}, u32[]{:S(2)}, u32[]{:S(2)}) collective-permute-start(bf16[48,768]{1,0:T(8,128)(2,1)S(1)} %get-tuple-element.8), channel_id=1, source_target_pairs={{0,16},{2,18},{4,20},{6,22},{8,24},{10,26},{12,28},{14,30},{16,0},... | collective-permute-start | bytes 221192 | tf_op jit(solution)/shard_map/ppermute | solution.py:396
  19.6 3.5 %collective-permute-done.other_ref = bf16[48,768]{1,0:T(8,128)(2,1)S(1)} collective-permute-done((bf16[48,768]{1,0:T(8,128)(2,1)S(1)}, bf16[48,768]{1,0:T(8,128)(2,1)S(1)}, u32[]{:S(2)}, u32[]{:S(2)}) %collective-permute-start) | collective-permute-done | bytes 73760 | tf_op jit(solution)/shard_map/ppermute | solution.py:396
  23.0 0.0 copy-done.2
  23.0 0.3 whiten.1
  23.3 11.0 %all_to_all.10.refs_2_ = bf16[8,48,768]{2,1,0:T(8,128)(2,1)S(1)} all-to-all(bf16[8,48,768]{2,1,0:T(8,128)(2,1)S(1)} %whiten.1), channel_id=1, replica_groups={{0,2,4,6,8,10,12,14},{16,18,20,22,24,26,28,30},{1,3,5,7,9,11,13,15},{17..., dimensions={0} | all-to-all | bytes 1179648 | tf_op jit(solution)/shard_map/all_to_all | solution.py:397
  34.3 0.0 collective-permute-start.1
  34.3 2.0 %collective-permute-done.1.refs_3_ = bf16[8,48,768]{2,1,0:T(8,128)(2,1)S(1)} collective-permute-done((bf16[8,48,768]{2,1,0:T(8,128)(2,1)S(1)}, bf16[8,48,768]{2,1,0:T(8,128)(2,1)S(1)}, u32[]{:S(2)}, u32[]{:S(2)}) %collective-permute-start.1) | collective-permute-done | bytes 589856 | tf_op jit(solution)/shard_map/ppermute | solution.py:401
  36.3 0.0 copy-done
  36.4 0.0 copy-done.4
  36.4 4.7 %correlate.1 = bf16[2048,512]{1,0:T(8,128)(2,1)} custom-call(s32[3]{0:T(128)S(1)} %pad_add_fusion.place_ref.refs_0_, s32[2,128]{1,0:T(2,128)S(1)} %bitcast.6, bf16[8,48,768]{2,1,0:T(8,128)(2,1)S(1)} %all_to_all.10.refs_2_, bf16[8,48,768]{2,1,0:T(8,128)(2,1)S(1)} %collective-permute-done.1.refs_3_, bf16[768,512]{1,0:T(8,128)(2,1)S(1)} %copy-done), custom_call_target="tpu_custom_call" | custom-call | tf_op jit(solution)/shard_map/correlate/pallas_call | solution.py:365
Async XLA Ops:
  0.0 15.8 %copy-start.1 = (bf16[512,768]{1,0:T(8,128)(2,1)S(1)}, bf16[512,768]{1,0:T(8,128)(2,1)}, u32[]{:S(2)}) copy-start(bf16[512,768]{1,0:T(8,128)(2,1)} %constant.50.inner_ref) | copy-start | bytes 2359300
  0.0 15.8 %copy-start.3 = (f32[33,1,768]{2,1,0:T(1,128)S(1)}, f32[33,1,768]{2,1,0:T(1,128)}, u32[]{:S(2)}) copy-start(f32[33,1,768]{2,1,0:T(1,128)} %constant.46.clone.phase_ref) | copy-start | bytes 304132
  0.0 23.0 %copy-start.2 = (bf16[384,384]{1,0:T(8,128)(2,1)S(1)}, bf16[384,384]{1,0:T(8,128)(2,1)}, u32[]{:S(2)}) copy-start(bf16[384,384]{1,0:T(8,128)(2,1)} %constant.51.band_ref) | copy-start | bytes 884740
  0.0 15.8 %copy-start.5 = (s32[3]{0:T(128)S(1)}, s32[3]{0:T(128)}, u32[]{:S(2)}) copy-start(s32[3]{0:T(128)} %start_ref.1) | copy-start | bytes 40
  2.5 33.9 %copy-start = (bf16[768,512]{1,0:T(8,128)(2,1)S(1)}, bf16[768,512]{1,0:T(8,128)(2,1)}, u32[]{:S(2)}) copy-start(bf16[768,512]{1,0:T(8,128)(2,1)} %constant.52.refs_4_) | copy-start | bytes 2359300
  2.5 33.9 %copy-start.4 = (s32[256]{0:T(256)S(1)}, s32[256]{0:T(256)}, u32[]{:S(2)}) copy-start(s32[256]{0:T(256)} %param.10) | copy-start | bytes 3076
  2.5 13.3 %all-to-all-start = ((bf16[8,16,1152]{2,1,0:T(8,128)(2,1)}), bf16[8,16,1152]{2,1,0:T(8,128)(2,1)S(1)}, u32[]{:S(2)}, u32[]{:S(2)}) async-start(bf16[8,16,1152]{2,1,0:T(8,128)(2,1)} %decimate.1), calls=%async_computation | async-start | bytes 589824 | tf_op jit(solution)/shard_map/all_to_all | solution.py:393
  16.9 6.1 %collective-permute-start = (bf16[48,768]{1,0:T(8,128)(2,1)S(1)}, bf16[48,768]{1,0:T(8,128)(2,1)S(1)}, u32[]{:S(2)}, u32[]{:S(2)}) collective-permute-start(bf16[48,768]{1,0:T(8,128)(2,1)S(1)} %get-tuple-element.8), channel_id=1, source_target_pairs={{0,16},{2,18},{4,20},{6,22},{8,24},{10,26},{12,28},{14,30},{16,0},... | collective-permute-start | bytes 221192 | tf_op jit(solution)/shard_map/ppermute | solution.py:396
  34.3 2.0 %collective-permute-start.1 = (bf16[8,48,768]{2,1,0:T(8,128)(2,1)S(1)}, bf16[8,48,768]{2,1,0:T(8,128)(2,1)S(1)}, u32[]{:S(2)}, u32[]{:S(2)}) collective-permute-start(bf16[8,48,768]{2,1,0:T(8,128)(2,1)S(1)} %all_to_all.10.refs_2_), channel_id=1, source_target_pairs={{1,0},{0,1},{3,2},{2,3},{5,4},{4,5},{7,6},{6,7},{9,8},{8,9},{11,10... | collective-permute-start | bytes 1769480 | tf_op jit(solution)/shard_map/ppermute | solution.py:401

commit v5 on v4

--- a/solution.py
+++ b/solution.py
@@ -81,14 +81,19 @@
     return jnp.dot(left, right, preferred_element_type=jnp.float32)
 
 
-def decimate_kernel(strain_ref, table_ref, out_ref):
-    halves, rows, length = strain_ref.shape
+def decimate_kernel(strain_hbm, table_hbm, out_ref, strain, table, arrived):
+    tiles, halves, rows, _ = strain.shape
     group = out_ref.shape[1] // halves
-    tiles = length // BLOCK
     many = halves * rows
-    x = strain_ref[...].reshape(many, length)
-    stacked = [x[:, tile * BLOCK : (tile + 1) * BLOCK] for tile in range(tiles)]
-    sums = dot(jnp.concatenate(stacked, axis=0), table_ref[...])
+    reads = [pltpu.make_async_copy(table_hbm, table, arrived.at[tiles])]
+    for tile in range(tiles):
+        piece = strain_hbm.at[:, :, tile * BLOCK : (tile + 1) * BLOCK]
+        reads.append(pltpu.make_async_copy(piece, strain.at[tile], arrived.at[tile]))
+    for read in reads:
+        read.start()
+    for read in reads:
+        read.wait()
+    sums = dot(strain[...].reshape(tiles * many, BLOCK), table[...])
     for tile in range(tiles + 1):
         if tile == tiles:
             values = sums[:many, LANES:]
@@ -109,16 +114,18 @@
     rows, length = strain.shape
     half_rows = rows // HALVES
     width = length // DEC + LANES
-    steps = 2
+    tiles = length // BLOCK
     return pl.pallas_call(
         decimate_kernel,
         out_shape=jax.ShapeDtypeStruct((peers, HALVES * group, width), jnp.bfloat16),
-        grid=(steps,),
-        in_specs=[
-            pl.BlockSpec((HALVES, half_rows // steps, length), lambda i: (0, i, 0)),
-            pl.BlockSpec((BLOCK, 2 * LANES), lambda i: (0, 0)),
+        in_specs=[pl.BlockSpec(memory_space=pltpu.HBM)] * 2,
+        out_specs=VMEM,
+        scratch_shapes=[
+            pltpu.VMEM((tiles, HALVES, half_rows, BLOCK), jnp.bfloat16),
+            pltpu.VMEM((BLOCK, 2 * LANES), jnp.bfloat16),
+            pltpu.SemaphoreType.DMA((tiles + 1,)),
         ],
-        out_specs=pl.BlockSpec((peers // steps, HALVES * group, width), lambda i: (i, 0, 0)),
+        compiler_params=pltpu.CompilerParams(vmem_limit_bytes=16 * 1024 * 1024),
         name="decimate",
     )(strain.reshape(HALVES, half_rows, length), filter_table())
 

time: 41.3 us -> 42.4 us (1.027)
  local copies, waits for them, and re-layouts: 0.02 us -> 2.22 us
  Pallas kernels: 8.56 us -> 7.41 us
    unnamed x12 -> x16, local copies, waits for them, and re-layouts: 0.02 us -> 2.22 us
    pallas_call x1, Pallas kernels: 2.49 us -> 1.41 us  [decimate(): pl.pallas_call(decimate_kernel, out_shape=jax.ShapeDtypeStruct((peers, HA...]
where the time goes in v5:
time: 42.4 us; the launch traced here: 42.1 us
  waiting for transfers between devices  12.3 us (29%)
  blocking collectives  11 us (26%)
  starting transfers between devices  8.98 us (21%)
  Pallas kernels  7.41 us (17%)
  local copies, waits for them, and re-layouts  2.22 us (5%)
    all_to_all x1, blocking collectives, on_device(): lax.all_to_all(white, 'chan', 0, 0, tiled=True, axis_index_groups=cubes)  11 us
    all_to_all x1, waiting for transfers between devices, on_device(): lax.all_to_all(sent, 'chan', 0, 0, tiled=True, axis_index_groups=cubes)  6.85 us
    all_to_all x1, starting transfers between devices, on_device(): lax.all_to_all(sent, 'chan', 0, 0, tiled=True, axis_index_groups=cubes)  6.32 us
    pallas_call x1, Pallas kernels, correlate(): pl.pallas_call(kernel, out_shape=jax.ShapeDtypeStruct((many * receivers,...  4.6 us
    ppermute x1, waiting for transfers between devices, on_device(): white = whiten(own, lax.ppermute(send, 'chan', across), peers)  3.45 us
    ppermute x1, starting transfers between devices, on_device(): white = whiten(own, lax.ppermute(send, 'chan', across), peers)  2.66 us
    unnamed x16, local copies, waits for them, and re-layouts  2.22 us
    ppermute x1, waiting for transfers between devices, on_device(): spectra.append(lax.ppermute(held, 'src', pairs))  2 us
  transfers between devices with their start and end apart: 3, of which 3 were waited for; matrix products, arithmetic and copies ran while one was open for 0% of the time, Pallas kernels for 0%

profile of v5, /device:TPU:0, one launch (start us, length us, event | category | flops | bytes accessed | tf_op | source)
XLA Modules:
  0.0 42.1 jit_solution(13574508081586883269)
XLA Ops:
  0.0 0.0 copy-start.7
  0.0 0.0 copy-start
  0.0 1.2 %copy-done = bf16[128,4096]{1,0:T(8,128)(2,1)S(1)} copy-done((bf16[128,4096]{1,0:T(8,128)(2,1)S(1)}, bf16[128,4096]{1,0:T(8,128)(2,1)}, u32[]{:S(2)}) %copy-start) | copy-done | bytes 1048600
  1.2 0.0 copy-start.4
  1.2 0.9 %copy-done.4 = bf16[512,256]{1,0:T(8,128)(2,1)S(1)} copy-done((bf16[512,256]{1,0:T(8,128)(2,1)S(1)}, bf16[512,256]{1,0:T(8,128)(2,1)}, u32[]{:S(2)}) %copy-start.4) | copy-done | bytes 262168
  2.2 0.0 copy-start.2
  2.2 0.0 copy-start.5
  2.2 0.0 copy-start.3
  2.2 1.4 %decimate.1 = bf16[8,16,1152]{2,1,0:T(8,128)(2,1)} custom-call(bf16[2,64,4096]{2,1,0:T(8,128)(2,1)S(1)} %bitcast.6, bf16[512,256]{1,0:T(8,128)(2,1)S(1)} %copy-done.4), custom_call_target="tpu_custom_call" | custom-call | tf_op jit(solution)/shard_map/decimate/pallas_call | solution.py:118
  3.6 0.0 copy-start.1
  3.6 0.0 copy-start.6
  3.6 6.3 %all-to-all-start = ((bf16[8,16,1152]{2,1,0:T(8,128)(2,1)}), bf16[8,16,1152]{2,1,0:T(8,128)(2,1)S(1)}, u32[]{:S(2)}, u32[]{:S(2)}) async-start(bf16[8,16,1152]{2,1,0:T(8,128)(2,1)} %decimate.1), calls=%async_computation | async-start | bytes 589824 | tf_op jit(solution)/shard_map/all_to_all | solution.py:400
  10.0 0.1 pad_add_fusion.place_ref.refs_0_
  10.0 6.8 %all-to-all-done.recv_ref = bf16[8,16,1152]{2,1,0:T(8,128)(2,1)S(1)} async-done(((bf16[8,16,1152]{2,1,0:T(8,128)(2,1)}), bf16[8,16,1152]{2,1,0:T(8,128)(2,1)S(1)}, u32[]{:S(2)}, u32[]{:S(2)}) %all-to-all-start) | async-done | bytes 294944 | tf_op jit(solution)/shard_map/all_to_all | solution.py:400
  16.9 0.0 copy-done.7
  16.9 0.0 copy-done.2
  16.9 0.0 copy-done.5
  16.9 1.1 %spectrum.1 = (f32[48,768]{1,0:T(8,128)S(1)}, bf16[48,768]{1,0:T(8,128)(2,1)S(1)}) custom-call(s32[3]{0:T(128)S(1)} %pad_add_fusion.place_ref.refs_0_, s32[3]{0:T(128)S(1)} %copy-done.7, bf16[8,16,1152]{2,1,0:T(8,128)(2,1)S(1)} %all-to-all-done.recv_ref, bf16[512,768]{1,0:T(8,128)(2,1)S(1)} %copy-done.2, f32[33,1,768]{2,1,0:T(1,128)S(1)} %copy-done.5), custom_call_target="tpu_custom_call" | custom-call | tf_op jit(solution)/shard_map/spectrum/pallas_call | solution.py:213
  18.0 2.7 %collective-permute-start = (bf16[48,768]{1,0:T(8,128)(2,1)S(1)}, bf16[48,768]{1,0:T(8,128)(2,1)S(1)}, u32[]{:S(2)}, u32[]{:S(2)}) collective-permute-start(bf16[48,768]{1,0:T(8,128)(2,1)S(1)} %get-tuple-element.8), channel_id=1, source_target_pairs={{0,16},{2,18},{4,20},{6,22},{8,24},{10,26},{12,28},{14,30},{16,0},... | collective-permute-start | bytes 221192 | tf_op jit(solution)/shard_map/ppermute | solution.py:403
  20.7 3.5 %collective-permute-done.other_ref = bf16[48,768]{1,0:T(8,128)(2,1)S(1)} collective-permute-done((bf16[48,768]{1,0:T(8,128)(2,1)S(1)}, bf16[48,768]{1,0:T(8,128)(2,1)S(1)}, u32[]{:S(2)}, u32[]{:S(2)}) %collective-permute-start) | collective-permute-done | bytes 73760 | tf_op jit(solution)/shard_map/ppermute | solution.py:403
  24.2 0.0 copy-done.3
  24.2 0.3 whiten.1
  24.4 11.0 %all_to_all.10.refs_2_ = bf16[8,48,768]{2,1,0:T(8,128)(2,1)S(1)} all-to-all(bf16[8,48,768]{2,1,0:T(8,128)(2,1)S(1)} %whiten.1), channel_id=1, replica_groups={{0,2,4,6,8,10,12,14},{16,18,20,22,24,26,28,30},{1,3,5,7,9,11,13,15},{17..., dimensions={0} | all-to-all | bytes 1179648 | tf_op jit(solution)/shard_map/all_to_all | solution.py:404
  35.5 0.0 collective-permute-start.1
  35.5 2.0 %collective-permute-done.1.refs_3_ = bf16[8,48,768]{2,1,0:T(8,128)(2,1)S(1)} collective-permute-done((bf16[8,48,768]{2,1,0:T(8,128)(2,1)S(1)}, bf16[8,48,768]{2,1,0:T(8,128)(2,1)S(1)}, u32[]{:S(2)}, u32[]{:S(2)}) %collective-permute-start.1) | collective-permute-done | bytes 589856 | tf_op jit(solution)/shard_map/ppermute | solution.py:408
  37.5 0.0 copy-done.1
  37.5 0.0 copy-done.6
  37.5 4.6 %correlate.1 = bf16[2048,512]{1,0:T(8,128)(2,1)} custom-call(s32[3]{0:T(128)S(1)} %pad_add_fusion.place_ref.refs_0_, s32[2,128]{1,0:T(2,128)S(1)} %bitcast.7, bf16[8,48,768]{2,1,0:T(8,128)(2,1)S(1)} %all_to_all.10.refs_2_, bf16[8,48,768]{2,1,0:T(8,128)(2,1)S(1)} %collective-permute-done.1.refs_3_, bf16[768,512]{1,0:T(8,128)(2,1)S(1)} %copy-done.1), custom_call_target="tpu_custom_call" | custom-call | tf_op jit(solution)/shard_map/correlate/pallas_call | solution.py:372
Async XLA Ops:
  0.0 16.9 %copy-start.7 = (s32[3]{0:T(128)S(1)}, s32[3]{0:T(128)}, u32[]{:S(2)}) copy-start(s32[3]{0:T(128)} %start_ref.1) | copy-start | bytes 40
  0.0 1.2 %copy-start = (bf16[128,4096]{1,0:T(8,128)(2,1)S(1)}, bf16[128,4096]{1,0:T(8,128)(2,1)}, u32[]{:S(2)}) copy-start(bf16[128,4096]{1,0:T(8,128)(2,1)} %param.8) | copy-start | bytes 3145732
  1.2 0.9 %copy-start.4 = (bf16[512,256]{1,0:T(8,128)(2,1)S(1)}, bf16[512,256]{1,0:T(8,128)(2,1)}, u32[]{:S(2)}) copy-start(bf16[512,256]{1,0:T(8,128)(2,1)} %constant.49.table_hbm) | copy-start | bytes 786436
  2.2 14.7 %copy-start.2 = (bf16[512,768]{1,0:T(8,128)(2,1)S(1)}, bf16[512,768]{1,0:T(8,128)(2,1)}, u32[]{:S(2)}) copy-start(bf16[512,768]{1,0:T(8,128)(2,1)} %constant.50.inner_ref) | copy-start | bytes 2359300
  2.2 14.7 %copy-start.5 = (f32[33,1,768]{2,1,0:T(1,128)S(1)}, f32[33,1,768]{2,1,0:T(1,128)}, u32[]{:S(2)}) copy-start(f32[33,1,768]{2,1,0:T(1,128)} %constant.46.clone.phase_ref) | copy-start | bytes 304132
  2.2 22.0 %copy-start.3 = (bf16[384,384]{1,0:T(8,128)(2,1)S(1)}, bf16[384,384]{1,0:T(8,128)(2,1)}, u32[]{:S(2)}) copy-start(bf16[384,384]{1,0:T(8,128)(2,1)} %constant.51.band_ref) | copy-start | bytes 884740
  3.6 33.8 %copy-start.1 = (bf16[768,512]{1,0:T(8,128)(2,1)S(1)}, bf16[768,512]{1,0:T(8,128)(2,1)}, u32[]{:S(2)}) copy-start(bf16[768,512]{1,0:T(8,128)(2,1)} %constant.52.refs_4_) | copy-start | bytes 2359300
  3.6 33.8 %copy-start.6 = (s32[256]{0:T(256)S(1)}, s32[256]{0:T(256)}, u32[]{:S(2)}) copy-start(s32[256]{0:T(256)} %param.10) | copy-start | bytes 3076
  3.6 13.2 %all-to-all-start = ((bf16[8,16,1152]{2,1,0:T(8,128)(2,1)}), bf16[8,16,1152]{2,1,0:T(8,128)(2,1)S(1)}, u32[]{:S(2)}, u32[]{:S(2)}) async-start(bf16[8,16,1152]{2,1,0:T(8,128)(2,1)} %decimate.1), calls=%async_computation | async-start | bytes 589824 | tf_op jit(solution)/shard_map/all_to_all | solution.py:400
  18.0 6.1 %collective-permute-start = (bf16[48,768]{1,0:T(8,128)(2,1)S(1)}, bf16[48,768]{1,0:T(8,128)(2,1)S(1)}, u32[]{:S(2)}, u32[]{:S(2)}) collective-permute-start(bf16[48,768]{1,0:T(8,128)(2,1)S(1)} %get-tuple-element.8), channel_id=1, source_target_pairs={{0,16},{2,18},{4,20},{6,22},{8,24},{10,26},{12,28},{14,30},{16,0},... | collective-permute-start | bytes 221192 | tf_op jit(solution)/shard_map/ppermute | solution.py:403
  35.5 2.0 %collective-permute-start.1 = (bf16[8,48,768]{2,1,0:T(8,128)(2,1)S(1)}, bf16[8,48,768]{2,1,0:T(8,128)(2,1)S(1)}, u32[]{:S(2)}, u32[]{:S(2)}) collective-permute-start(bf16[8,48,768]{2,1,0:T(8,128)(2,1)S(1)} %all_to_all.10.refs_2_), channel_id=1, source_target_pairs={{1,0},{0,1},{3,2},{2,3},{5,4},{4,5},{7,6},{6,7},{9,8},{8,9},{11,10... | collective-permute-start | bytes 1769480 | tf_op jit(solution)/shard_map/ppermute | solution.py:408

commit v6 on v4

--- a/solution.py
+++ b/solution.py
@@ -20,6 +20,16 @@
 CHUNKS = NBIN // LANES
 VMEM = pl.BlockSpec(memory_space=pltpu.VMEM)
 SMEM = pl.BlockSpec(memory_space=pltpu.SMEM)
+
+
+def ordered(peers):
+    return [place ^ (place >> 1) for place in range(peers)]
+
+
+def position(peer):
+    peer = peer ^ (peer >> 1)
+    peer = peer ^ (peer >> 2)
+    return peer ^ (peer >> 4)
 
 
 def chunked(real, imag):
@@ -86,6 +96,7 @@
     group = out_ref.shape[1] // halves
     tiles = length // BLOCK
     many = halves * rows
+    first = pl.program_id(0) * (rows // group)
     x = strain_ref[...].reshape(many, length)
     stacked = [x[:, tile * BLOCK : (tile + 1) * BLOCK] for tile in range(tiles)]
     sums = dot(jnp.concatenate(stacked, axis=0), table_ref[...])
@@ -102,7 +113,7 @@
                 for half in range(halves)
             ]
             part = jnp.concatenate(part, axis=0).astype(jnp.bfloat16)
-            out_ref[peer, :, tile * LANES : (tile + 1) * LANES] = part
+            out_ref[position(first + peer) - first, :, tile * LANES : (tile + 1) * LANES] = part
 
 
 def decimate(strain, peers, group):
@@ -133,9 +144,9 @@
 
     for peer in range(peers):
         for tile in range(span // LANES):
-            values = recv_ref[peer, :, tile * LANES : (tile + 1) * LANES]
+            values = recv_ref[position(peer), :, tile * LANES : (tile + 1) * LANES]
             if tile == span // LANES - 1 and peer + 1 < peers:
-                carried = recv_ref[peer + 1, :, span:].astype(jnp.float32)
+                carried = recv_ref[position(peer + 1), :, span:].astype(jnp.float32)
                 values = (values.astype(jnp.float32) + carried).astype(jnp.bfloat16)
             block, inside = divmod(peer * span + tile * LANES, BLOCK)
             lhs[block * rows : (block + 1) * rows, inside : inside + LANES] = values
@@ -267,11 +278,11 @@
         owner = lax.rem(mine + step, groups)
         local = wanted - owner * channels
         in_half = jnp.bitwise_and(local, channels // HALVES - 1)
-        row = (in_half // group) * rows + (local // (channels // HALVES)) * group + in_half % group
+        row = position(in_half // group) * rows + (local // (channels // HALVES)) * group + in_half % group
         row = jnp.where((local >= 0) & (local < channels), row, -1)
         picks.append((spot == row).astype(jnp.float32))
         for number in range(NSEG):
-            here = spectrum[peer, number * rows : (number + 1) * rows, :].astype(jnp.float32)
+            here = spectrum[position(peer), number * rows : (number + 1) * rows, :].astype(jnp.float32)
             here = jnp.where(half == 0, here[:group], here[group:]) * (1.0 / NSEG)
             receiver[number, owner] = here
     pick = jnp.concatenate(picks, axis=0).T.astype(jnp.bfloat16)
@@ -387,7 +398,7 @@
     per_device = strain.shape[0] // chan_count
     index = lax.axis_index("chan")
     place = jnp.stack([index // peers, index % peers, lax.axis_index("src")]).astype(jnp.int32)
-    cubes = [[half * peers + peer for peer in range(peers)] for half in range(HALVES)]
+    cubes = [[half * peers + peer for peer in ordered(peers)] for half in range(HALVES)]
 
     sent = decimate(strain, peers, per_device)
     samples = lax.all_to_all(sent, "chan", 0, 0, tiled=True, axis_index_groups=cubes)

time: 41.3 us -> 40.8 us (0.988)
  waiting for transfers between devices: 12.3 us -> 11.1 us
  blocking collectives: 11 us -> 11.7 us
    ppermute x1, waiting for transfers between devices: 3.46 us -> 2.67 us  [on_device(): white = whiten(own, lax.ppermute(send, 'chan', across), peers)]
    all_to_all x1, blocking collectives: 11 us -> 11.7 us  [on_device(): lax.all_to_all(white, 'chan', 0, 0, tiled=True, axis_index_groups=cubes)]
where the time goes in v6:
time: 40.8 us; the launch traced here: 40.5 us
  blocking collectives  11.7 us (29%)
  waiting for transfers between devices  11.1 us (27%)
  starting transfers between devices  8.98 us (22%)
  Pallas kernels  8.59 us (21%)
    all_to_all x1, blocking collectives, on_device(): lax.all_to_all(white, 'chan', 0, 0, tiled=True, axis_index_groups=cubes)  11.7 us
    all_to_all x1, waiting for transfers between devices, on_device(): lax.all_to_all(sent, 'chan', 0, 0, tiled=True, axis_index_groups=cubes)  6.45 us
    all_to_all x1, starting transfers between devices, on_device(): lax.all_to_all(sent, 'chan', 0, 0, tiled=True, axis_index_groups=cubes)  6.33 us
    pallas_call x1, Pallas kernels, correlate(): pl.pallas_call(kernel, out_shape=jax.ShapeDtypeStruct((many * receivers,...  4.66 us
    ppermute x1, waiting for transfers between devices, on_device(): white = whiten(own, lax.ppermute(send, 'chan', across), peers)  2.67 us
    ppermute x1, starting transfers between devices, on_device(): white = whiten(own, lax.ppermute(send, 'chan', across), peers)  2.65 us
    pallas_call x1, Pallas kernels, decimate(): pl.pallas_call(decimate_kernel, out_shape=jax.ShapeDtypeStruct((peers, HA...  2.5 us
    ppermute x1, waiting for transfers between devices, on_device(): spectra.append(lax.ppermute(held, 'src', pairs))  2 us
  transfers between devices with their start and end apart: 3, of which 3 were waited for; matrix products, arithmetic and copies ran while one was open for 0% of the time, Pallas kernels for 0%

profile of v6, /device:TPU:0, one launch (start us, length us, event | category | flops | bytes accessed | tf_op | source)
XLA Modules:
  0.0 40.5 jit_solution(4521562713384074834)
XLA Ops:
  0.0 0.0 copy-start.1
  0.0 0.0 copy-start.3
  0.0 0.0 copy-start.2
  0.0 0.0 copy-start.5
  0.0 2.5 %decimate.1 = bf16[8,16,1152]{2,1,0:T(8,128)(2,1)} custom-call(bf16[2,64,4096]{2,1,0:T(8,128)(2,1)} %bitcast.7, bf16[512,256]{1,0:T(8,128)(2,1)} %constant.49.table_ref), custom_call_target="tpu_custom_call" | custom-call | tf_op jit(solution)/shard_map/decimate/pallas_call | solution.py:124
  2.5 0.0 copy-start
  2.5 0.0 copy-start.4
  2.5 6.3 %all-to-all-start = ((bf16[8,16,1152]{2,1,0:T(8,128)(2,1)}), bf16[8,16,1152]{2,1,0:T(8,128)(2,1)S(1)}, u32[]{:S(2)}, u32[]{:S(2)}) async-start(bf16[8,16,1152]{2,1,0:T(8,128)(2,1)} %decimate.1), calls=%async_computation | async-start | bytes 589824 | tf_op jit(solution)/shard_map/all_to_all | solution.py:404
  8.8 0.1 pad_add_fusion.place_ref.refs_0_
  8.9 6.4 %all-to-all-done.recv_ref = bf16[8,16,1152]{2,1,0:T(8,128)(2,1)S(1)} async-done(((bf16[8,16,1152]{2,1,0:T(8,128)(2,1)}), bf16[8,16,1152]{2,1,0:T(8,128)(2,1)S(1)}, u32[]{:S(2)}, u32[]{:S(2)}) %all-to-all-start) | async-done | bytes 294944 | tf_op jit(solution)/shard_map/all_to_all | solution.py:404
  15.4 0.0 copy-done.1
  15.4 0.0 copy-done.3
  15.4 0.0 copy-done.5
  15.4 1.2 %spectrum.1 = (f32[48,768]{1,0:T(8,128)S(1)}, bf16[48,768]{1,0:T(8,128)(2,1)S(1)}) custom-call(s32[3]{0:T(128)S(1)} %pad_add_fusion.place_ref.refs_0_, s32[3]{0:T(128)S(1)} %copy-done.5, bf16[8,16,1152]{2,1,0:T(8,128)(2,1)S(1)} %all-to-all-done.recv_ref, bf16[512,768]{1,0:T(8,128)(2,1)S(1)} %copy-done.1, f32[33,1,768]{2,1,0:T(1,128)S(1)} %copy-done.3), custom_call_target="tpu_custom_call" | custom-call | tf_op jit(solution)/shard_map/spectrum/pallas_call | solution.py:217
  16.5 2.7 %collective-permute-start = (bf16[48,768]{1,0:T(8,128)(2,1)S(1)}, bf16[48,768]{1,0:T(8,128)(2,1)S(1)}, u32[]{:S(2)}, u32[]{:S(2)}) collective-permute-start(bf16[48,768]{1,0:T(8,128)(2,1)S(1)} %get-tuple-element.8), channel_id=1, source_target_pairs={{0,16},{2,18},{4,20},{6,22},{8,24},{10,26},{12,28},{14,30},{16,0},... | collective-permute-start | bytes 221192 | tf_op jit(solution)/shard_map/ppermute | solution.py:407
  19.2 2.7 %collective-permute-done.other_ref = bf16[48,768]{1,0:T(8,128)(2,1)S(1)} collective-permute-done((bf16[48,768]{1,0:T(8,128)(2,1)S(1)}, bf16[48,768]{1,0:T(8,128)(2,1)S(1)}, u32[]{:S(2)}, u32[]{:S(2)}) %collective-permute-start) | collective-permute-done | bytes 73760 | tf_op jit(solution)/shard_map/ppermute | solution.py:407
  21.9 0.0 copy-done.2
  21.9 0.3 whiten.1
  22.1 11.7 %all_to_all.10.refs_2_ = bf16[8,48,768]{2,1,0:T(8,128)(2,1)S(1)} all-to-all(bf16[8,48,768]{2,1,0:T(8,128)(2,1)S(1)} %whiten.1), channel_id=1, replica_groups={{0,2,6,4,12,14,10,8},{16,18,22,20,28,30,26,24},{1,3,7,5,13,15,11,9},{17..., dimensions={0} | all-to-all | bytes 1179648 | tf_op jit(solution)/shard_map/all_to_all | solution.py:408
  33.8 0.0 collective-permute-start.1
  33.8 2.0 %collective-permute-done.1.refs_3_ = bf16[8,48,768]{2,1,0:T(8,128)(2,1)S(1)} collective-permute-done((bf16[8,48,768]{2,1,0:T(8,128)(2,1)S(1)}, bf16[8,48,768]{2,1,0:T(8,128)(2,1)S(1)}, u32[]{:S(2)}, u32[]{:S(2)}) %collective-permute-start.1) | collective-permute-done | bytes 589856 | tf_op jit(solution)/shard_map/ppermute | solution.py:412
  35.8 0.0 copy-done
  35.8 0.0 copy-done.4
  35.8 4.7 %correlate.1 = bf16[2048,512]{1,0:T(8,128)(2,1)} custom-call(s32[3]{0:T(128)S(1)} %pad_add_fusion.place_ref.refs_0_, s32[2,128]{1,0:T(2,128)S(1)} %bitcast.6, bf16[8,48,768]{2,1,0:T(8,128)(2,1)S(1)} %all_to_all.10.refs_2_, bf16[8,48,768]{2,1,0:T(8,128)(2,1)S(1)} %collective-permute-done.1.refs_3_, bf16[768,512]{1,0:T(8,128)(2,1)S(1)} %copy-done), custom_call_target="tpu_custom_call" | custom-call | tf_op jit(solution)/shard_map/correlate/pallas_call | solution.py:376
Async XLA Ops:
  0.0 15.4 %copy-start.1 = (bf16[512,768]{1,0:T(8,128)(2,1)S(1)}, bf16[512,768]{1,0:T(8,128)(2,1)}, u32[]{:S(2)}) copy-start(bf16[512,768]{1,0:T(8,128)(2,1)} %constant.50.inner_ref) | copy-start | bytes 2359300
  0.0 15.4 %copy-start.3 = (f32[33,1,768]{2,1,0:T(1,128)S(1)}, f32[33,1,768]{2,1,0:T(1,128)}, u32[]{:S(2)}) copy-start(f32[33,1,768]{2,1,0:T(1,128)} %constant.46.clone.phase_ref) | copy-start | bytes 304132
  0.0 21.9 %copy-start.2 = (bf16[384,384]{1,0:T(8,128)(2,1)S(1)}, bf16[384,384]{1,0:T(8,128)(2,1)}, u32[]{:S(2)}) copy-start(bf16[384,384]{1,0:T(8,128)(2,1)} %constant.51.band_ref) | copy-start | bytes 884740
  0.0 15.4 %copy-start.5 = (s32[3]{0:T(128)S(1)}, s32[3]{0:T(128)}, u32[]{:S(2)}) copy-start(s32[3]{0:T(128)} %start_ref.1) | copy-start | bytes 40
  2.5 33.3 %copy-start = (bf16[768,512]{1,0:T(8,128)(2,1)S(1)}, bf16[768,512]{1,0:T(8,128)(2,1)}, u32[]{:S(2)}) copy-start(bf16[768,512]{1,0:T(8,128)(2,1)} %constant.52.refs_4_) | copy-start | bytes 2359300
  2.5 33.3 %copy-start.4 = (s32[256]{0:T(256)S(1)}, s32[256]{0:T(256)}, u32[]{:S(2)}) copy-start(s32[256]{0:T(256)} %param.10) | copy-start | bytes 3076
  2.5 12.9 %all-to-all-start = ((bf16[8,16,1152]{2,1,0:T(8,128)(2,1)}), bf16[8,16,1152]{2,1,0:T(8,128)(2,1)S(1)}, u32[]{:S(2)}, u32[]{:S(2)}) async-start(bf16[8,16,1152]{2,1,0:T(8,128)(2,1)} %decimate.1), calls=%async_computation | async-start | bytes 589824 | tf_op jit(solution)/shard_map/all_to_all | solution.py:404
  16.5 5.3 %collective-permute-start = (bf16[48,768]{1,0:T(8,128)(2,1)S(1)}, bf16[48,768]{1,0:T(8,128)(2,1)S(1)}, u32[]{:S(2)}, u32[]{:S(2)}) collective-permute-start(bf16[48,768]{1,0:T(8,128)(2,1)S(1)} %get-tuple-element.8), channel_id=1, source_target_pairs={{0,16},{2,18},{4,20},{6,22},{8,24},{10,26},{12,28},{14,30},{16,0},... | collective-permute-start | bytes 221192 | tf_op jit(solution)/shard_map/ppermute | solution.py:407
  33.8 2.0 %collective-permute-start.1 = (bf16[8,48,768]{2,1,0:T(8,128)(2,1)S(1)}, bf16[8,48,768]{2,1,0:T(8,128)(2,1)S(1)}, u32[]{:S(2)}, u32[]{:S(2)}) collective-permute-start(bf16[8,48,768]{2,1,0:T(8,128)(2,1)S(1)} %all_to_all.10.refs_2_), channel_id=1, source_target_pairs={{1,0},{0,1},{3,2},{2,3},{5,4},{4,5},{7,6},{6,7},{9,8},{8,9},{11,10... | collective-permute-start | bytes 1769480 | tf_op jit(solution)/shard_map/ppermute | solution.py:412

commit v7 on v6

--- a/solution.py
+++ b/solution.py
@@ -134,13 +134,13 @@
     )(strain.reshape(HALVES, half_rows, length), filter_table())
 
 
-def spectrum_kernel(place_ref, start_ref, recv_ref, inner_ref, phase_ref, own_ref, send_ref, lhs, edge):
+def spectrum_kernel(info_ref, recv_ref, inner_ref, phase_ref, own_ref, send_ref, lhs, edge):
     peers, rows, width = recv_ref.shape
     span = width - LANES
     blocks = peers * span // BLOCK
-    base = place_ref[0] * (peers * span)
-    first = place_ref[0] * blocks + 1
-    starts = [start_ref[number] - base for number in range(NSEG)]
+    base = info_ref[0] * (peers * span)
+    first = info_ref[0] * blocks + 1
+    starts = [info_ref[1 + number] - base for number in range(NSEG)]
 
     for peer in range(peers):
         for tile in range(span // LANES):
@@ -210,7 +210,7 @@
             send_ref[at, im_at] = total_im.astype(jnp.bfloat16)
 
 
-def partial_spectrum(place, seg_start, recv):
+def partial_spectrum(info, recv):
     peers, rows, width = recv.shape
     blocks = peers * (width - LANES) // BLOCK
     many = NSEG * rows
@@ -220,7 +220,7 @@
             jax.ShapeDtypeStruct((many, 2 * NBIN), jnp.float32),
             jax.ShapeDtypeStruct((many, 2 * NBIN), jnp.bfloat16),
         ],
-        in_specs=[SMEM, SMEM, VMEM, VMEM, VMEM],
+        in_specs=[SMEM, VMEM, VMEM, VMEM],
         out_specs=[VMEM, VMEM],
         scratch_shapes=[
             pltpu.VMEM(((blocks + 2 * NSEG) * rows, BLOCK), jnp.bfloat16),
@@ -228,7 +228,7 @@
         ],
         compiler_params=pltpu.CompilerParams(vmem_limit_bytes=32 * 1024 * 1024),
         name="spectrum",
-    )(place, seg_start, recv, inner_table(), phase_table(-1, HALVES * blocks + 1))
+    )(info, recv, inner_table(), phase_table(-1, HALVES * blocks + 1))
 
 
 def whiten_kernel(own_ref, other_ref, band_ref, out_ref):
@@ -260,41 +260,30 @@
     )(own, other, band_table())
 
 
-def correlate_kernel(groups, group, block, place_ref, chan_ref, *refs):
+def correlate_kernel(groups, group, block, info_ref, *refs):
     spectra = refs[:groups]
     basis_ref, out_ref, source, receiver, cross_even, cross_odd, lagged, sent = refs[groups:]
-    peers = spectra[0].shape[0]
     rows = HALVES * group
-    channels = peers * rows
+    channels = spectra[0].shape[0] * rows
     receivers = groups * group
-    many = chan_ref.shape[1]
-    blocks = many // block
-    half, peer, mine = place_ref[0], place_ref[1], place_ref[2]
-
-    wanted = chan_ref[pl.ds(mine, 1), :]
-    spot = lax.broadcasted_iota(jnp.int32, (channels, many), 0)
-    picks = []
+    blocks = sent.shape[0]
+    half, peer, mine = info_ref[0], info_ref[1], info_ref[2]
+
     for step, spectrum in enumerate(spectra):
         owner = lax.rem(mine + step, groups)
-        local = wanted - owner * channels
-        in_half = jnp.bitwise_and(local, channels // HALVES - 1)
-        row = position(in_half // group) * rows + (local // (channels // HALVES)) * group + in_half % group
-        row = jnp.where((local >= 0) & (local < channels), row, -1)
-        picks.append((spot == row).astype(jnp.float32))
         for number in range(NSEG):
             here = spectrum[position(peer), number * rows : (number + 1) * rows, :].astype(jnp.float32)
             here = jnp.where(half == 0, here[:group], here[group:]) * (1.0 / NSEG)
             receiver[number, owner] = here
-    pick = jnp.concatenate(picks, axis=0).T.astype(jnp.bfloat16)
-
-    def get(chunk):
-        columns = slice(2 * chunk * LANES, 2 * (chunk + 1) * LANES)
-        for number in range(NSEG):
-            at = slice(number * rows, (number + 1) * rows)
-            held = [part[:, at, columns].reshape(channels, 2 * LANES) for part in spectra]
-            found = dot(pick, jnp.concatenate(held, axis=0))
-            source[number, 2 * chunk] = found[:, :LANES]
-            source[number, 2 * chunk + 1] = found[:, LANES:]
+
+    def widen(chunk):
+        for step, spectrum in enumerate(spectra):
+            for number in range(NSEG):
+                for part, columns in enumerate(places(chunk)):
+                    held = spectrum[:, number * rows : (number + 1) * rows, columns]
+                    held = held.astype(jnp.float32).reshape(channels, LANES)
+                    at = slice(step * channels, (step + 1) * channels)
+                    source[number, 2 * chunk + part, at, :] = held
 
     def fill(number, cross, chunks):
         for chunk in chunks:
@@ -304,8 +293,8 @@
             recv_im = [part[:, im_at].astype(jnp.bfloat16) for part in recv]
             for k in range(block):
                 total_re = total_im = None
+                same = pl.ds(info_ref[3 + number * block + k], 8, stride=0)
                 for seg in range(NSEG):
-                    same = pl.ds(number * block + k, 8, stride=0)
                     source_re = source[seg, 2 * chunk, same, :]
                     source_im = source[seg, 2 * chunk + 1, same, :]
                     source_re = jnp.concatenate([source_re] * (receivers // 8), axis=0)
@@ -334,7 +323,7 @@
 
     everything = range(CHUNKS)
     for chunk in everything:
-        get(chunk)
+        widen(chunk)
         fill(0, cross_even, [chunk])
 
     def pair(number):
@@ -362,10 +351,11 @@
     lax.fori_loop(0, blocks, finish, 0)
 
 
-def correlate(place, src_chan, spectra, group):
+def correlate(info, spectra, group):
     groups = len(spectra)
-    many = src_chan.shape[0] // groups
+    many = info.shape[0] - 3
     receivers = groups * group
+    channels = groups * spectra[0].shape[0] * HALVES * group
     block = 256 // receivers
     rows = block * receivers
 
@@ -376,19 +366,32 @@
     return pl.pallas_call(
         kernel,
         out_shape=jax.ShapeDtypeStruct((many * receivers, NLAG), jnp.bfloat16),
-        in_specs=[SMEM] + [VMEM] * (groups + 2),
+        in_specs=[SMEM] + [VMEM] * (groups + 1),
         out_specs=pl.BlockSpec(memory_space=pl.ANY),
         scratch_shapes=[
-            pltpu.VMEM((NSEG, 2 * CHUNKS, many, LANES), jnp.float32),
+            pltpu.VMEM((NSEG, 2 * CHUNKS, channels, LANES), jnp.float32),
             pltpu.VMEM((NSEG, groups, group, 2 * NBIN), jnp.float32),
             pltpu.VMEM((rows, 2 * NBIN), jnp.bfloat16),
             pltpu.VMEM((rows, 2 * NBIN), jnp.bfloat16),
             pltpu.VMEM((many * receivers, NLAG), jnp.bfloat16),
             pltpu.SemaphoreType.DMA((many // block,)),
         ],
-        compiler_params=pltpu.CompilerParams(vmem_limit_bytes=16 * 1024 * 1024 + 2 * held),
+        compiler_params=pltpu.CompilerParams(
+            vmem_limit_bytes=min(16 * 1024 * 1024 + 3 * held, 63 * 1024 * 1024)
+        ),
         name="correlate",
-    )(place, src_chan.reshape(groups, many), *spectra, lag_table())
+    )(info, *spectra, lag_table())
+
+
+def source_rows(src_chan, group_count, local_rows, peers, per_device):
+    mine = lax.axis_index("src")
+    many = src_chan.shape[0] // group_count
+    wanted = lax.dynamic_slice_in_dim(src_chan, mine * many, many, 0)
+    step = jnp.mod(wanted // local_rows - mine, group_count)
+    local = wanted % local_rows
+    half, inside = local // (local_rows // HALVES), local % (local_rows // HALVES)
+    place = position(inside // per_device) * HALVES + half
+    return step * local_rows + place * per_device + inside % per_device
 
 
 def on_device(strain, seg_start, src_chan):
@@ -397,12 +400,14 @@
     peers = chan_count // HALVES
     per_device = strain.shape[0] // chan_count
     index = lax.axis_index("chan")
+    half = (index // peers).reshape(1).astype(jnp.int32)
     place = jnp.stack([index // peers, index % peers, lax.axis_index("src")]).astype(jnp.int32)
+    rows = source_rows(src_chan, group_count, strain.shape[0], peers, per_device)
     cubes = [[half * peers + peer for peer in ordered(peers)] for half in range(HALVES)]
 
     sent = decimate(strain, peers, per_device)
     samples = lax.all_to_all(sent, "chan", 0, 0, tiled=True, axis_index_groups=cubes)
-    own, send = partial_spectrum(place, seg_start, samples)
+    own, send = partial_spectrum(jnp.concatenate([half, seg_start]), samples)
     across = [(i, (i + peers) % chan_count) for i in range(chan_count)]
     white = whiten(own, lax.ppermute(send, "chan", across), peers)
     held = lax.all_to_all(white, "chan", 0, 0, tiled=True, axis_index_groups=cubes)
@@ -410,7 +415,7 @@
     for step in range(1, group_count):
         pairs = [((i + step) % group_count, i) for i in range(group_count)]
         spectra.append(lax.ppermute(held, "src", pairs))
-    lagged = correlate(place, src_chan, spectra, per_device)
+    lagged = correlate(jnp.concatenate([place, rows]), spectra, per_device)
     return lagged.reshape(-1, group_count, per_device, NLAG)
 
 

time: 40.8 us -> 40.7 us (level)
  transfers between devices with their start and end apart: 3 -> 3, of which waited for: 3 -> 3; matrix products, arithmetic and copies ran while one was open for 0% -> 1% of each run, Pallas kernels for 0% -> 0%
where the time goes in v7:
time: 40.7 us; the launch traced here: 40.4 us
  blocking collectives  11.7 us (29%)
  waiting for transfers between devices  10.9 us (27%)
  starting transfers between devices  8.98 us (22%)
  Pallas kernels  8.51 us (21%)
    all_to_all x1, blocking collectives, on_device(): lax.all_to_all(white, 'chan', 0, 0, tiled=True, axis_index_groups=cubes)  11.7 us
    all_to_all x1, waiting for transfers between devices, on_device(): lax.all_to_all(sent, 'chan', 0, 0, tiled=True, axis_index_groups=cubes)  6.44 us
    all_to_all x1, starting transfers between devices, on_device(): lax.all_to_all(sent, 'chan', 0, 0, tiled=True, axis_index_groups=cubes)  6.33 us
    pallas_call x1, Pallas kernels, correlate(): pl.pallas_call(kernel, out_shape=jax.ShapeDtypeStruct((many * receivers,...  4.6 us
    ppermute x1, waiting for transfers between devices, on_device(): white = whiten(own, lax.ppermute(send, 'chan', across), peers)  2.67 us
    ppermute x1, starting transfers between devices, on_device(): white = whiten(own, lax.ppermute(send, 'chan', across), peers)  2.65 us
    pallas_call x1, Pallas kernels, decimate(): pl.pallas_call(decimate_kernel, out_shape=jax.ShapeDtypeStruct((peers, HA...  2.5 us
    ppermute x1, waiting for transfers between devices, on_device(): spectra.append(lax.ppermute(held, 'src', pairs))  1.81 us
  transfers between devices with their start and end apart: 3, of which 3 were waited for; matrix products, arithmetic and copies ran while one was open for 1% of the time, Pallas kernels for 0%

profile of v7, /device:TPU:0, one launch (start us, length us, event | category | flops | bytes accessed | tf_op | source)
XLA Modules:
  0.0 40.4 jit_solution(17966225519363518546)
XLA Ops:
  0.0 0.0 copy-start.1
  0.0 0.0 copy-start.3
  0.0 0.0 copy-start.2
  0.0 0.0 copy-start.5
  0.0 2.5 %decimate.1 = bf16[8,16,1152]{2,1,0:T(8,128)(2,1)} custom-call(bf16[2,64,4096]{2,1,0:T(8,128)(2,1)} %bitcast.5, bf16[512,256]{1,0:T(8,128)(2,1)} %constant.126.table_ref), custom_call_target="tpu_custom_call" | custom-call | tf_op jit(solution)/shard_map/decimate/pallas_call | solution.py:124
  2.5 0.0 copy-start.4
  2.5 0.0 copy-start
  2.5 6.3 %all-to-all-start = ((bf16[8,16,1152]{2,1,0:T(8,128)(2,1)}), bf16[8,16,1152]{2,1,0:T(8,128)(2,1)S(1)}, u32[]{:S(2)}, u32[]{:S(2)}) async-start(bf16[8,16,1152]{2,1,0:T(8,128)(2,1)} %decimate.1), calls=%async_computation | async-start | bytes 589824 | tf_op jit(solution)/shard_map/all_to_all | solution.py:409
  8.8 0.0 copy-done.5
  8.9 0.1 pad_add_fusion.1.info_ref
  8.9 6.4 %all-to-all-done.recv_ref = bf16[8,16,1152]{2,1,0:T(8,128)(2,1)S(1)} async-done(((bf16[8,16,1152]{2,1,0:T(8,128)(2,1)}), bf16[8,16,1152]{2,1,0:T(8,128)(2,1)S(1)}, u32[]{:S(2)}, u32[]{:S(2)}) %all-to-all-start) | async-done | bytes 294944 | tf_op jit(solution)/shard_map/all_to_all | solution.py:409
  15.4 0.0 copy-done.1
  15.4 0.0 copy-done.3
  15.4 1.1 %spectrum.1 = (f32[48,768]{1,0:T(8,128)S(1)}, bf16[48,768]{1,0:T(8,128)(2,1)S(1)}) custom-call(s32[4]{0:T(128)S(1)} %pad_add_fusion.1.info_ref, bf16[8,16,1152]{2,1,0:T(8,128)(2,1)S(1)} %all-to-all-done.recv_ref, bf16[512,768]{1,0:T(8,128)(2,1)S(1)} %copy-done.1, f32[33,1,768]{2,1,0:T(1,128)S(1)} %copy-done.3), custom_call_target="tpu_custom_call" | custom-call | tf_op jit(solution)/shard_map/spectrum/pallas_call | solution.py:217
  16.5 2.6 %collective-permute-start = (bf16[48,768]{1,0:T(8,128)(2,1)S(1)}, bf16[48,768]{1,0:T(8,128)(2,1)S(1)}, u32[]{:S(2)}, u32[]{:S(2)}) collective-permute-start(bf16[48,768]{1,0:T(8,128)(2,1)S(1)} %get-tuple-element.8), channel_id=1, source_target_pairs={{0,16},{2,18},{4,20},{6,22},{8,24},{10,26},{12,28},{14,30},{16,0},... | collective-permute-start | bytes 221192 | tf_op jit(solution)/shard_map/ppermute | solution.py:412
  19.2 2.7 %collective-permute-done.other_ref = bf16[48,768]{1,0:T(8,128)(2,1)S(1)} collective-permute-done((bf16[48,768]{1,0:T(8,128)(2,1)S(1)}, bf16[48,768]{1,0:T(8,128)(2,1)S(1)}, u32[]{:S(2)}, u32[]{:S(2)}) %collective-permute-start) | collective-permute-done | bytes 73760 | tf_op jit(solution)/shard_map/ppermute | solution.py:412
  21.8 0.0 copy-done.2
  21.8 0.3 whiten.1
  22.1 11.7 %all_to_all.10.refs_1_ = bf16[8,48,768]{2,1,0:T(8,128)(2,1)S(1)} all-to-all(bf16[8,48,768]{2,1,0:T(8,128)(2,1)S(1)} %whiten.1), channel_id=1, replica_groups={{0,2,6,4,12,14,10,8},{16,18,22,20,28,30,26,24},{1,3,7,5,13,15,11,9},{17..., dimensions={0} | all-to-all | bytes 1179648 | tf_op jit(solution)/shard_map/all_to_all | solution.py:413
  33.8 0.0 collective-permute-start.1
  33.8 0.0 copy-done.4
  33.8 0.1 fusion
  33.9 0.1 pad_add_fusion.refs_0_
  34.0 1.8 %collective-permute-done.1.refs_2_ = bf16[8,48,768]{2,1,0:T(8,128)(2,1)S(1)} collective-permute-done((bf16[8,48,768]{2,1,0:T(8,128)(2,1)S(1)}, bf16[8,48,768]{2,1,0:T(8,128)(2,1)S(1)}, u32[]{:S(2)}, u32[]{:S(2)}) %collective-permute-start.1) | collective-permute-done | bytes 589856 | tf_op jit(solution)/shard_map/ppermute | solution.py:417
  35.8 0.0 copy-done
  35.8 4.6 %correlate.1 = bf16[2048,512]{1,0:T(8,128)(2,1)} custom-call(s32[131]{0:T(256)S(1)} %pad_add_fusion.refs_0_, bf16[8,48,768]{2,1,0:T(8,128)(2,1)S(1)} %all_to_all.10.refs_1_, bf16[8,48,768]{2,1,0:T(8,128)(2,1)S(1)} %collective-permute-done.1.refs_2_, bf16[768,512]{1,0:T(8,128)(2,1)S(1)} %copy-done), custom_call_target="tpu_custom_call" | custom-call | tf_op jit(solution)/shard_map/correlate/pallas_call | solution.py:366
Async XLA Ops:
  0.0 15.4 %copy-start.1 = (bf16[512,768]{1,0:T(8,128)(2,1)S(1)}, bf16[512,768]{1,0:T(8,128)(2,1)}, u32[]{:S(2)}) copy-start(bf16[512,768]{1,0:T(8,128)(2,1)} %constant.127.inner_ref) | copy-start | bytes 2359300
  0.0 15.4 %copy-start.3 = (f32[33,1,768]{2,1,0:T(1,128)S(1)}, f32[33,1,768]{2,1,0:T(1,128)}, u32[]{:S(2)}) copy-start(f32[33,1,768]{2,1,0:T(1,128)} %constant.123.clone.phase_ref) | copy-start | bytes 304132
  0.0 21.8 %copy-start.2 = (bf16[384,384]{1,0:T(8,128)(2,1)S(1)}, bf16[384,384]{1,0:T(8,128)(2,1)}, u32[]{:S(2)}) copy-start(bf16[384,384]{1,0:T(8,128)(2,1)} %constant.128.band_ref) | copy-start | bytes 884740
  0.0 8.8 %copy-start.5 = (s32[3]{0:T(128)S(1)}, s32[3]{0:T(128)}, u32[]{:S(2)}) copy-start(s32[3]{0:T(128)} %param.9) | copy-start | bytes 40
  2.5 31.3 %copy-start.4 = (s32[256]{0:T(256)S(1)}, s32[256]{0:T(256)}, u32[]{:S(2)}) copy-start(s32[256]{0:T(256)} %param.10) | copy-start | bytes 3076
  2.5 33.3 %copy-start = (bf16[768,512]{1,0:T(8,128)(2,1)S(1)}, bf16[768,512]{1,0:T(8,128)(2,1)}, u32[]{:S(2)}) copy-start(bf16[768,512]{1,0:T(8,128)(2,1)} %constant.129.refs_3_) | copy-start | bytes 2359300
  2.5 12.9 %all-to-all-start = ((bf16[8,16,1152]{2,1,0:T(8,128)(2,1)}), bf16[8,16,1152]{2,1,0:T(8,128)(2,1)S(1)}, u32[]{:S(2)}, u32[]{:S(2)}) async-start(bf16[8,16,1152]{2,1,0:T(8,128)(2,1)} %decimate.1), calls=%async_computation | async-start | bytes 589824 | tf_op jit(solution)/shard_map/all_to_all | solution.py:409
  16.5 5.3 %collective-permute-start = (bf16[48,768]{1,0:T(8,128)(2,1)S(1)}, bf16[48,768]{1,0:T(8,128)(2,1)S(1)}, u32[]{:S(2)}, u32[]{:S(2)}) collective-permute-start(bf16[48,768]{1,0:T(8,128)(2,1)S(1)} %get-tuple-element.8), channel_id=1, source_target_pairs={{0,16},{2,18},{4,20},{6,22},{8,24},{10,26},{12,28},{14,30},{16,0},... | collective-permute-start | bytes 221192 | tf_op jit(solution)/shard_map/ppermute | solution.py:412
  33.8 2.0 %collective-permute-start.1 = (bf16[8,48,768]{2,1,0:T(8,128)(2,1)S(1)}, bf16[8,48,768]{2,1,0:T(8,128)(2,1)S(1)}, u32[]{:S(2)}, u32[]{:S(2)}) collective-permute-start(bf16[8,48,768]{2,1,0:T(8,128)(2,1)S(1)} %all_to_all.10.refs_1_), channel_id=1, source_target_pairs={{1,0},{0,1},{3,2},{2,3},{5,4},{4,5},{7,6},{6,7},{9,8},{8,9},{11,10... | collective-permute-start | bytes 1769480 | tf_op jit(solution)/shard_map/ppermute | solution.py:417

commit v8 on v7

--- a/solution.py
+++ b/solution.py
@@ -262,7 +262,7 @@
 
 def correlate_kernel(groups, group, block, info_ref, *refs):
     spectra = refs[:groups]
-    basis_ref, out_ref, source, receiver, cross_even, cross_odd, lagged, sent = refs[groups:]
+    basis_ref, out_ref, source, near, receiver, cross_even, cross_odd, lagged, sent = refs[groups:]
     rows = HALVES * group
     channels = spectra[0].shape[0] * rows
     receivers = groups * group
@@ -274,7 +274,10 @@
         for number in range(NSEG):
             here = spectrum[position(peer), number * rows : (number + 1) * rows, :].astype(jnp.float32)
             here = jnp.where(half == 0, here[:group], here[group:]) * (1.0 / NSEG)
-            receiver[number, owner] = here
+            near[number, owner] = here
+
+    for number in range(NSEG):
+        receiver[number] = near[number].reshape(receivers, 2 * NBIN).astype(jnp.bfloat16)
 
     def widen(chunk):
         for step, spectrum in enumerate(spectra):
@@ -288,9 +291,8 @@
     def fill(number, cross, chunks):
         for chunk in chunks:
             re_at, im_at = places(chunk)
-            recv = [receiver[seg].reshape(receivers, 2 * NBIN) for seg in range(NSEG)]
-            recv_re = [part[:, re_at].astype(jnp.bfloat16) for part in recv]
-            recv_im = [part[:, im_at].astype(jnp.bfloat16) for part in recv]
+            recv_re = [receiver[seg, :, re_at] for seg in range(NSEG)]
+            recv_im = [receiver[seg, :, im_at] for seg in range(NSEG)]
             for k in range(block):
                 total_re = total_im = None
                 same = pl.ds(info_ref[3 + number * block + k], 8, stride=0)
@@ -324,7 +326,7 @@
     everything = range(CHUNKS)
     for chunk in everything:
         widen(chunk)
-        fill(0, cross_even, [chunk])
+    fill(0, cross_even, everything)
 
     def pair(number):
         lag(2 * number, cross_even)
@@ -369,8 +371,9 @@
         in_specs=[SMEM] + [VMEM] * (groups + 1),
         out_specs=pl.BlockSpec(memory_space=pl.ANY),
         scratch_shapes=[
-            pltpu.VMEM((NSEG, 2 * CHUNKS, channels, LANES), jnp.float32),
+            pltpu.VMEM((NSEG, 2 * CHUNKS, channels + 8, LANES), jnp.float32),
             pltpu.VMEM((NSEG, groups, group, 2 * NBIN), jnp.float32),
+            pltpu.VMEM((NSEG, receivers, 2 * NBIN), jnp.bfloat16),
             pltpu.VMEM((rows, 2 * NBIN), jnp.bfloat16),
             pltpu.VMEM((rows, 2 * NBIN), jnp.bfloat16),
             pltpu.VMEM((many * receivers, NLAG), jnp.bfloat16),

time: 40.7 us -> 40.6 us (level)
  no operation moved by 1% of the time
where the time goes in v8:
time: 40.6 us; the launch traced here: 40.3 us
  blocking collectives  11.7 us (29%)
  waiting for transfers between devices  10.9 us (27%)
  starting transfers between devices  8.98 us (22%)
  Pallas kernels  8.45 us (21%)
    all_to_all x1, blocking collectives, on_device(): lax.all_to_all(white, 'chan', 0, 0, tiled=True, axis_index_groups=cubes)  11.7 us
    all_to_all x1, waiting for transfers between devices, on_device(): lax.all_to_all(sent, 'chan', 0, 0, tiled=True, axis_index_groups=cubes)  6.44 us
    all_to_all x1, starting transfers between devices, on_device(): lax.all_to_all(sent, 'chan', 0, 0, tiled=True, axis_index_groups=cubes)  6.33 us
    pallas_call x1, Pallas kernels, correlate(): pl.pallas_call(kernel, out_shape=jax.ShapeDtypeStruct((many * receivers,...  4.54 us
    ppermute x1, waiting for transfers between devices, on_device(): white = whiten(own, lax.ppermute(send, 'chan', across), peers)  2.67 us
    ppermute x1, starting transfers between devices, on_device(): white = whiten(own, lax.ppermute(send, 'chan', across), peers)  2.65 us
    pallas_call x1, Pallas kernels, decimate(): pl.pallas_call(decimate_kernel, out_shape=jax.ShapeDtypeStruct((peers, HA...  2.5 us
    ppermute x1, waiting for transfers between devices, on_device(): spectra.append(lax.ppermute(held, 'src', pairs))  1.81 us
  transfers between devices with their start and end apart: 3, of which 3 were waited for; matrix products, arithmetic and copies ran while one was open for 1% of the time, Pallas kernels for 0%

profile of v8, /device:TPU:0, one launch (start us, length us, event | category | flops | bytes accessed | tf_op | source)
XLA Modules:
  0.0 40.3 jit_solution(11841565314994763016)
XLA Ops:
  0.0 0.0 copy-start.1
  0.0 0.0 copy-start.3
  0.0 0.0 copy-start.2
  0.0 0.0 copy-start.5
  0.0 2.5 %decimate.1 = bf16[8,16,1152]{2,1,0:T(8,128)(2,1)} custom-call(bf16[2,64,4096]{2,1,0:T(8,128)(2,1)} %bitcast.5, bf16[512,256]{1,0:T(8,128)(2,1)} %constant.126.table_ref), custom_call_target="tpu_custom_call" | custom-call | tf_op jit(solution)/shard_map/decimate/pallas_call | solution.py:124
  2.5 0.0 copy-start.4
  2.5 0.0 copy-start
  2.5 6.3 %all-to-all-start = ((bf16[8,16,1152]{2,1,0:T(8,128)(2,1)}), bf16[8,16,1152]{2,1,0:T(8,128)(2,1)S(1)}, u32[]{:S(2)}, u32[]{:S(2)}) async-start(bf16[8,16,1152]{2,1,0:T(8,128)(2,1)} %decimate.1), calls=%async_computation | async-start | bytes 589824 | tf_op jit(solution)/shard_map/all_to_all | solution.py:412
  8.8 0.0 copy-done.5
  8.9 0.1 pad_add_fusion.1.info_ref
  8.9 6.4 %all-to-all-done.recv_ref = bf16[8,16,1152]{2,1,0:T(8,128)(2,1)S(1)} async-done(((bf16[8,16,1152]{2,1,0:T(8,128)(2,1)}), bf16[8,16,1152]{2,1,0:T(8,128)(2,1)S(1)}, u32[]{:S(2)}, u32[]{:S(2)}) %all-to-all-start) | async-done | bytes 294944 | tf_op jit(solution)/shard_map/all_to_all | solution.py:412
  15.4 0.0 copy-done.1
  15.4 0.0 copy-done.3
  15.4 1.1 %spectrum.1 = (f32[48,768]{1,0:T(8,128)S(1)}, bf16[48,768]{1,0:T(8,128)(2,1)S(1)}) custom-call(s32[4]{0:T(128)S(1)} %pad_add_fusion.1.info_ref, bf16[8,16,1152]{2,1,0:T(8,128)(2,1)S(1)} %all-to-all-done.recv_ref, bf16[512,768]{1,0:T(8,128)(2,1)S(1)} %copy-done.1, f32[33,1,768]{2,1,0:T(1,128)S(1)} %copy-done.3), custom_call_target="tpu_custom_call" | custom-call | tf_op jit(solution)/shard_map/spectrum/pallas_call | solution.py:217
  16.5 2.6 %collective-permute-start = (bf16[48,768]{1,0:T(8,128)(2,1)S(1)}, bf16[48,768]{1,0:T(8,128)(2,1)S(1)}, u32[]{:S(2)}, u32[]{:S(2)}) collective-permute-start(bf16[48,768]{1,0:T(8,128)(2,1)S(1)} %get-tuple-element.8), channel_id=1, source_target_pairs={{0,16},{2,18},{4,20},{6,22},{8,24},{10,26},{12,28},{14,30},{16,0},... | collective-permute-start | bytes 221192 | tf_op jit(solution)/shard_map/ppermute | solution.py:415
  19.2 2.7 %collective-permute-done.other_ref = bf16[48,768]{1,0:T(8,128)(2,1)S(1)} collective-permute-done((bf16[48,768]{1,0:T(8,128)(2,1)S(1)}, bf16[48,768]{1,0:T(8,128)(2,1)S(1)}, u32[]{:S(2)}, u32[]{:S(2)}) %collective-permute-start) | collective-permute-done | bytes 73760 | tf_op jit(solution)/shard_map/ppermute | solution.py:415
  21.8 0.0 copy-done.2
  21.8 0.3 whiten.1
  22.1 11.7 %all_to_all.10.refs_1_ = bf16[8,48,768]{2,1,0:T(8,128)(2,1)S(1)} all-to-all(bf16[8,48,768]{2,1,0:T(8,128)(2,1)S(1)} %whiten.1), channel_id=1, replica_groups={{0,2,6,4,12,14,10,8},{16,18,22,20,28,30,26,24},{1,3,7,5,13,15,11,9},{17..., dimensions={0} | all-to-all | bytes 1179648 | tf_op jit(solution)/shard_map/all_to_all | solution.py:416
  33.8 0.0 collective-permute-start.1
  33.8 0.0 copy-done.4
  33.8 0.1 fusion
  33.9 0.1 pad_add_fusion.refs_0_
  34.0 1.8 %collective-permute-done.1.refs_2_ = bf16[8,48,768]{2,1,0:T(8,128)(2,1)S(1)} collective-permute-done((bf16[8,48,768]{2,1,0:T(8,128)(2,1)S(1)}, bf16[8,48,768]{2,1,0:T(8,128)(2,1)S(1)}, u32[]{:S(2)}, u32[]{:S(2)}) %collective-permute-start.1) | collective-permute-done | bytes 589856 | tf_op jit(solution)/shard_map/ppermute | solution.py:420
  35.8 0.0 copy-done
  35.8 4.5 %correlate.1 = bf16[2048,512]{1,0:T(8,128)(2,1)} custom-call(s32[131]{0:T(256)S(1)} %pad_add_fusion.refs_0_, bf16[8,48,768]{2,1,0:T(8,128)(2,1)S(1)} %all_to_all.10.refs_1_, bf16[8,48,768]{2,1,0:T(8,128)(2,1)S(1)} %collective-permute-done.1.refs_2_, bf16[768,512]{1,0:T(8,128)(2,1)S(1)} %copy-done), custom_call_target="tpu_custom_call" | custom-call | tf_op jit(solution)/shard_map/correlate/pallas_call | solution.py:368
Async XLA Ops:
  0.0 15.4 %copy-start.1 = (bf16[512,768]{1,0:T(8,128)(2,1)S(1)}, bf16[512,768]{1,0:T(8,128)(2,1)}, u32[]{:S(2)}) copy-start(bf16[512,768]{1,0:T(8,128)(2,1)} %constant.127.inner_ref) | copy-start | bytes 2359300
  0.0 15.4 %copy-start.3 = (f32[33,1,768]{2,1,0:T(1,128)S(1)}, f32[33,1,768]{2,1,0:T(1,128)}, u32[]{:S(2)}) copy-start(f32[33,1,768]{2,1,0:T(1,128)} %constant.123.clone.phase_ref) | copy-start | bytes 304132
  0.0 21.8 %copy-start.2 = (bf16[384,384]{1,0:T(8,128)(2,1)S(1)}, bf16[384,384]{1,0:T(8,128)(2,1)}, u32[]{:S(2)}) copy-start(bf16[384,384]{1,0:T(8,128)(2,1)} %constant.128.band_ref) | copy-start | bytes 884740
  0.0 8.8 %copy-start.5 = (s32[3]{0:T(128)S(1)}, s32[3]{0:T(128)}, u32[]{:S(2)}) copy-start(s32[3]{0:T(128)} %param.9) | copy-start | bytes 40
  2.5 31.3 %copy-start.4 = (s32[256]{0:T(256)S(1)}, s32[256]{0:T(256)}, u32[]{:S(2)}) copy-start(s32[256]{0:T(256)} %param.10) | copy-start | bytes 3076
  2.5 33.3 %copy-start = (bf16[768,512]{1,0:T(8,128)(2,1)S(1)}, bf16[768,512]{1,0:T(8,128)(2,1)}, u32[]{:S(2)}) copy-start(bf16[768,512]{1,0:T(8,128)(2,1)} %constant.129.refs_3_) | copy-start | bytes 2359300
  2.5 12.9 %all-to-all-start = ((bf16[8,16,1152]{2,1,0:T(8,128)(2,1)}), bf16[8,16,1152]{2,1,0:T(8,128)(2,1)S(1)}, u32[]{:S(2)}, u32[]{:S(2)}) async-start(bf16[8,16,1152]{2,1,0:T(8,128)(2,1)} %decimate.1), calls=%async_computation | async-start | bytes 589824 | tf_op jit(solution)/shard_map/all_to_all | solution.py:412
  16.5 5.3 %collective-permute-start = (bf16[48,768]{1,0:T(8,128)(2,1)S(1)}, bf16[48,768]{1,0:T(8,128)(2,1)S(1)}, u32[]{:S(2)}, u32[]{:S(2)}) collective-permute-start(bf16[48,768]{1,0:T(8,128)(2,1)S(1)} %get-tuple-element.8), channel_id=1, source_target_pairs={{0,16},{2,18},{4,20},{6,22},{8,24},{10,26},{12,28},{14,30},{16,0},... | collective-permute-start | bytes 221192 | tf_op jit(solution)/shard_map/ppermute | solution.py:415
  33.8 2.0 %collective-permute-start.1 = (bf16[8,48,768]{2,1,0:T(8,128)(2,1)S(1)}, bf16[8,48,768]{2,1,0:T(8,128)(2,1)S(1)}, u32[]{:S(2)}, u32[]{:S(2)}) collective-permute-start(bf16[8,48,768]{2,1,0:T(8,128)(2,1)S(1)} %all_to_all.10.refs_1_), channel_id=1, source_target_pairs={{1,0},{0,1},{3,2},{2,3},{5,4},{4,5},{7,6},{6,7},{9,8},{8,9},{11,10... | collective-permute-start | bytes 1769480 | tf_op jit(solution)/shard_map/ppermute | solution.py:420

commit v9 on v8

--- a/solution.py
+++ b/solution.py
@@ -134,13 +134,12 @@
     )(strain.reshape(HALVES, half_rows, length), filter_table())
 
 
-def spectrum_kernel(info_ref, recv_ref, inner_ref, phase_ref, own_ref, send_ref, lhs, edge):
+def spectrum_kernel(info_vmem, recv_ref, inner_ref, phase_ref, own_ref, send_ref, lhs, edge, info_ref, told):
     peers, rows, width = recv_ref.shape
     span = width - LANES
     blocks = peers * span // BLOCK
-    base = info_ref[0] * (peers * span)
-    first = info_ref[0] * blocks + 1
-    starts = [info_ref[1 + number] - base for number in range(NSEG)]
+    tell = pltpu.make_async_copy(info_vmem, info_ref, told)
+    tell.start()
 
     for peer in range(peers):
         for tile in range(span // LANES):
@@ -150,6 +149,11 @@
                 values = (values.astype(jnp.float32) + carried).astype(jnp.bfloat16)
             block, inside = divmod(peer * span + tile * LANES, BLOCK)
             lhs[block * rows : (block + 1) * rows, inside : inside + LANES] = values
+
+    tell.wait()
+    base = info_ref[0] * (peers * span)
+    first = info_ref[0] * blocks + 1
+    starts = [info_ref[1 + number] - base for number in range(NSEG)]
 
     cuts = []
     lane = lax.broadcasted_iota(jnp.int32, (rows, BLOCK), 1)
@@ -220,11 +224,13 @@
             jax.ShapeDtypeStruct((many, 2 * NBIN), jnp.float32),
             jax.ShapeDtypeStruct((many, 2 * NBIN), jnp.bfloat16),
         ],
-        in_specs=[SMEM, VMEM, VMEM, VMEM],
+        in_specs=[VMEM] * 4,
         out_specs=[VMEM, VMEM],
         scratch_shapes=[
             pltpu.VMEM(((blocks + 2 * NSEG) * rows, BLOCK), jnp.bfloat16),
             pltpu.VMEM((many, LANES), jnp.bfloat16),
+            pltpu.SMEM(info.shape, jnp.int32),
+            pltpu.SemaphoreType.DMA,
         ],
         compiler_params=pltpu.CompilerParams(vmem_limit_bytes=32 * 1024 * 1024),
         name="spectrum",
@@ -260,24 +266,15 @@
     )(own, other, band_table())
 
 
-def correlate_kernel(groups, group, block, info_ref, *refs):
+def correlate_kernel(groups, group, block, info_vmem, *refs):
     spectra = refs[:groups]
-    basis_ref, out_ref, source, near, receiver, cross_even, cross_odd, lagged, sent = refs[groups:]
+    basis_ref, out_ref, source, near, receiver, cross_even, cross_odd, lagged, sent, info_ref, told = refs[groups:]
     rows = HALVES * group
     channels = spectra[0].shape[0] * rows
     receivers = groups * group
     blocks = sent.shape[0]
-    half, peer, mine = info_ref[0], info_ref[1], info_ref[2]
-
-    for step, spectrum in enumerate(spectra):
-        owner = lax.rem(mine + step, groups)
-        for number in range(NSEG):
-            here = spectrum[position(peer), number * rows : (number + 1) * rows, :].astype(jnp.float32)
-            here = jnp.where(half == 0, here[:group], here[group:]) * (1.0 / NSEG)
-            near[number, owner] = here
-
-    for number in range(NSEG):
-        receiver[number] = near[number].reshape(receivers, 2 * NBIN).astype(jnp.bfloat16)
+    tell = pltpu.make_async_copy(info_vmem, info_ref, told)
+    tell.start()
 
     def widen(chunk):
         for step, spectrum in enumerate(spectra):
@@ -287,6 +284,21 @@
                     held = held.astype(jnp.float32).reshape(channels, LANES)
                     at = slice(step * channels, (step + 1) * channels)
                     source[number, 2 * chunk + part, at, :] = held
+
+    for chunk in range(CHUNKS):
+        widen(chunk)
+    tell.wait()
+    half, peer, mine = info_ref[0], info_ref[1], info_ref[2]
+
+    for step, spectrum in enumerate(spectra):
+        owner = lax.rem(mine + step, groups)
+        for number in range(NSEG):
+            here = spectrum[position(peer), number * rows : (number + 1) * rows, :].astype(jnp.float32)
+            here = jnp.where(half == 0, here[:group], here[group:]) * (1.0 / NSEG)
+            near[number, owner] = here
+
+    for number in range(NSEG):
+        receiver[number] = near[number].reshape(receivers, 2 * NBIN).astype(jnp.bfloat16)
 
     def fill(number, cross, chunks):
         for chunk in chunks:
@@ -324,8 +336,6 @@
         return pltpu.make_async_copy(lagged.at[at], out_ref.at[at], sent.at[number])
 
     everything = range(CHUNKS)
-    for chunk in everything:
-        widen(chunk)
     fill(0, cross_even, everything)
 
     def pair(number):
@@ -368,7 +378,7 @@
     return pl.pallas_call(
         kernel,
         out_shape=jax.ShapeDtypeStruct((many * receivers, NLAG), jnp.bfloat16),
-        in_specs=[SMEM] + [VMEM] * (groups + 1),
+        in_specs=[VMEM] * (groups + 2),
         out_specs=pl.BlockSpec(memory_space=pl.ANY),
         scratch_shapes=[
             pltpu.VMEM((NSEG, 2 * CHUNKS, channels + 8, LANES), jnp.float32),
@@ -378,6 +388,8 @@
             pltpu.VMEM((rows, 2 * NBIN), jnp.bfloat16),
             pltpu.VMEM((many * receivers, NLAG), jnp.bfloat16),
             pltpu.SemaphoreType.DMA((many // block,)),
+            pltpu.SMEM(info.shape, jnp.int32),
+            pltpu.SemaphoreType.DMA,
         ],
         compiler_params=pltpu.CompilerParams(
             vmem_limit_bytes=min(16 * 1024 * 1024 + 3 * held, 63 * 1024 * 1024)

time: 40.6 us -> 40.5 us (level)
  no operation moved by 1% of the time
where the time goes in v9:
time: 40.5 us; the launch traced here: 40.2 us
  blocking collectives  11.7 us (29%)
  waiting for transfers between devices  10.9 us (27%)
  starting transfers between devices  8.98 us (22%)
  Pallas kernels  8.33 us (21%)
    all_to_all x1, blocking collectives, on_device(): lax.all_to_all(white, 'chan', 0, 0, tiled=True, axis_index_groups=cubes)  11.7 us
    all_to_all x1, waiting for transfers between devices, on_device(): lax.all_to_all(sent, 'chan', 0, 0, tiled=True, axis_index_groups=cubes)  6.44 us
    all_to_all x1, starting transfers between devices, on_device(): lax.all_to_all(sent, 'chan', 0, 0, tiled=True, axis_index_groups=cubes)  6.33 us
    pallas_call x1, Pallas kernels, correlate(): pl.pallas_call(kernel, out_shape=jax.ShapeDtypeStruct((many * receivers,...  4.41 us
    ppermute x1, waiting for transfers between devices, on_device(): white = whiten(own, lax.ppermute(send, 'chan', across), peers)  2.67 us
    ppermute x1, starting transfers between devices, on_device(): white = whiten(own, lax.ppermute(send, 'chan', across), peers)  2.65 us
    pallas_call x1, Pallas kernels, decimate(): pl.pallas_call(decimate_kernel, out_shape=jax.ShapeDtypeStruct((peers, HA...  2.5 us
    ppermute x1, waiting for transfers between devices, on_device(): spectra.append(lax.ppermute(held, 'src', pairs))  1.81 us
  transfers between devices with their start and end apart: 3, of which 3 were waited for; matrix products, arithmetic and copies ran while one was open for 1% of the time, Pallas kernels for 0%

profile of v9, /device:TPU:0, one launch (start us, length us, event | category | flops | bytes accessed | tf_op | source)
XLA Modules:
  0.0 40.2 jit_solution(8672625261150735829)
XLA Ops:
  0.0 0.0 copy-start.1
  0.0 0.0 copy-start.3
  0.0 0.0 copy-start.2
  0.0 0.0 copy-start.5
  0.0 2.5 %decimate.1 = bf16[8,16,1152]{2,1,0:T(8,128)(2,1)} custom-call(bf16[2,64,4096]{2,1,0:T(8,128)(2,1)} %bitcast.5, bf16[512,256]{1,0:T(8,128)(2,1)} %constant.126.table_ref), custom_call_target="tpu_custom_call" | custom-call | tf_op jit(solution)/shard_map/decimate/pallas_call | solution.py:124
  2.5 0.0 copy-start.4
  2.5 0.0 copy-start
  2.5 6.3 %all-to-all-start = ((bf16[8,16,1152]{2,1,0:T(8,128)(2,1)}), bf16[8,16,1152]{2,1,0:T(8,128)(2,1)S(1)}, u32[]{:S(2)}, u32[]{:S(2)}) async-start(bf16[8,16,1152]{2,1,0:T(8,128)(2,1)} %decimate.1), calls=%async_computation | async-start | bytes 589824 | tf_op jit(solution)/shard_map/all_to_all | solution.py:424
  8.8 0.0 copy-done.5
  8.9 0.1 pad_add_fusion.1.info_vmem
  8.9 6.4 %all-to-all-done.recv_ref = bf16[8,16,1152]{2,1,0:T(8,128)(2,1)S(1)} async-done(((bf16[8,16,1152]{2,1,0:T(8,128)(2,1)}), bf16[8,16,1152]{2,1,0:T(8,128)(2,1)S(1)}, u32[]{:S(2)}, u32[]{:S(2)}) %all-to-all-start) | async-done | bytes 294944 | tf_op jit(solution)/shard_map/all_to_all | solution.py:424
  15.4 0.0 copy-done.1
  15.4 0.0 copy-done.3
  15.4 1.2 %spectrum.1 = (f32[48,768]{1,0:T(8,128)S(1)}, bf16[48,768]{1,0:T(8,128)(2,1)S(1)}) custom-call(s32[4]{0:T(128)S(1)} %pad_add_fusion.1.info_vmem, bf16[8,16,1152]{2,1,0:T(8,128)(2,1)S(1)} %all-to-all-done.recv_ref, bf16[512,768]{1,0:T(8,128)(2,1)S(1)} %copy-done.1, f32[33,1,768]{2,1,0:T(1,128)S(1)} %copy-done.3), custom_call_target="tpu_custom_call" | custom-call | tf_op jit(solution)/shard_map/spectrum/pallas_call | solution.py:221
  16.5 2.6 %collective-permute-start = (bf16[48,768]{1,0:T(8,128)(2,1)S(1)}, bf16[48,768]{1,0:T(8,128)(2,1)S(1)}, u32[]{:S(2)}, u32[]{:S(2)}) collective-permute-start(bf16[48,768]{1,0:T(8,128)(2,1)S(1)} %get-tuple-element.8), channel_id=1, source_target_pairs={{0,16},{2,18},{4,20},{6,22},{8,24},{10,26},{12,28},{14,30},{16,0},... | collective-permute-start | bytes 221192 | tf_op jit(solution)/shard_map/ppermute | solution.py:427
  19.2 2.7 %collective-permute-done.other_ref = bf16[48,768]{1,0:T(8,128)(2,1)S(1)} collective-permute-done((bf16[48,768]{1,0:T(8,128)(2,1)S(1)}, bf16[48,768]{1,0:T(8,128)(2,1)S(1)}, u32[]{:S(2)}, u32[]{:S(2)}) %collective-permute-start) | collective-permute-done | bytes 73760 | tf_op jit(solution)/shard_map/ppermute | solution.py:427
  21.9 0.0 copy-done.2
  21.9 0.3 whiten.1
  22.1 11.7 %all_to_all.10.refs_1_ = bf16[8,48,768]{2,1,0:T(8,128)(2,1)S(1)} all-to-all(bf16[8,48,768]{2,1,0:T(8,128)(2,1)S(1)} %whiten.1), channel_id=1, replica_groups={{0,2,6,4,12,14,10,8},{16,18,22,20,28,30,26,24},{1,3,7,5,13,15,11,9},{17..., dimensions={0} | all-to-all | bytes 1179648 | tf_op jit(solution)/shard_map/all_to_all | solution.py:428
  33.8 0.0 collective-permute-start.1
  33.8 0.0 copy-done.4
  33.8 0.1 fusion
  33.9 0.1 pad_add_fusion.refs_0_
  34.0 1.8 %collective-permute-done.1.refs_2_ = bf16[8,48,768]{2,1,0:T(8,128)(2,1)S(1)} collective-permute-done((bf16[8,48,768]{2,1,0:T(8,128)(2,1)S(1)}, bf16[8,48,768]{2,1,0:T(8,128)(2,1)S(1)}, u32[]{:S(2)}, u32[]{:S(2)}) %collective-permute-start.1) | collective-permute-done | bytes 589856 | tf_op jit(solution)/shard_map/ppermute | solution.py:432
  35.8 0.0 copy-done
  35.8 4.4 %correlate.1 = bf16[2048,512]{1,0:T(8,128)(2,1)} custom-call(s32[131]{0:T(256)S(1)} %pad_add_fusion.refs_0_, bf16[8,48,768]{2,1,0:T(8,128)(2,1)S(1)} %all_to_all.10.refs_1_, bf16[8,48,768]{2,1,0:T(8,128)(2,1)S(1)} %collective-permute-done.1.refs_2_, bf16[768,512]{1,0:T(8,128)(2,1)S(1)} %copy-done), custom_call_target="tpu_custom_call" | custom-call | tf_op jit(solution)/shard_map/correlate/pallas_call | solution.py:378
Async XLA Ops:
  0.0 15.4 %copy-start.1 = (bf16[512,768]{1,0:T(8,128)(2,1)S(1)}, bf16[512,768]{1,0:T(8,128)(2,1)}, u32[]{:S(2)}) copy-start(bf16[512,768]{1,0:T(8,128)(2,1)} %constant.127.inner_ref) | copy-start | bytes 2359300
  0.0 15.4 %copy-start.3 = (f32[33,1,768]{2,1,0:T(1,128)S(1)}, f32[33,1,768]{2,1,0:T(1,128)}, u32[]{:S(2)}) copy-start(f32[33,1,768]{2,1,0:T(1,128)} %constant.123.clone.phase_ref) | copy-start | bytes 304132
  0.0 21.9 %copy-start.2 = (bf16[384,384]{1,0:T(8,128)(2,1)S(1)}, bf16[384,384]{1,0:T(8,128)(2,1)}, u32[]{:S(2)}) copy-start(bf16[384,384]{1,0:T(8,128)(2,1)} %constant.128.band_ref) | copy-start | bytes 884740
  0.0 8.8 %copy-start.5 = (s32[3]{0:T(128)S(1)}, s32[3]{0:T(128)}, u32[]{:S(2)}) copy-start(s32[3]{0:T(128)} %param.9) | copy-start | bytes 40
  2.5 31.3 %copy-start.4 = (s32[256]{0:T(256)S(1)}, s32[256]{0:T(256)}, u32[]{:S(2)}) copy-start(s32[256]{0:T(256)} %param.10) | copy-start | bytes 3076
  2.5 33.3 %copy-start = (bf16[768,512]{1,0:T(8,128)(2,1)S(1)}, bf16[768,512]{1,0:T(8,128)(2,1)}, u32[]{:S(2)}) copy-start(bf16[768,512]{1,0:T(8,128)(2,1)} %constant.129.refs_3_) | copy-start | bytes 2359300
  2.5 12.9 %all-to-all-start = ((bf16[8,16,1152]{2,1,0:T(8,128)(2,1)}), bf16[8,16,1152]{2,1,0:T(8,128)(2,1)S(1)}, u32[]{:S(2)}, u32[]{:S(2)}) async-start(bf16[8,16,1152]{2,1,0:T(8,128)(2,1)} %decimate.1), calls=%async_computation | async-start | bytes 589824 | tf_op jit(solution)/shard_map/all_to_all | solution.py:424
  16.5 5.3 %collective-permute-start = (bf16[48,768]{1,0:T(8,128)(2,1)S(1)}, bf16[48,768]{1,0:T(8,128)(2,1)S(1)}, u32[]{:S(2)}, u32[]{:S(2)}) collective-permute-start(bf16[48,768]{1,0:T(8,128)(2,1)S(1)} %get-tuple-element.8), channel_id=1, source_target_pairs={{0,16},{2,18},{4,20},{6,22},{8,24},{10,26},{12,28},{14,30},{16,0},... | collective-permute-start | bytes 221192 | tf_op jit(solution)/shard_map/ppermute | solution.py:427
  33.8 2.0 %collective-permute-start.1 = (bf16[8,48,768]{2,1,0:T(8,128)(2,1)S(1)}, bf16[8,48,768]{2,1,0:T(8,128)(2,1)S(1)}, u32[]{:S(2)}, u32[]{:S(2)}) collective-permute-start(bf16[8,48,768]{2,1,0:T(8,128)(2,1)S(1)} %all_to_all.10.refs_1_), channel_id=1, source_target_pairs={{1,0},{0,1},{3,2},{2,3},{5,4},{4,5},{7,6},{6,7},{9,8},{8,9},{11,10... | collective-permute-start | bytes 1769480 | tf_op jit(solution)/shard_map/ppermute | solution.py:432

commit v10 on v9

--- a/solution.py
+++ b/solution.py
@@ -93,8 +93,9 @@
 
 def decimate_kernel(strain_ref, table_ref, out_ref):
     halves, rows, length = strain_ref.shape
-    group = out_ref.shape[1] // halves
     tiles = length // BLOCK
+    group = out_ref.shape[1] // (halves * tiles + 1)
+    wide = halves * group
     many = halves * rows
     first = pl.program_id(0) * (rows // group)
     x = strain_ref[...].reshape(many, length)
@@ -112,41 +113,55 @@
                 values[half * rows + peer * group : half * rows + (peer + 1) * group]
                 for half in range(halves)
             ]
-            part = jnp.concatenate(part, axis=0).astype(jnp.bfloat16)
-            out_ref[position(first + peer) - first, :, tile * LANES : (tile + 1) * LANES] = part
+            place = position(first + peer) - first
+            if tile < tiles:
+                part = jnp.concatenate(part, axis=0).astype(jnp.bfloat16)
+                out_ref[place, tile * wide : (tile + 1) * wide, :] = part
+            else:
+                part = part[0] + pltpu.roll(part[1], LANES // 2, axis=1)
+                out_ref[place, tiles * wide :, :] = part.astype(jnp.bfloat16)
 
 
 def decimate(strain, peers, group):
     rows, length = strain.shape
     half_rows = rows // HALVES
-    width = length // DEC + LANES
+    many = length // BLOCK * HALVES * group + group
     steps = 2
     return pl.pallas_call(
         decimate_kernel,
-        out_shape=jax.ShapeDtypeStruct((peers, HALVES * group, width), jnp.bfloat16),
+        out_shape=jax.ShapeDtypeStruct((peers, many, LANES), jnp.bfloat16),
         grid=(steps,),
         in_specs=[
             pl.BlockSpec((HALVES, half_rows // steps, length), lambda i: (0, i, 0)),
             pl.BlockSpec((BLOCK, 2 * LANES), lambda i: (0, 0)),
         ],
-        out_specs=pl.BlockSpec((peers // steps, HALVES * group, width), lambda i: (i, 0, 0)),
+        out_specs=pl.BlockSpec((peers // steps, many, LANES), lambda i: (i, 0, 0)),
         name="decimate",
     )(strain.reshape(HALVES, half_rows, length), filter_table())
 
 
 def spectrum_kernel(info_vmem, recv_ref, inner_ref, phase_ref, own_ref, send_ref, lhs, edge, info_ref, told):
-    peers, rows, width = recv_ref.shape
-    span = width - LANES
+    peers, many, _ = recv_ref.shape
+    rows = own_ref.shape[0] // NSEG
+    group = rows // HALVES
+    tiles = (many - group) // rows
+    span = tiles * LANES
     blocks = peers * span // BLOCK
+    spot = lax.broadcasted_iota(jnp.int32, (rows, LANES), 1)
+
+    def tail(peer):
+        held = recv_ref[position(peer), tiles * rows :, :].astype(jnp.float32)
+        held = jnp.concatenate([held, pltpu.roll(held, LANES // 2, axis=1)], axis=0)
+        return jnp.where(spot >= LANES // 2, held, 0.0)
+
     tell = pltpu.make_async_copy(info_vmem, info_ref, told)
     tell.start()
 
     for peer in range(peers):
         for tile in range(span // LANES):
-            values = recv_ref[position(peer), :, tile * LANES : (tile + 1) * LANES]
+            values = recv_ref[position(peer), tile * rows : (tile + 1) * rows, :]
             if tile == span // LANES - 1 and peer + 1 < peers:
-                carried = recv_ref[position(peer + 1), :, span:].astype(jnp.float32)
-                values = (values.astype(jnp.float32) + carried).astype(jnp.bfloat16)
+                values = (values.astype(jnp.float32) + tail(peer + 1)).astype(jnp.bfloat16)
             block, inside = divmod(peer * span + tile * LANES, BLOCK)
             lhs[block * rows : (block + 1) * rows, inside : inside + LANES] = values
 
@@ -170,7 +185,7 @@
             lhs[row : row + rows, :] = values
             cuts.append((number, held))
     before = lax.broadcasted_iota(jnp.int32, (rows, LANES), 1) - LANES
-    carried = recv_ref[0, :, span:].astype(jnp.float32)
+    carried = tail(0)
     for number, start in enumerate(starts):
         kept = (before >= start) & (before < start + SEG)
         values = jnp.where(kept, carried, 0.0).astype(jnp.bfloat16)
@@ -193,8 +208,8 @@
 
         table = inner_ref[:, re_at.start : im_at.stop]
         body = dot(lhs[...], table)
-        tail = dot(edge[...], table[BLOCK - LANES :])
-        totals = [turned(tail[number * rows : (number + 1) * rows], -1) for number in range(NSEG)]
+        ends = dot(edge[...], table[BLOCK - LANES :])
+        totals = [turned(ends[number * rows : (number + 1) * rows], -1) for number in range(NSEG)]
         for block in range(blocks):
             part_re, part_im = turned(body[block * rows : (block + 1) * rows], block)
             for number in range(NSEG):
@@ -214,9 +229,10 @@
             send_ref[at, im_at] = total_im.astype(jnp.bfloat16)
 
 
-def partial_spectrum(info, recv):
-    peers, rows, width = recv.shape
-    blocks = peers * (width - LANES) // BLOCK
+def partial_spectrum(info, recv, group):
+    rows = HALVES * group
+    peers = recv.shape[0]
+    blocks = peers * (recv.shape[1] - group) // rows * LANES // BLOCK
     many = NSEG * rows
     return pl.pallas_call(
         spectrum_kernel,
@@ -422,7 +438,7 @@
 
     sent = decimate(strain, peers, per_device)
     samples = lax.all_to_all(sent, "chan", 0, 0, tiled=True, axis_index_groups=cubes)
-    own, send = partial_spectrum(jnp.concatenate([half, seg_start]), samples)
+    own, send = partial_spectrum(jnp.concatenate([half, seg_start]), samples, per_device)
     across = [(i, (i + peers) % chan_count) for i in range(chan_count)]
     white = whiten(own, lax.ppermute(send, "chan", across), peers)
     held = lax.all_to_all(white, "chan", 0, 0, tiled=True, axis_index_groups=cubes)

time: 40.5 us -> 40.4 us (level)
  no operation moved by 1% of the time
where the time goes in v10:
time: 40.4 us; the launch traced here: 40.1 us
  blocking collectives  11.6 us (29%)
  waiting for transfers between devices  10.8 us (27%)
  starting transfers between devices  8.98 us (22%)
  Pallas kernels  8.35 us (21%)
    all_to_all x1, blocking collectives, on_device(): lax.all_to_all(white, 'chan', 0, 0, tiled=True, axis_index_groups=cubes)  11.6 us
    all_to_all x1, starting transfers between devices, on_device(): lax.all_to_all(sent, 'chan', 0, 0, tiled=True, axis_index_groups=cubes)  6.33 us
    all_to_all x1, waiting for transfers between devices, on_device(): lax.all_to_all(sent, 'chan', 0, 0, tiled=True, axis_index_groups=cubes)  6.31 us
    pallas_call x1, Pallas kernels, correlate(): pl.pallas_call(kernel, out_shape=jax.ShapeDtypeStruct((many * receivers,...  4.42 us
    ppermute x1, waiting for transfers between devices, on_device(): white = whiten(own, lax.ppermute(send, 'chan', across), peers)  2.68 us
    ppermute x1, starting transfers between devices, on_device(): white = whiten(own, lax.ppermute(send, 'chan', across), peers)  2.65 us
    pallas_call x1, Pallas kernels, decimate(): pl.pallas_call(decimate_kernel, out_shape=jax.ShapeDtypeStruct((peers, ma...  2.5 us
    ppermute x1, waiting for transfers between devices, on_device(): spectra.append(lax.ppermute(held, 'src', pairs))  1.81 us
  transfers between devices with their start and end apart: 3, of which 3 were waited for; matrix products, arithmetic and copies ran while one was open for 1% of the time, Pallas kernels for 0%

profile of v10, /device:TPU:0, one launch (start us, length us, event | category | flops | bytes accessed | tf_op | source)
XLA Modules:
  0.0 40.1 jit_solution(10551069629045889259)
XLA Ops:
  0.0 0.0 copy-start.1
  0.0 0.0 copy-start.3
  0.0 0.0 copy-start.2
  0.0 0.0 copy-start.5
  0.0 2.5 %decimate.1 = bf16[8,136,128]{2,1,0:T(8,128)(2,1)} custom-call(bf16[2,64,4096]{2,1,0:T(8,128)(2,1)} %bitcast.5, bf16[512,256]{1,0:T(8,128)(2,1)} %constant.126.table_ref), custom_call_target="tpu_custom_call" | custom-call | tf_op jit(solution)/shard_map/decimate/pallas_call | solution.py:130
  2.5 0.0 copy-start.4
  2.5 0.0 copy-start
  2.5 6.3 %all-to-all-start = ((bf16[8,136,128]{2,1,0:T(8,128)(2,1)}), bf16[8,136,128]{2,1,0:T(8,128)(2,1)S(1)}, u32[]{:S(2)}, u32[]{:S(2)}) async-start(bf16[8,136,128]{2,1,0:T(8,128)(2,1)} %decimate.1), calls=%async_computation | async-start | bytes 557056 | tf_op jit(solution)/shard_map/all_to_all | solution.py:440
  8.8 0.0 copy-done.5
  8.8 0.1 pad_add_fusion.1.info_vmem
  8.9 6.3 %all-to-all-done.recv_ref = bf16[8,136,128]{2,1,0:T(8,128)(2,1)S(1)} async-done(((bf16[8,136,128]{2,1,0:T(8,128)(2,1)}), bf16[8,136,128]{2,1,0:T(8,128)(2,1)S(1)}, u32[]{:S(2)}, u32[]{:S(2)}) %all-to-all-start) | async-done | bytes 278560 | tf_op jit(solution)/shard_map/all_to_all | solution.py:440
  15.2 0.0 copy-done.1
  15.2 0.0 copy-done.3
  15.2 1.2 %spectrum.1 = (f32[48,768]{1,0:T(8,128)S(1)}, bf16[48,768]{1,0:T(8,128)(2,1)S(1)}) custom-call(s32[4]{0:T(128)S(1)} %pad_add_fusion.1.info_vmem, bf16[8,136,128]{2,1,0:T(8,128)(2,1)S(1)} %all-to-all-done.recv_ref, bf16[512,768]{1,0:T(8,128)(2,1)S(1)} %copy-done.1, f32[33,1,768]{2,1,0:T(1,128)S(1)} %copy-done.3), custom_call_target="tpu_custom_call" | custom-call | tf_op jit(solution)/shard_map/spectrum/pallas_call | solution.py:237
  16.4 2.6 %collective-permute-start = (bf16[48,768]{1,0:T(8,128)(2,1)S(1)}, bf16[48,768]{1,0:T(8,128)(2,1)S(1)}, u32[]{:S(2)}, u32[]{:S(2)}) collective-permute-start(bf16[48,768]{1,0:T(8,128)(2,1)S(1)} %get-tuple-element.8), channel_id=1, source_target_pairs={{0,16},{2,18},{4,20},{6,22},{8,24},{10,26},{12,28},{14,30},{16,0},... | collective-permute-start | bytes 221192 | tf_op jit(solution)/shard_map/ppermute | solution.py:443
  19.1 2.7 %collective-permute-done.other_ref = bf16[48,768]{1,0:T(8,128)(2,1)S(1)} collective-permute-done((bf16[48,768]{1,0:T(8,128)(2,1)S(1)}, bf16[48,768]{1,0:T(8,128)(2,1)S(1)}, u32[]{:S(2)}, u32[]{:S(2)}) %collective-permute-start) | collective-permute-done | bytes 73760 | tf_op jit(solution)/shard_map/ppermute | solution.py:443
  21.7 0.0 copy-done.2
  21.8 0.3 whiten.1
  22.0 11.6 %all_to_all.10.refs_1_ = bf16[8,48,768]{2,1,0:T(8,128)(2,1)S(1)} all-to-all(bf16[8,48,768]{2,1,0:T(8,128)(2,1)S(1)} %whiten.1), channel_id=1, replica_groups={{0,2,6,4,12,14,10,8},{16,18,22,20,28,30,26,24},{1,3,7,5,13,15,11,9},{17..., dimensions={0} | all-to-all | bytes 1179648 | tf_op jit(solution)/shard_map/all_to_all | solution.py:444
  33.6 0.0 collective-permute-start.1
  33.6 0.0 copy-done.4
  33.6 0.1 fusion
  33.8 0.1 pad_add_fusion.refs_0_
  33.8 1.8 %collective-permute-done.1.refs_2_ = bf16[8,48,768]{2,1,0:T(8,128)(2,1)S(1)} collective-permute-done((bf16[8,48,768]{2,1,0:T(8,128)(2,1)S(1)}, bf16[8,48,768]{2,1,0:T(8,128)(2,1)S(1)}, u32[]{:S(2)}, u32[]{:S(2)}) %collective-permute-start.1) | collective-permute-done | bytes 589856 | tf_op jit(solution)/shard_map/ppermute | solution.py:448
  35.6 0.0 copy-done
  35.7 4.4 %correlate.1 = bf16[2048,512]{1,0:T(8,128)(2,1)} custom-call(s32[131]{0:T(256)S(1)} %pad_add_fusion.refs_0_, bf16[8,48,768]{2,1,0:T(8,128)(2,1)S(1)} %all_to_all.10.refs_1_, bf16[8,48,768]{2,1,0:T(8,128)(2,1)S(1)} %collective-permute-done.1.refs_2_, bf16[768,512]{1,0:T(8,128)(2,1)S(1)} %copy-done), custom_call_target="tpu_custom_call" | custom-call | tf_op jit(solution)/shard_map/correlate/pallas_call | solution.py:394
Async XLA Ops:
  0.0 15.2 %copy-start.1 = (bf16[512,768]{1,0:T(8,128)(2,1)S(1)}, bf16[512,768]{1,0:T(8,128)(2,1)}, u32[]{:S(2)}) copy-start(bf16[512,768]{1,0:T(8,128)(2,1)} %constant.127.inner_ref) | copy-start | bytes 2359300
  0.0 15.2 %copy-start.3 = (f32[33,1,768]{2,1,0:T(1,128)S(1)}, f32[33,1,768]{2,1,0:T(1,128)}, u32[]{:S(2)}) copy-start(f32[33,1,768]{2,1,0:T(1,128)} %constant.123.clone.phase_ref) | copy-start | bytes 304132
  0.0 21.7 %copy-start.2 = (bf16[384,384]{1,0:T(8,128)(2,1)S(1)}, bf16[384,384]{1,0:T(8,128)(2,1)}, u32[]{:S(2)}) copy-start(bf16[384,384]{1,0:T(8,128)(2,1)} %constant.128.band_ref) | copy-start | bytes 884740
  0.0 8.8 %copy-start.5 = (s32[3]{0:T(128)S(1)}, s32[3]{0:T(128)}, u32[]{:S(2)}) copy-start(s32[3]{0:T(128)} %param.9) | copy-start | bytes 40
  2.5 31.1 %copy-start.4 = (s32[256]{0:T(256)S(1)}, s32[256]{0:T(256)}, u32[]{:S(2)}) copy-start(s32[256]{0:T(256)} %param.10) | copy-start | bytes 3076
  2.5 33.1 %copy-start = (bf16[768,512]{1,0:T(8,128)(2,1)S(1)}, bf16[768,512]{1,0:T(8,128)(2,1)}, u32[]{:S(2)}) copy-start(bf16[768,512]{1,0:T(8,128)(2,1)} %constant.129.refs_3_) | copy-start | bytes 2359300
  2.5 12.7 %all-to-all-start = ((bf16[8,136,128]{2,1,0:T(8,128)(2,1)}), bf16[8,136,128]{2,1,0:T(8,128)(2,1)S(1)}, u32[]{:S(2)}, u32[]{:S(2)}) async-start(bf16[8,136,128]{2,1,0:T(8,128)(2,1)} %decimate.1), calls=%async_computation | async-start | bytes 557056 | tf_op jit(solution)/shard_map/all_to_all | solution.py:440
  16.4 5.3 %collective-permute-start = (bf16[48,768]{1,0:T(8,128)(2,1)S(1)}, bf16[48,768]{1,0:T(8,128)(2,1)S(1)}, u32[]{:S(2)}, u32[]{:S(2)}) collective-permute-start(bf16[48,768]{1,0:T(8,128)(2,1)S(1)} %get-tuple-element.8), channel_id=1, source_target_pairs={{0,16},{2,18},{4,20},{6,22},{8,24},{10,26},{12,28},{14,30},{16,0},... | collective-permute-start | bytes 221192 | tf_op jit(solution)/shard_map/ppermute | solution.py:443
  33.6 2.0 %collective-permute-start.1 = (bf16[8,48,768]{2,1,0:T(8,128)(2,1)S(1)}, bf16[8,48,768]{2,1,0:T(8,128)(2,1)S(1)}, u32[]{:S(2)}, u32[]{:S(2)}) collective-permute-start(bf16[8,48,768]{2,1,0:T(8,128)(2,1)S(1)} %all_to_all.10.refs_1_), channel_id=1, source_target_pairs={{1,0},{0,1},{3,2},{2,3},{5,4},{4,5},{7,6},{6,7},{9,8},{8,9},{11,10... | collective-permute-start | bytes 1769480 | tf_op jit(solution)/shard_map/ppermute | solution.py:448

commit v11 on v10

--- a/solution.py
+++ b/solution.py
@@ -248,7 +248,7 @@
             pltpu.SMEM(info.shape, jnp.int32),
             pltpu.SemaphoreType.DMA,
         ],
-        compiler_params=pltpu.CompilerParams(vmem_limit_bytes=32 * 1024 * 1024),
+        compiler_params=pltpu.CompilerParams(vmem_limit_bytes=12 * 1024 * 1024),
         name="spectrum",
     )(info, recv, inner_table(), phase_table(-1, HALVES * blocks + 1))
 
@@ -277,7 +277,7 @@
         out_shape=jax.ShapeDtypeStruct((peers, *own.shape), jnp.bfloat16),
         in_specs=[VMEM] * 3,
         out_specs=VMEM,
-        compiler_params=pltpu.CompilerParams(vmem_limit_bytes=32 * 1024 * 1024),
+        compiler_params=pltpu.CompilerParams(vmem_limit_bytes=12 * 1024 * 1024),
         name="whiten",
     )(own, other, band_table())
 
@@ -408,7 +408,7 @@
             pltpu.SemaphoreType.DMA,
         ],
         compiler_params=pltpu.CompilerParams(
-            vmem_limit_bytes=min(16 * 1024 * 1024 + 3 * held, 63 * 1024 * 1024)
+            vmem_limit_bytes=min(10 * 1024 * 1024 + 3 * held, 63 * 1024 * 1024)
         ),
         name="correlate",
     )(info, *spectra, lag_table())

time: 40.4 us -> 40.3 us (level)
  no operation moved by 1% of the time
where the time goes in v11:
time: 40.3 us; the launch traced here: 40.1 us
  blocking collectives  11.6 us (29%)
  waiting for transfers between devices  10.8 us (27%)
  starting transfers between devices  8.98 us (22%)
  Pallas kernels  8.36 us (21%)
    all_to_all x1, blocking collectives, on_device(): lax.all_to_all(white, 'chan', 0, 0, tiled=True, axis_index_groups=cubes)  11.6 us
    all_to_all x1, starting transfers between devices, on_device(): lax.all_to_all(sent, 'chan', 0, 0, tiled=True, axis_index_groups=cubes)  6.33 us
    all_to_all x1, waiting for transfers between devices, on_device(): lax.all_to_all(sent, 'chan', 0, 0, tiled=True, axis_index_groups=cubes)  6.31 us
    pallas_call x1, Pallas kernels, correlate(): pl.pallas_call(kernel, out_shape=jax.ShapeDtypeStruct((many * receivers,...  4.43 us
    ppermute x1, waiting for transfers between devices, on_device(): white = whiten(own, lax.ppermute(send, 'chan', across), peers)  2.68 us
    ppermute x1, starting transfers between devices, on_device(): white = whiten(own, lax.ppermute(send, 'chan', across), peers)  2.65 us
    pallas_call x1, Pallas kernels, decimate(): pl.pallas_call(decimate_kernel, out_shape=jax.ShapeDtypeStruct((peers, ma...  2.5 us
    ppermute x1, waiting for transfers between devices, on_device(): spectra.append(lax.ppermute(held, 'src', pairs))  1.81 us
  transfers between devices with their start and end apart: 3, of which 3 were waited for; matrix products, arithmetic and copies ran while one was open for 1% of the time, Pallas kernels for 0%

profile of v11, /device:TPU:0, one launch (start us, length us, event | category | flops | bytes accessed | tf_op | source)
XLA Modules:
  0.0 40.1 jit_solution(7193924173648063065)
XLA Ops:
  0.0 0.0 copy-start.1
  0.0 0.0 copy-start.3
  0.0 0.0 copy-start.2
  0.0 0.0 copy-start.5
  0.0 2.5 %decimate.1 = bf16[8,136,128]{2,1,0:T(8,128)(2,1)} custom-call(bf16[2,64,4096]{2,1,0:T(8,128)(2,1)} %bitcast.5, bf16[512,256]{1,0:T(8,128)(2,1)} %constant.126.table_ref), custom_call_target="tpu_custom_call" | custom-call | tf_op jit(solution)/shard_map/decimate/pallas_call | solution.py:130
  2.5 0.0 copy-start.4
  2.5 0.0 copy-start
  2.5 6.3 %all-to-all-start = ((bf16[8,136,128]{2,1,0:T(8,128)(2,1)}), bf16[8,136,128]{2,1,0:T(8,128)(2,1)S(1)}, u32[]{:S(2)}, u32[]{:S(2)}) async-start(bf16[8,136,128]{2,1,0:T(8,128)(2,1)} %decimate.1), calls=%async_computation | async-start | bytes 557056 | tf_op jit(solution)/shard_map/all_to_all | solution.py:440
  8.8 0.0 copy-done.5
  8.8 0.1 pad_add_fusion.1.info_vmem
  8.9 6.3 %all-to-all-done.recv_ref = bf16[8,136,128]{2,1,0:T(8,128)(2,1)S(1)} async-done(((bf16[8,136,128]{2,1,0:T(8,128)(2,1)}), bf16[8,136,128]{2,1,0:T(8,128)(2,1)S(1)}, u32[]{:S(2)}, u32[]{:S(2)}) %all-to-all-start) | async-done | bytes 278560 | tf_op jit(solution)/shard_map/all_to_all | solution.py:440
  15.2 0.0 copy-done.1
  15.2 0.0 copy-done.3
  15.2 1.2 %spectrum.1 = (f32[48,768]{1,0:T(8,128)S(1)}, bf16[48,768]{1,0:T(8,128)(2,1)S(1)}) custom-call(s32[4]{0:T(128)S(1)} %pad_add_fusion.1.info_vmem, bf16[8,136,128]{2,1,0:T(8,128)(2,1)S(1)} %all-to-all-done.recv_ref, bf16[512,768]{1,0:T(8,128)(2,1)S(1)} %copy-done.1, f32[33,1,768]{2,1,0:T(1,128)S(1)} %copy-done.3), custom_call_target="tpu_custom_call" | custom-call | tf_op jit(solution)/shard_map/spectrum/pallas_call | solution.py:237
  16.4 2.6 %collective-permute-start = (bf16[48,768]{1,0:T(8,128)(2,1)S(1)}, bf16[48,768]{1,0:T(8,128)(2,1)S(1)}, u32[]{:S(2)}, u32[]{:S(2)}) collective-permute-start(bf16[48,768]{1,0:T(8,128)(2,1)S(1)} %get-tuple-element.8), channel_id=1, source_target_pairs={{0,16},{2,18},{4,20},{6,22},{8,24},{10,26},{12,28},{14,30},{16,0},... | collective-permute-start | bytes 221192 | tf_op jit(solution)/shard_map/ppermute | solution.py:443
  19.1 2.7 %collective-permute-done.other_ref = bf16[48,768]{1,0:T(8,128)(2,1)S(1)} collective-permute-done((bf16[48,768]{1,0:T(8,128)(2,1)S(1)}, bf16[48,768]{1,0:T(8,128)(2,1)S(1)}, u32[]{:S(2)}, u32[]{:S(2)}) %collective-permute-start) | collective-permute-done | bytes 73760 | tf_op jit(solution)/shard_map/ppermute | solution.py:443
  21.7 0.0 copy-done.2
  21.8 0.3 whiten.1
  22.0 11.6 %all_to_all.10.refs_1_ = bf16[8,48,768]{2,1,0:T(8,128)(2,1)S(1)} all-to-all(bf16[8,48,768]{2,1,0:T(8,128)(2,1)S(1)} %whiten.1), channel_id=1, replica_groups={{0,2,6,4,12,14,10,8},{16,18,22,20,28,30,26,24},{1,3,7,5,13,15,11,9},{17..., dimensions={0} | all-to-all | bytes 1179648 | tf_op jit(solution)/shard_map/all_to_all | solution.py:444
  33.6 0.0 collective-permute-start.1
  33.6 0.0 copy-done.4
  33.6 0.1 fusion
  33.8 0.1 pad_add_fusion.refs_0_
  33.8 1.8 %collective-permute-done.1.refs_2_ = bf16[8,48,768]{2,1,0:T(8,128)(2,1)S(1)} collective-permute-done((bf16[8,48,768]{2,1,0:T(8,128)(2,1)S(1)}, bf16[8,48,768]{2,1,0:T(8,128)(2,1)S(1)}, u32[]{:S(2)}, u32[]{:S(2)}) %collective-permute-start.1) | collective-permute-done | bytes 589856 | tf_op jit(solution)/shard_map/ppermute | solution.py:448
  35.6 0.0 copy-done
  35.7 4.4 %correlate.1 = bf16[2048,512]{1,0:T(8,128)(2,1)} custom-call(s32[131]{0:T(256)S(1)} %pad_add_fusion.refs_0_, bf16[8,48,768]{2,1,0:T(8,128)(2,1)S(1)} %all_to_all.10.refs_1_, bf16[8,48,768]{2,1,0:T(8,128)(2,1)S(1)} %collective-permute-done.1.refs_2_, bf16[768,512]{1,0:T(8,128)(2,1)S(1)} %copy-done), custom_call_target="tpu_custom_call" | custom-call | tf_op jit(solution)/shard_map/correlate/pallas_call | solution.py:394
Async XLA Ops:
  0.0 15.2 %copy-start.1 = (bf16[512,768]{1,0:T(8,128)(2,1)S(1)}, bf16[512,768]{1,0:T(8,128)(2,1)}, u32[]{:S(2)}) copy-start(bf16[512,768]{1,0:T(8,128)(2,1)} %constant.127.inner_ref) | copy-start | bytes 2359300
  0.0 15.2 %copy-start.3 = (f32[33,1,768]{2,1,0:T(1,128)S(1)}, f32[33,1,768]{2,1,0:T(1,128)}, u32[]{:S(2)}) copy-start(f32[33,1,768]{2,1,0:T(1,128)} %constant.123.clone.phase_ref) | copy-start | bytes 304132
  0.0 21.7 %copy-start.2 = (bf16[384,384]{1,0:T(8,128)(2,1)S(1)}, bf16[384,384]{1,0:T(8,128)(2,1)}, u32[]{:S(2)}) copy-start(bf16[384,384]{1,0:T(8,128)(2,1)} %constant.128.band_ref) | copy-start | bytes 884740
  0.0 8.8 %copy-start.5 = (s32[3]{0:T(128)S(1)}, s32[3]{0:T(128)}, u32[]{:S(2)}) copy-start(s32[3]{0:T(128)} %param.9) | copy-start | bytes 40
  2.5 31.1 %copy-start.4 = (s32[256]{0:T(256)S(1)}, s32[256]{0:T(256)}, u32[]{:S(2)}) copy-start(s32[256]{0:T(256)} %param.10) | copy-start | bytes 3076
  2.5 33.1 %copy-start = (bf16[768,512]{1,0:T(8,128)(2,1)S(1)}, bf16[768,512]{1,0:T(8,128)(2,1)}, u32[]{:S(2)}) copy-start(bf16[768,512]{1,0:T(8,128)(2,1)} %constant.129.refs_3_) | copy-start | bytes 2359300
  2.5 12.7 %all-to-all-start = ((bf16[8,136,128]{2,1,0:T(8,128)(2,1)}), bf16[8,136,128]{2,1,0:T(8,128)(2,1)S(1)}, u32[]{:S(2)}, u32[]{:S(2)}) async-start(bf16[8,136,128]{2,1,0:T(8,128)(2,1)} %decimate.1), calls=%async_computation | async-start | bytes 557056 | tf_op jit(solution)/shard_map/all_to_all | solution.py:440
  16.4 5.3 %collective-permute-start = (bf16[48,768]{1,0:T(8,128)(2,1)S(1)}, bf16[48,768]{1,0:T(8,128)(2,1)S(1)}, u32[]{:S(2)}, u32[]{:S(2)}) collective-permute-start(bf16[48,768]{1,0:T(8,128)(2,1)S(1)} %get-tuple-element.8), channel_id=1, source_target_pairs={{0,16},{2,18},{4,20},{6,22},{8,24},{10,26},{12,28},{14,30},{16,0},... | collective-permute-start | bytes 221192 | tf_op jit(solution)/shard_map/ppermute | solution.py:443
  33.6 2.0 %collective-permute-start.1 = (bf16[8,48,768]{2,1,0:T(8,128)(2,1)S(1)}, bf16[8,48,768]{2,1,0:T(8,128)(2,1)S(1)}, u32[]{:S(2)}, u32[]{:S(2)}) collective-permute-start(bf16[8,48,768]{2,1,0:T(8,128)(2,1)S(1)} %all_to_all.10.refs_1_), channel_id=1, source_target_pairs={{1,0},{0,1},{3,2},{2,3},{5,4},{4,5},{7,6},{6,7},{9,8},{8,9},{11,10... | collective-permute-start | bytes 1769480 | tf_op jit(solution)/shard_map/ppermute | solution.py:448

commit v12 on v11

--- a/solution.py
+++ b/solution.py
@@ -288,7 +288,7 @@
     rows = HALVES * group
     channels = spectra[0].shape[0] * rows
     receivers = groups * group
-    blocks = sent.shape[0]
+    blocks = sent.shape[0] - 1
     tell = pltpu.make_async_copy(info_vmem, info_ref, told)
     tell.start()
 
@@ -370,13 +370,19 @@
     lax.fori_loop(0, last, step, 0)
     pair(last)
     lag(2 * last + 1, cross_odd)
-    store(2 * last + 1).start()
+    parts = []
+    for part in range(2):
+        at = pl.ds((blocks - 1) * size + part * (size // 2), size // 2)
+        parts.append(pltpu.make_async_copy(lagged.at[at], out_ref.at[at], sent.at[blocks - 1 + part]))
+        parts[-1].start()
 
     def finish(number, carry):
         store(number).wait()
         return carry
 
-    lax.fori_loop(0, blocks, finish, 0)
+    lax.fori_loop(0, blocks - 1, finish, 0)
+    for part in parts:
+        part.wait()
 
 
 def correlate(info, spectra, group):
@@ -403,7 +409,7 @@
             pltpu.VMEM((rows, 2 * NBIN), jnp.bfloat16),
             pltpu.VMEM((rows, 2 * NBIN), jnp.bfloat16),
             pltpu.VMEM((many * receivers, NLAG), jnp.bfloat16),
-            pltpu.SemaphoreType.DMA((many // block,)),
+            pltpu.SemaphoreType.DMA((many // block + 1,)),
             pltpu.SMEM(info.shape, jnp.int32),
             pltpu.SemaphoreType.DMA,
         ],

time: 40.3 us -> 40.3 us (level)
  no operation moved by 1% of the time
where the time goes in v12:
time: 40.3 us; the launch traced here: 40.1 us
  blocking collectives  11.6 us (29%)
  waiting for transfers between devices  10.8 us (27%)
  starting transfers between devices  8.98 us (22%)
  Pallas kernels  8.34 us (21%)
    all_to_all x1, blocking collectives, on_device(): lax.all_to_all(white, 'chan', 0, 0, tiled=True, axis_index_groups=cubes)  11.6 us
    all_to_all x1, starting transfers between devices, on_device(): lax.all_to_all(sent, 'chan', 0, 0, tiled=True, axis_index_groups=cubes)  6.33 us
    all_to_all x1, waiting for transfers between devices, on_device(): lax.all_to_all(sent, 'chan', 0, 0, tiled=True, axis_index_groups=cubes)  6.31 us
    pallas_call x1, Pallas kernels, correlate(): pl.pallas_call(kernel, out_shape=jax.ShapeDtypeStruct((many * receivers,...  4.41 us
    ppermute x1, waiting for transfers between devices, on_device(): white = whiten(own, lax.ppermute(send, 'chan', across), peers)  2.68 us
    ppermute x1, starting transfers between devices, on_device(): white = whiten(own, lax.ppermute(send, 'chan', across), peers)  2.65 us
    pallas_call x1, Pallas kernels, decimate(): pl.pallas_call(decimate_kernel, out_shape=jax.ShapeDtypeStruct((peers, ma...  2.5 us
    ppermute x1, waiting for transfers between devices, on_device(): spectra.append(lax.ppermute(held, 'src', pairs))  1.81 us
  transfers between devices with their start and end apart: 3, of which 3 were waited for; matrix products, arithmetic and copies ran while one was open for 1% of the time, Pallas kernels for 0%

profile of v12, /device:TPU:0, one launch (start us, length us, event | category | flops | bytes accessed | tf_op | source)
XLA Modules:
  0.0 40.1 jit_solution(4002915557131028569)
XLA Ops:
  0.0 0.0 copy-start.1
  0.0 0.0 copy-start.3
  0.0 0.0 copy-start.2
  0.0 0.0 copy-start.5
  0.0 2.5 %decimate.1 = bf16[8,136,128]{2,1,0:T(8,128)(2,1)} custom-call(bf16[2,64,4096]{2,1,0:T(8,128)(2,1)} %bitcast.5, bf16[512,256]{1,0:T(8,128)(2,1)} %constant.126.table_ref), custom_call_target="tpu_custom_call" | custom-call | tf_op jit(solution)/shard_map/decimate/pallas_call | solution.py:130
  2.5 0.0 copy-start.4
  2.5 0.0 copy-start
  2.5 6.3 %all-to-all-start = ((bf16[8,136,128]{2,1,0:T(8,128)(2,1)}), bf16[8,136,128]{2,1,0:T(8,128)(2,1)S(1)}, u32[]{:S(2)}, u32[]{:S(2)}) async-start(bf16[8,136,128]{2,1,0:T(8,128)(2,1)} %decimate.1), calls=%async_computation | async-start | bytes 557056 | tf_op jit(solution)/shard_map/all_to_all | solution.py:446
  8.8 0.0 copy-done.5
  8.8 0.1 pad_add_fusion.1.info_vmem
  8.9 6.3 %all-to-all-done.recv_ref = bf16[8,136,128]{2,1,0:T(8,128)(2,1)S(1)} async-done(((bf16[8,136,128]{2,1,0:T(8,128)(2,1)}), bf16[8,136,128]{2,1,0:T(8,128)(2,1)S(1)}, u32[]{:S(2)}, u32[]{:S(2)}) %all-to-all-start) | async-done | bytes 278560 | tf_op jit(solution)/shard_map/all_to_all | solution.py:446
  15.2 0.0 copy-done.1
  15.2 0.0 copy-done.3
  15.2 1.2 %spectrum.1 = (f32[48,768]{1,0:T(8,128)S(1)}, bf16[48,768]{1,0:T(8,128)(2,1)S(1)}) custom-call(s32[4]{0:T(128)S(1)} %pad_add_fusion.1.info_vmem, bf16[8,136,128]{2,1,0:T(8,128)(2,1)S(1)} %all-to-all-done.recv_ref, bf16[512,768]{1,0:T(8,128)(2,1)S(1)} %copy-done.1, f32[33,1,768]{2,1,0:T(1,128)S(1)} %copy-done.3), custom_call_target="tpu_custom_call" | custom-call | tf_op jit(solution)/shard_map/spectrum/pallas_call | solution.py:237
  16.4 2.6 %collective-permute-start = (bf16[48,768]{1,0:T(8,128)(2,1)S(1)}, bf16[48,768]{1,0:T(8,128)(2,1)S(1)}, u32[]{:S(2)}, u32[]{:S(2)}) collective-permute-start(bf16[48,768]{1,0:T(8,128)(2,1)S(1)} %get-tuple-element.8), channel_id=1, source_target_pairs={{0,16},{2,18},{4,20},{6,22},{8,24},{10,26},{12,28},{14,30},{16,0},... | collective-permute-start | bytes 221192 | tf_op jit(solution)/shard_map/ppermute | solution.py:449
  19.1 2.7 %collective-permute-done.other_ref = bf16[48,768]{1,0:T(8,128)(2,1)S(1)} collective-permute-done((bf16[48,768]{1,0:T(8,128)(2,1)S(1)}, bf16[48,768]{1,0:T(8,128)(2,1)S(1)}, u32[]{:S(2)}, u32[]{:S(2)}) %collective-permute-start) | collective-permute-done | bytes 73760 | tf_op jit(solution)/shard_map/ppermute | solution.py:449
  21.7 0.0 copy-done.2
  21.8 0.3 whiten.1
  22.0 11.6 %all_to_all.10.refs_1_ = bf16[8,48,768]{2,1,0:T(8,128)(2,1)S(1)} all-to-all(bf16[8,48,768]{2,1,0:T(8,128)(2,1)S(1)} %whiten.1), channel_id=1, replica_groups={{0,2,6,4,12,14,10,8},{16,18,22,20,28,30,26,24},{1,3,7,5,13,15,11,9},{17..., dimensions={0} | all-to-all | bytes 1179648 | tf_op jit(solution)/shard_map/all_to_all | solution.py:450
  33.6 0.0 collective-permute-start.1
  33.6 0.0 copy-done.4
  33.6 0.1 fusion
  33.8 0.1 pad_add_fusion.refs_0_
  33.8 1.8 %collective-permute-done.1.refs_2_ = bf16[8,48,768]{2,1,0:T(8,128)(2,1)S(1)} collective-permute-done((bf16[8,48,768]{2,1,0:T(8,128)(2,1)S(1)}, bf16[8,48,768]{2,1,0:T(8,128)(2,1)S(1)}, u32[]{:S(2)}, u32[]{:S(2)}) %collective-permute-start.1) | collective-permute-done | bytes 589856 | tf_op jit(solution)/shard_map/ppermute | solution.py:454
  35.6 0.0 copy-done
  35.7 4.4 %correlate.1 = bf16[2048,512]{1,0:T(8,128)(2,1)} custom-call(s32[131]{0:T(256)S(1)} %pad_add_fusion.refs_0_, bf16[8,48,768]{2,1,0:T(8,128)(2,1)S(1)} %all_to_all.10.refs_1_, bf16[8,48,768]{2,1,0:T(8,128)(2,1)S(1)} %collective-permute-done.1.refs_2_, bf16[768,512]{1,0:T(8,128)(2,1)S(1)} %copy-done), custom_call_target="tpu_custom_call" | custom-call | tf_op jit(solution)/shard_map/correlate/pallas_call | solution.py:400
Async XLA Ops:
  0.0 15.2 %copy-start.1 = (bf16[512,768]{1,0:T(8,128)(2,1)S(1)}, bf16[512,768]{1,0:T(8,128)(2,1)}, u32[]{:S(2)}) copy-start(bf16[512,768]{1,0:T(8,128)(2,1)} %constant.127.inner_ref) | copy-start | bytes 2359300
  0.0 15.2 %copy-start.3 = (f32[33,1,768]{2,1,0:T(1,128)S(1)}, f32[33,1,768]{2,1,0:T(1,128)}, u32[]{:S(2)}) copy-start(f32[33,1,768]{2,1,0:T(1,128)} %constant.123.clone.phase_ref) | copy-start | bytes 304132
  0.0 21.7 %copy-start.2 = (bf16[384,384]{1,0:T(8,128)(2,1)S(1)}, bf16[384,384]{1,0:T(8,128)(2,1)}, u32[]{:S(2)}) copy-start(bf16[384,384]{1,0:T(8,128)(2,1)} %constant.128.band_ref) | copy-start | bytes 884740
  0.0 8.8 %copy-start.5 = (s32[3]{0:T(128)S(1)}, s32[3]{0:T(128)}, u32[]{:S(2)}) copy-start(s32[3]{0:T(128)} %param.9) | copy-start | bytes 40
  2.5 31.1 %copy-start.4 = (s32[256]{0:T(256)S(1)}, s32[256]{0:T(256)}, u32[]{:S(2)}) copy-start(s32[256]{0:T(256)} %param.10) | copy-start | bytes 3076
  2.5 33.1 %copy-start = (bf16[768,512]{1,0:T(8,128)(2,1)S(1)}, bf16[768,512]{1,0:T(8,128)(2,1)}, u32[]{:S(2)}) copy-start(bf16[768,512]{1,0:T(8,128)(2,1)} %constant.129.refs_3_) | copy-start | bytes 2359300
  2.5 12.7 %all-to-all-start = ((bf16[8,136,128]{2,1,0:T(8,128)(2,1)}), bf16[8,136,128]{2,1,0:T(8,128)(2,1)S(1)}, u32[]{:S(2)}, u32[]{:S(2)}) async-start(bf16[8,136,128]{2,1,0:T(8,128)(2,1)} %decimate.1), calls=%async_computation | async-start | bytes 557056 | tf_op jit(solution)/shard_map/all_to_all | solution.py:446
  16.4 5.3 %collective-permute-start = (bf16[48,768]{1,0:T(8,128)(2,1)S(1)}, bf16[48,768]{1,0:T(8,128)(2,1)S(1)}, u32[]{:S(2)}, u32[]{:S(2)}) collective-permute-start(bf16[48,768]{1,0:T(8,128)(2,1)S(1)} %get-tuple-element.8), channel_id=1, source_target_pairs={{0,16},{2,18},{4,20},{6,22},{8,24},{10,26},{12,28},{14,30},{16,0},... | collective-permute-start | bytes 221192 | tf_op jit(solution)/shard_map/ppermute | solution.py:449
  33.6 2.0 %collective-permute-start.1 = (bf16[8,48,768]{2,1,0:T(8,128)(2,1)S(1)}, bf16[8,48,768]{2,1,0:T(8,128)(2,1)S(1)}, u32[]{:S(2)}, u32[]{:S(2)}) collective-permute-start(bf16[8,48,768]{2,1,0:T(8,128)(2,1)S(1)} %all_to_all.10.refs_1_), channel_id=1, source_target_pairs={{1,0},{0,1},{3,2},{2,3},{5,4},{4,5},{7,6},{6,7},{9,8},{8,9},{11,10... | collective-permute-start | bytes 1769480 | tf_op jit(solution)/shard_map/ppermute | solution.py:454
